TPU v7x, 128 devices: a whole 4x4x4 slice. The times are simulated.
128 devices in a mesh: seq: 8 (over z_lo, x), mp: 16 (over z_hi, y, core).
Axes of the slice: x: 4, y: 4, z: 4 (z_hi: 2, z_lo: 2; z = z_hi * 2 + z_lo), core: 2. Of those that a mesh axis runs over, the one named last changes fastest.
Arguments:
- features: bfloat16 [8192, 768], P('seq'), may hold values from -13 to 13
- base_tokens: int32 [524288], P('seq'), may hold values from 0 to 3
- base_proj: float32 [4, 768], replicated, may hold values from -6 to 6
- conv_weight: bfloat16 [5, 1536, 768], P(None, 'mp'), may hold values from -0.23399274 to 0.23399274
- conv_bias: float32 [1536], P('mp'), may hold values from -3 to 3
- w_query: bfloat16 [1536, 1536], P('mp'), may hold values from -0.5434805 to 0.5434805
- w_key: bfloat16 [1536, 1536], P('mp'), may hold values from -0.5434805 to 0.5434805
- w_value: bfloat16 [1536, 1536], P('mp'), may hold values from -0.15625 to 0.15625
- w_out: bfloat16 [1536, 1536], P('mp'), may hold values from -0.15625 to 0.15625
- cotangent: bfloat16 [4096, 1536], P('seq', 'mp'), may hold values from -6 to 6
Outputs:
- layer_out: bfloat16 [4096, 1536], P('seq', 'mp')
- grad_conv_weight: float32 [5, 1536, 768], P(None, 'mp')
- grad_conv_bias: float32 [1536], P('mp')
- grad_w_query: float32 [1536, 1536], P('mp')
- grad_w_key: float32 [1536, 1536], P('mp')
- grad_w_value: float32 [1536, 1536], P('mp')
- grad_w_out: float32 [1536, 1536], P('mp')
All inputs are finite; a program needn't handle non-finite values.
Results may differ from a plain program's by a relative error of at most 0.03.
Values may be sent and summed in bfloat16 or wider, within the bound.
A program may use at most 128 MiB of HBM per device.

v0:
```python
import jax
import jax.numpy as jnp
from jax import lax
from jax.sharding import PartitionSpec as P

D = 1536
KERNEL = 5
BIN_WIDTH = 64


EPS = 1e-06


def with_halo(cells, sides, width):
    for axis, dim in sides:
        count = lax.axis_size(axis)
        ends = count - 1
        head = lax.slice_in_dim(cells, 0, width, axis=dim)
        tail = lax.slice_in_dim(cells, cells.shape[dim] - width, cells.shape[dim], axis=dim)
        cells = jnp.concatenate(
            [
                lax.ppermute(tail, axis, [(i, (i + 1) % count) for i in range(ends)]),
                cells,
                lax.ppermute(head, axis, [((i + 1) % count, i) for i in range(ends)]),
            ],
            axis=dim,
        )
    return cells


def swapped(shard, axis, stride):
    return lax.ppermute(shard, axis, [(i, i ^ 1 << stride) for i in range(lax.axis_size(axis))])


def composition(base_tokens):
    letters = jnp.arange(4, dtype=jnp.int32)
    matches = (base_tokens[None, :] == letters[:, None]).astype(jnp.float32)
    return jnp.sum(matches.reshape(4, -1, BIN_WIDTH), axis=2) / BIN_WIDTH


def gelu_slope(pre_act):
    return jax.vjp(jax.nn.gelu, pre_act)[1](jnp.ones_like(pre_act))[0]


def convolve(padded, weight, offset):
    length = padded.shape[0] - (KERNEL - 1)
    running = jnp.zeros((length, weight.shape[1]), jnp.float32) + offset[None, :]
    for tap_index in range(KERNEL):
        running = running + lax.dot_general(
            padded[tap_index : tap_index + length],
            weight[tap_index],
            (((1,), (1,)), ((), ())),
            preferred_element_type=jnp.float32,
        )
    return running


def attend(query_rows, key_rows, value_rows, block_rows):
    score_scale = query_rows.shape[1] ** (-0.5)

    def one_block(row_block):
        scores = (
            lax.dot_general(
                row_block, key_rows, (((1,), (1,)), ((), ())), preferred_element_type=jnp.float32
            )
            * score_scale
        )
        row_max = jnp.max(scores, axis=1, keepdims=True)
        log_total = jnp.log(jnp.sum(jnp.exp(scores - row_max), axis=1, keepdims=True)) + row_max
        attn_probs = jnp.exp(scores - log_total).astype(jnp.bfloat16)
        result = jnp.dot(attn_probs, value_rows, preferred_element_type=jnp.float32).astype(
            jnp.bfloat16
        )
        return (result, log_total[:, 0])

    results, totals = lax.map(one_block, query_rows.reshape(-1, block_rows, query_rows.shape[1]))
    return (results.reshape(-1, value_rows.shape[1]), totals.reshape(-1))


def attend_grad(query_rows, key_rows, value_rows, totals, grad_rows, block_rows, width):
    score_scale = query_rows.shape[1] ** (-0.5)
    head_dim = query_rows.shape[1]

    def one_block(running, pieces):
        row_block, row_totals, row_grads = pieces
        scores = (
            lax.dot_general(
                row_block, key_rows, (((1,), (1,)), ((), ())), preferred_element_type=jnp.float32
            )
            * score_scale
        )
        attn_probs = jnp.exp(scores - row_totals[:, None])
        grad_probs = lax.dot_general(
            row_grads, value_rows, (((1,), (1,)), ((), ())), preferred_element_type=jnp.float32
        )
        row_delta = jnp.sum(attn_probs * grad_probs, axis=1, keepdims=True)
        grad_scores = (attn_probs * (grad_probs - row_delta) * score_scale).astype(jnp.bfloat16)
        grad_query = jnp.dot(
            grad_scores, key_rows[:, :width], preferred_element_type=jnp.float32
        ).astype(jnp.bfloat16)
        key_sum = running[0] + lax.dot_general(
            grad_scores,
            row_block[:, :width],
            (((0,), (0,)), ((), ())),
            preferred_element_type=jnp.float32,
        )
        value_sum = running[1] + lax.dot_general(
            attn_probs.astype(jnp.bfloat16),
            row_grads[:, :width],
            (((0,), (0,)), ((), ())),
            preferred_element_type=jnp.float32,
        )
        return ((key_sum, value_sum), grad_query)

    initial = (
        jnp.zeros((key_rows.shape[0], width), jnp.float32),
        jnp.zeros((key_rows.shape[0], width), jnp.float32),
    )
    sums, grads = lax.scan(
        one_block,
        initial,
        (
            query_rows.reshape(-1, block_rows, head_dim),
            totals.reshape(-1, block_rows),
            grad_rows.reshape(-1, block_rows, head_dim),
        ),
    )
    return (grads.reshape(-1, width), sums[0], sums[1])


def project(normed, weight):
    return lax.dot_general(
        normed, weight, (((1,), (1,)), ((), ())), preferred_element_type=jnp.float32
    ).astype(jnp.bfloat16)


def body(
    features,
    base_tokens,
    base_proj,
    conv_weight,
    conv_bias,
    w_query,
    w_key,
    w_value,
    w_out,
    cotangent,
):
    col_share = conv_weight.shape[1]
    column = lax.axis_index("mp") * col_share
    mixed_in = features.astype(jnp.float32) + lax.dot_general(
        composition(base_tokens),
        base_proj,
        (((0,), (0,)), ((), ())),
        precision=lax.Precision.HIGHEST,
        preferred_element_type=jnp.float32,
    )
    conv_input = mixed_in.astype(jnp.bfloat16)
    padded = with_halo(conv_input, (("seq", 0),), KERNEL // 2)
    pre_act = convolve(padded, conv_weight, conv_bias)
    own_tok = jnp.mean(jax.nn.gelu(pre_act).reshape(-1, 2, col_share), axis=1).astype(jnp.bfloat16)
    tok_rows = own_tok.shape[0]
    whole_tok = lax.all_gather(own_tok, "mp", axis=1, tiled=True)
    tok_wide = whole_tok.astype(jnp.float32)
    inverse = lax.rsqrt(jnp.mean(tok_wide * tok_wide, axis=1, keepdims=True) + EPS)
    unit_rows = tok_wide * inverse
    normed = unit_rows.astype(jnp.bfloat16)
    query_own = project(normed, w_query)
    key_own = project(normed, w_key)
    value_own = project(normed, w_value)
    query_head, key_head, value_head = (query_own, key_own, value_own)
    query_pair, key_pair, value_pair = swapped((query_own, key_own, value_own), "mp", 0)
    query_head = jnp.concatenate([query_own, query_pair], axis=1)
    key_head = jnp.concatenate([key_own, key_pair], axis=1)
    value_head = jnp.concatenate([value_own, value_pair], axis=1)
    key_every, value_every = (
        lax.all_gather(key_head, "seq", axis=0, tiled=True),
        lax.all_gather(value_head, "seq", axis=0, tiled=True),
    )
    block_rows = min(512, tok_rows)
    out_head, log_totals = attend(query_head, key_every, value_every, block_rows)
    out_own = out_head[:, :col_share]
    contract_rows = (((0,), (0,)), ((), ()))
    partial_out = jnp.dot(out_own, w_out, preferred_element_type=jnp.float32)
    attn_cols = lax.psum_scatter(
        partial_out.astype(jnp.bfloat16), "mp", scatter_dimension=1, tiled=True
    ).astype(jnp.float32)
    layer_out = (own_tok.astype(jnp.float32) + attn_cols).astype(jnp.bfloat16)
    grad_full = lax.all_gather(cotangent, "mp", axis=1, tiled=True)
    contract_cols = (((1,), (1,)), ((), ()))
    grad_out_own = lax.dot_general(
        grad_full, w_out, contract_cols, preferred_element_type=jnp.float32
    ).astype(jnp.bfloat16)
    grad_w_out = lax.dot_general(
        out_own, grad_full, contract_rows, preferred_element_type=jnp.float32
    )
    grad_out_head = jnp.concatenate([grad_out_own, swapped(grad_out_own, "mp", 0)], axis=1)
    grad_query, key_sums, value_sums = attend_grad(
        query_head, key_every, value_every, log_totals, grad_out_head, block_rows, col_share
    )
    key_grads, value_grads = (
        lax.psum_scatter(
            key_sums.astype(jnp.bfloat16), "seq", scatter_dimension=0, tiled=True
        ).astype(jnp.float32),
        lax.psum_scatter(
            value_sums.astype(jnp.bfloat16), "seq", scatter_dimension=0, tiled=True
        ).astype(jnp.float32),
    )
    grad_key = key_grads.astype(jnp.bfloat16)
    grad_value = value_grads.astype(jnp.bfloat16)
    grad_w_query = lax.dot_general(
        grad_query, normed, contract_rows, preferred_element_type=jnp.float32
    )
    grad_w_key = lax.dot_general(
        grad_key, normed, contract_rows, preferred_element_type=jnp.float32
    )
    grad_w_value = lax.dot_general(
        grad_value, normed, contract_rows, preferred_element_type=jnp.float32
    )
    partial_norm = jnp.dot(grad_query, w_query, preferred_element_type=jnp.float32)
    partial_norm = partial_norm + jnp.dot(grad_key, w_key, preferred_element_type=jnp.float32)
    partial_norm = partial_norm + jnp.dot(grad_value, w_value, preferred_element_type=jnp.float32)
    norm_cols = lax.psum_scatter(
        partial_norm.astype(jnp.bfloat16), "mp", scatter_dimension=1, tiled=True
    ).astype(jnp.float32)
    unit_cols = lax.dynamic_slice_in_dim(unit_rows, column, col_share, 1)
    row_stat = lax.psum(jnp.sum(norm_cols * unit_cols, axis=1), "mp") / D
    tok_grad = cotangent.astype(jnp.float32) + inverse * (norm_cols - unit_cols * row_stat[:, None])
    spread_grad = jnp.broadcast_to(tok_grad[:, None, :], (tok_rows, 2, col_share)).reshape(
        -1, col_share
    )
    pre_grad = (0.5 * spread_grad * gelu_slope(pre_act)).astype(jnp.bfloat16)
    length = pre_grad.shape[0]
    conv_grad = jnp.stack(
        [
            lax.dot_general(
                pre_grad,
                padded[tap_index : tap_index + length],
                contract_rows,
                preferred_element_type=jnp.float32,
            )
            for tap_index in range(KERNEL)
        ]
    )
    bias_grad = jnp.sum(pre_grad.astype(jnp.float32), axis=0)
    summed = (
        lax.psum(conv_grad.astype(jnp.bfloat16), "seq").astype(jnp.float32),
        lax.psum(bias_grad.astype(jnp.bfloat16), "seq").astype(jnp.float32),
        lax.psum(grad_w_query.astype(jnp.bfloat16), "seq").astype(jnp.float32),
        lax.psum(grad_w_key.astype(jnp.bfloat16), "seq").astype(jnp.float32),
        lax.psum(grad_w_value.astype(jnp.bfloat16), "seq").astype(jnp.float32),
        lax.psum(grad_w_out.astype(jnp.bfloat16), "seq").astype(jnp.float32),
    )
    return (layer_out, summed[0], summed[1], summed[2], summed[3], summed[4], summed[5])


def solution(mesh):
    placed = (
        P("seq", None),
        P("seq"),
        P(),
        P(None, "mp", None),
        P("mp"),
        P("mp", None),
        P("mp", None),
        P("mp", None),
        P("mp", None),
        P("seq", "mp"),
    )
    return jax.shard_map(
        body,
        mesh=mesh,
        in_specs=placed,
        out_specs=(
            P("seq", "mp"),
            P(None, "mp", None),
            P("mp"),
            P("mp", None),
            P("mp", None),
            P("mp", None),
            P("mp", None),
        ),
        check_vma=False,
    )
```

profile of v0, /device:TPU:1, one launch (start us, length us, event | category | flops | bytes accessed | tf_op | source)
XLA Modules:
  0.0 537.2 jit_solution(8104079625566493694)
XLA Ops:
  7.2 1.2 eq.16
  8.8 2.8 add_convert_fusion
  11.6 3.9 collective-permute-start
  15.6 1.3 collective-permute-start.1
  18.1 1.8 collective-permute-done.1
  21.2 1.5 multiply_multiply_fusion.2
  25.2 52.2 %all-gather.5.cloned.1.call-done = bf16[512,1536]{0,1:T(8,128)(2,1)} async-done(((bf16[512,96]{0,1:T(8,128)(2,1)}), bf16[512,1536]{0,1:T(8,128)(2,1)}) %all-gather.5.cloned.1.call-update) | async-done | bytes 1572880 | tf_op jit(solution)/shard_map/all_gather | solution.py:163
  77.4 1.8 fusion.1
  79.2 2.1 convolution_convert_fusion.14
  81.6 1.1 collective-permute-done.3
  83.4 1.4 convolution_convert_fusion.13
  85.2 1.1 collective-permute-done.4
  87.0 1.1 convolution_convert_fusion.15
  88.4 36.9 %all-gather.11.cloned.1.call-done = bf16[512,1536]{0,1:T(8,128)(2,1)} async-done(((bf16[512,96]{0,1:T(8,128)(2,1)}), bf16[512,1536]{0,1:T(8,128)(2,1)}) %all-gather.11.cloned.1.call-update) | async-done | bytes 1572880 | tf_op jit(solution)/shard_map/all_gather | solution.py:189
  125.3 1.9 convolution_convert_fusion.12
  127.7 32.4 %all-gather.7.cloned.1.call-done = bf16[4096,192]{0,1:T(8,128)(2,1)} async-done(((bf16[512,192]{0,1:T(8,128)(2,1)}), bf16[4096,192]{0,1:T(8,128)(2,1)}) %all-gather.7.cloned.1.call-update) | async-done | bytes 1572880 | tf_op jit(solution)/shard_map/all_gather | solution.py:177
  160.2 2.9 multiply_reduce_fusion.1
  163.1 1.5 exponential_reduce_fusion
  164.6 1.7 copy-done.1
  166.3 35.7 %all-gather.9.cloned.1.call-done = bf16[4096,192]{0,1:T(8,128)(2,1)} async-done(((bf16[512,192]{0,1:T(8,128)(2,1)}), bf16[4096,192]{0,1:T(8,128)(2,1)}) %all-gather.9.cloned.1.call-update) | async-done | bytes 1572880 | tf_op jit(solution)/shard_map/all_gather | solution.py:178
  202.0 6.2 %multiply_reduce_fusion = (f32[512]{0:T(512)S(1)}, f32[512,4096]{1,0:T(8,128)S(1)}) fusion(f32[512,4096]{1,0:T(8,128)} %copy-done.1, f32[512]{0:T(512)S(1)} %log_add_fusion, bf16[4096,192]{0,1:T(8,128)(2,1)} %all-gather.9.cloned.1.call-done, bf16[512,96]{0,1:T(8,128)(2,1)} %collective-permute-done.5, bf16[512,96]{0,1:T(8,128)(2,1)S(1)} %convolution_convert_fusion.12), kind=kOutput, calls=%fused_computation.1 | convolution fusion | flops 814087680 | bytes 18550784 | tf_op jit(solution)/shard_map/while/body/eval_jaxpr/dot_general | solution.py:93
  208.3 4.5 multiply_convert_fusion
  212.8 2.0 copy-done.4
  214.7 2.6 convolution_convert_fusion.1
  217.4 3.9 convolution_convert_fusion
  221.3 3.8 convolution_convert_fusion.16
  225.2 2.3 fusion.76
  227.5 28.6 %reduce-scatter.7.cloned.1.call-done = bf16[512,96]{0,1:T(8,128)(2,1)} async-done(((bf16[4096,96]{0,1:T(8,128)(2,1)}), bf16[512,96]{0,1:T(8,128)(2,1)}) %reduce-scatter.7.cloned.1.call-update) | async-done | bytes 98320 | tf_op jit(solution)/shard_map/reduce_scatter | solution.py:202
  256.1 4.4 convolution_add_fusion.1
  260.4 35.1 %reduce-scatter.9.cloned.1.call-done = bf16[512,96]{0,1:T(8,128)(2,1)} async-done(((bf16[4096,96]{0,1:T(8,128)(2,1)}), bf16[512,96]{0,1:T(8,128)(2,1)}) %reduce-scatter.9.cloned.1.call-update) | async-done | bytes 98320 | tf_op jit(solution)/shard_map/reduce_scatter | solution.py:205
  295.6 3.9 fusion.2
  299.8 2.1 convert_multiply_fusion
  302.0 1.2 copy-done.3
  303.1 3.1 fusion.75
  306.9 1.8 convolution_convert_fusion.2
  308.8 1.3 convolution_convert_fusion.6
  310.2 1.3 convolution_convert_fusion.3
  311.5 1.3 convolution_convert_fusion.5
  312.8 1.3 convolution_convert_fusion.4
  314.2 56.4 %reduce-scatter.11.cloned.1.call-done = bf16[512,96]{0,1:T(8,128)(2,1)} async-done(((bf16[512,1536]{0,1:T(8,128)(2,1)}), bf16[512,96]{0,1:T(8,128)(2,1)}) %reduce-scatter.11.cloned.1.call-update) | async-done | bytes 98320 | tf_op jit(solution)/shard_map/reduce_scatter | solution.py:223
  370.6 1.0 fusion.36
  371.6 35.1 %psum.49 = f32[512]{0:T(512)S(1)} all-reduce(f32[512]{0:T(512)S(1)} %fusion.36), channel_id=1, replica_groups=mesh['seq'=8,'mp'=16] {'mp'}, use_global_device_ids=true, to_apply=%region_11.12 | all-reduce | flops 512 | bytes 4096 | tf_op jit(solution)/shard_map/psum | solution.py:227
  406.7 1.0 fusion.39
  412.2 30.1 %reduce-scatter.5.cloned.1.call-done = bf16[512,96]{0,1:T(8,128)(2,1)} async-done(((bf16[512,1536]{0,1:T(8,128)(2,1)}), bf16[512,96]{0,1:T(8,128)(2,1)}) %reduce-scatter.5.cloned.1.call-update) | async-done | bytes 98320 | tf_op jit(solution)/shard_map/reduce_scatter | solution.py:185
  442.3 1.6 add_convert_fusion.1
  443.9 15.0 %psum.51 = bf16[96]{0:T(256)(128)(2,1)S(1)} all-reduce(bf16[96]{0:T(256)(128)(2,1)S(1)} %get-tuple-element.48), channel_id=1, replica_groups=mesh['seq'=8,'mp'=16] {'seq'}, use_global_device_ids=true, to_apply=%region_14.15 | all-reduce | flops 96 | bytes 384 | tf_op jit(solution)/shard_map/psum | solution.py:248
  459.4 65.4 %all-reduce.3.cloned.1.call-done = (bf16[5,96,768]{2,1,0:T(8,128)(2,1)}, bf16[96,1536]{1,0:T(8,128)(2,1)}, bf16[96,1536]{1,0:T(8,128)(2,1)}, bf16[96,1536]{1,0:T(8,128)(2,1)}, bf16[96,1536]{1,0:T(8,128)(2,1)}) async-done(((bf16[5,96,768]{2,1,0:T(8,128)(2,1)}, bf16[96,1536]{1,0:T(8,128)(2,1)}, bf16[96,1536]{1,0:T(8,128)(2,1)}, bf16[96,1536]{1,0:T(8,128)(2,1)}, bf16[96,1536]{1,0:T(8,128)(2,1)}), ...) | async-done | bytes 1916944 | tf_op jit(solution)/shard_map/psum | solution.py:247
  524.8 2.4 convert_element_type.140
  (102 shorter events, 17.8 us)
Async XLA Ops:
  7.2 79.8 %copy-start = (bf16[96,1536]{1,0:T(8,128)(2,1)S(1)}, bf16[96,1536]{1,0:T(8,128)(2,1)}, u32[]{:S(2)}) copy-start(bf16[96,1536]{1,0:T(8,128)(2,1)} %param.15) | copy-start | bytes 884740
  7.2 1.6 copy-start.9
  7.2 1.6 copy-start.23
  7.2 70.2 %all-gather.5.cloned.1.call-start = ((), (), s32[]{:S(2)}) async-start(), calls=%async_computation.4 | async-start | bytes 1671168 | tf_op jit(solution)/shard_map/all_gather | solution.py:163
  8.8 8.1 %copy-start.22 = (bf16[5,96,768]{2,1,0:T(8,128)(2,1)S(1)}, bf16[5,96,768]{2,1,0:T(8,128)(2,1)}, u32[]{:S(2)}) copy-start(bf16[5,96,768]{2,1,0:T(8,128)(2,1)} %param.13) | copy-start | bytes 2211844
  11.6 5.9 %collective-permute-start = (bf16[2,768]{1,0:T(2,128)(2,1)S(1)}, bf16[2,768]{1,0:T(2,128)(2,1)S(1)}, u32[]{:S(2)}, u32[]{:S(2)}) collective-permute-start(bf16[2,768]{1,0:T(2,128)(2,1)S(1)} %get-tuple-element.61), channel_id=1, source_target_pairs={{0,16},{16,32},{32,48},{48,64},{64,80},{80,96},{96,112},{1,17},{17... | collective-permute-start | bytes 9224 | tf_op jit(solution)/shard_map/ppermute | solution.py:22
  15.6 4.3 collective-permute-start.1
  18.1 2.4 copy-start.24
  23.7 53.7 %copy-start.7 = (f32[512,96]{0,1:T(8,128)}, f32[512,96]{0,1:T(8,128)S(1)}, u32[]{:S(2)}) copy-start(f32[512,96]{0,1:T(8,128)S(1)} %copy.26) | copy-start | bytes 589828
  24.4 100.9 %all-gather.11.cloned.1.call-start = ((), (), s32[]{:S(2)}) async-start(), calls=%async_computation.8 | async-start | bytes 1671168 | tf_op jit(solution)/shard_map/all_gather | solution.py:189
  25.1 135.0 %all-gather.7.cloned.1.call-start = ((), (), s32[]{:S(2)}) async-start(), calls=%async_computation.5 | async-start | bytes 1769472 | tf_op jit(solution)/shard_map/all_gather | solution.py:177
  79.2 4.2 copy-start.5
  81.3 1.4 collective-permute-start.3
  83.4 118.7 %all-gather.9.cloned.1.call-start = ((), (), s32[]{:S(2)}) async-start(), calls=%async_computation.6 | async-start | bytes 1769472 | tf_op jit(solution)/shard_map/all_gather | solution.py:178
  84.8 1.4 collective-permute-start.4
  86.9 169.1 %reduce-scatter.7.cloned.1.call-start = ((), (), s32[]{:S(2)}) async-start(), calls=%async_computation.9 | async-start | bytes 884736 | tf_op jit(solution)/shard_map/reduce_scatter | solution.py:202
  88.1 39.6 %collective-permute-start.2 = (bf16[512,96]{0,1:T(8,128)(2,1)}, bf16[512,96]{0,1:T(8,128)(2,1)}, u32[]{:S(2)}, u32[]{:S(2)}) collective-permute-start(bf16[512,96]{0,1:T(8,128)(2,1)} %convolution_convert_fusion.15), channel_id=1, source_target_pairs={{0,1},{1,0},{2,3},{3,2},{4,5},{5,4},{6,7},{7,6},{8,9},{9,8},{10,11... | collective-permute-start | bytes 294920 | tf_op jit(solution)/shard_map/ppermute | solution.py:32
  127.2 39.1 %collective-permute-start.5 = (bf16[512,96]{0,1:T(8,128)(2,1)S(1)}, bf16[512,96]{0,1:T(8,128)(2,1)}, u32[]{:S(2)}, u32[]{:S(2)}) collective-permute-start(bf16[512,96]{0,1:T(8,128)(2,1)S(1)} %convolution_convert_fusion.12), channel_id=1, source_target_pairs={{0,1},{1,0},{2,3},{3,2},{4,5},{5,4},{6,7},{7,6},{8,9},{9,8},{10,11... | collective-permute-start | bytes 294920 | tf_op jit(solution)/shard_map/ppermute | solution.py:32
  163.1 3.2 copy-start.1
  202.0 6.3 %copy-start.2 = (f32[512,4096]{1,0:T(8,128)S(1)}, f32[512,4096]{1,0:T(8,128)}, u32[]{:S(2)}) copy-start(f32[512,4096]{1,0:T(8,128)} %copy-done.1) | copy-start | bytes 25165828
  212.8 2.0 copy-start.4
  217.3 78.2 %reduce-scatter.9.cloned.1.call-start = ((), (), s32[]{:S(2)}) async-start(), calls=%async_computation.10 | async-start | bytes 884736 | tf_op jit(solution)/shard_map/reduce_scatter | solution.py:205
  221.3 149.3 %reduce-scatter.11.cloned.1.call-start = ((), (), s32[]{:S(2)}) async-start(), calls=%async_computation.11 | async-start | bytes 1671168 | tf_op jit(solution)/shard_map/reduce_scatter | solution.py:223
  299.5 142.8 %reduce-scatter.5.cloned.1.call-start = ((), (), s32[]{:S(2)}) async-start(), calls=%async_computation.7 | async-start | bytes 1671168 | tf_op jit(solution)/shard_map/reduce_scatter | solution.py:185
  299.8 3.3 copy-start.3
  303.1 3.8 copy-start.10
  306.2 0.7 copy-start.18
  308.7 216.1 %all-reduce.3.cloned.1.call-start = ((), (), s32[]{:S(2)}) async-start(), calls=%async_computation.12 | async-start | bytes 3833856 | tf_op jit(solution)/shard_map/psum | solution.py:247
  308.8 1.4 copy-start.6
  308.8 1.4 copy-start.19
  308.8 2.7 copy-start.20
  310.2 2.7 copy-start.21
  312.8 93.9 %copy-start.13 = (bf16[512,96]{0,1:T(8,128)(2,1)S(1)}, bf16[512,96]{0,1:T(8,128)(2,1)}, u32[]{:S(2)}) copy-start(bf16[512,96]{0,1:T(8,128)(2,1)} %param.19) | copy-start | bytes 294916
  314.2 94.1 %copy-start.12 = (f32[1024,96]{0,1:T(8,128)S(1)}, f32[1024,96]{0,1:T(8,128)}, u32[]{:S(2)}) copy-start(f32[1024,96]{0,1:T(8,128)} %get-tuple-element.64) | copy-start | bytes 1179652
  411.3 0.9 copy-start.11
  411.3 31.0 %copy-start.8 = (f32[512,96]{0,1:T(8,128)S(1)}, f32[512,96]{0,1:T(8,128)}, u32[]{:S(2)}) copy-start(f32[512,96]{0,1:T(8,128)} %copy-done.7) | copy-start | bytes 589828
  524.8 2.4 copy-start.17
  524.8 3.3 copy-start.16
  524.8 4.2 copy-start.15
  527.2 2.6 copy-start.14
Sparse Core Ops, SparseCore 0:
  24.5 52.8 all-gather.4
  79.8 45.4 all-gather.10
  127.5 32.5 all-gather.6
  162.2 39.7 all-gather.8
  217.5 38.5 reduce-scatter.6
  258.5 37.0 reduce-scatter.8
  299.6 70.8 reduce-scatter.10
  374.4 67.8 reduce-scatter.4
  445.8 78.8 all-reduce.2
where the time goes:
time: 542 us; the launch traced here: 537 us
  waiting for transfers between devices  378 us (70%)
  matrix products  56 us (10%)
  blocking collectives  50.1 us (9%)
  other arithmetic  23.1 us (4%)
  between operations  14.2 us (3%)
  local copies, waits for them, and re-layouts  8.81 us (2%)
  starting transfers between devices  7.24 us (1%)
    psum x1, waiting for transfers between devices, body(): lax.psum(conv_grad.astype(jnp.bfloat16), 'seq').astype(jnp.float32)  65.4 us
    reduce_scatter x1, waiting for transfers between devices, body(): lax.psum_scatter(partial_norm.astype(jnp.bfloat16), 'mp', scatter_dimensi...  56.4 us
    all_gather x1, waiting for transfers between devices, body(): whole_tok = lax.all_gather(own_tok, 'mp', axis=1, tiled=True)  52.2 us
    all_gather x1, waiting for transfers between devices, body(): grad_full = lax.all_gather(cotangent, 'mp', axis=1, tiled=True)  36.9 us
    all_gather x1, waiting for transfers between devices, body(): lax.all_gather(value_head, 'seq', axis=0, tiled=True)  35.7 us
    reduce_scatter x1, waiting for transfers between devices, body(): lax.psum_scatter(value_sums.astype(jnp.bfloat16), 'seq', scatter_dimensio...  35.1 us
    psum x1, blocking collectives, body(): row_stat = lax.psum(jnp.sum(norm_cols * unit_cols, axis=1), 'mp') / D  35.1 us
    all_gather x1, waiting for transfers between devices, body(): lax.all_gather(key_head, 'seq', axis=0, tiled=True)  32.4 us
  transfers between devices with their start and end apart: 15, of which 12 were waited for; matrix products, arithmetic and copies ran while one was open for 9% of the time, Pallas kernels for 0%

commit v1 on v0

v1 whole, which is shorter than its diff:
```python
import functools

import jax
import jax.numpy as jnp
from jax import lax
from jax.experimental import pallas as pl
from jax.experimental.pallas import tpu as pltpu
from jax.sharding import PartitionSpec as P

D = 1536
CIN = 768
TAPS = 5
BIN_WIDTH = 64
EPS = 1e-06
HEAD = 192
SHARE = 96
TOK = 256
PAIRS = 512
WIDE = 640
BF = jnp.bfloat16
F32 = jnp.float32
MESH = pl.DeviceIdType.MESH
SCALE = HEAD ** (-0.5)
ROOT2PI = 0.7978845608028654

TOK_AG, COT_AG, OUT_RS, NORM_RS = 0, 16, 32, 48
G_RS, G_AG, C_RS, C_AG = 64, 72, 80, 88
W_SIB, HALO, Q_X, DO_X, ST_X, O_X, DQ_X = 96, 100, 104, 108, 112, 116, 120
KV_Z, KV_SIB, DKV_SIB, DKV_Z, G_SIB = 124, 125, 127, 129, 130
SEMS = 132


def mm(a, b):
    return jnp.dot(a, b, preferred_element_type=F32)


def nt(a, b):
    return lax.dot_general(a, b, (((1,), (1,)), ((), ())), preferred_element_type=F32)


def tn(a, b):
    return lax.dot_general(a, b, (((0,), (0,)), ((), ())), preferred_element_type=F32)


def kernel(
    feat, toks, bproj, cw, cbias, wq, wk, wv, wo, cot,
    o_layer, o_conv, o_bias, o_q, o_k, o_v, o_o,
    xf, r3, xe, halo, wt, w4, z, slope, tok_own, cot_own, tok_t, cot_t, norm_t,
    q, kv, kn, vn, do, et, dp, st, st_in, o_f, o_send, o_in, ot, fac,
    dq_f, dq_send, dq_in, dkv, dkv_send, dkv_in, z_send, z_in, dqkv, ng,
    n_send, n_in, a_send, a_in, g_part, g_send, g_sib, g_acc, g_in, g_red, g_all,
    pgs, c_send, c_in, c_red, c_all, ssem, rsem,
):
    s = lax.axis_index("seq")
    m = lax.axis_index("mp")
    zl = s // 4
    x = s % 4
    c = m % 2
    sib = (s, m + 1 - 2 * c)
    zpart = ((1 - zl) * 4 + x, m)
    sent = []

    def xpeer(r):
        return (zl * 4 + (x + r) % 4, m)

    def seqpeer(r):
        return ((s + r) % 8, m)

    def mppeer(r):
        return (s, (m + r) % 16)

    def push(src, dst, sem, dev):
        copy = pltpu.make_async_remote_copy(
            src_ref=src, dst_ref=dst, send_sem=ssem.at[sem], recv_sem=rsem.at[sem],
            device_id=dev, device_id_type=MESH,
        )
        copy.start()
        sent.append(copy)

    def land(dst, sem):
        pltpu.make_async_remote_copy(
            src_ref=dst, dst_ref=dst, send_sem=ssem.at[sem], recv_sem=rsem.at[sem],
            device_id=sib, device_id_type=MESH,
        ).wait_recv()

    def al(v, n):
        return pl.multiple_of(v, n)

    barrier = pltpu.get_barrier_semaphore()
    for r in range(1, 16):
        pl.semaphore_signal(barrier, inc=1, device_id=mppeer(r), device_id_type=MESH)
    for r in range(1, 8):
        pl.semaphore_signal(barrier, inc=1, device_id=seqpeer(r), device_id_type=MESH)

    bp = bproj[...]
    hi = bp.astype(BF).astype(F32)
    mid = (bp - hi).astype(BF).astype(F32)
    low = (bp - hi - mid).astype(BF).astype(F32)
    r3[...] = jnp.zeros_like(r3)
    for k, part in enumerate((hi, mid, low)):
        r3[8 * k : 8 * k + 4, 0:CIN] = part
        r3[8 * k + 4 : 8 * k + 8, CIN:D] = part
    lane = lax.broadcasted_iota(jnp.int32, (128, 32), 0)
    col = lax.broadcasted_iota(jnp.int32, (128, 32), 1)
    group = jnp.where(lane >= BIN_WIDTH, 4, 0)
    counts = jnp.zeros((PAIRS, 32), F32)
    for b in range(4):
        pick = jnp.where((col < 24) & (col % 8 == group + b), 1.0, 0.0).astype(BF)
        match = jnp.where(toks[...] == b, 1.0, 0.0).astype(BF)
        counts = counts + mm(match, pick)
    comp = (counts * (1.0 / BIN_WIDTH)).astype(BF)
    for k in range(6):
        xf[k] = feat[:, 128 * k : 128 * k + 128].astype(F32)
    for k in range(6):
        for half in range(2):
            lo = CIN * half + 128 * k
            extra = mm(comp, r3[:, lo : lo + 128].astype(BF))
            own = xf[k, pl.ds(half, PAIRS, stride=2), :]
            xe[0:PAIRS, lo : lo + 128] = (own + extra).astype(BF)

    pl.semaphore_wait(barrier, 22)
    push(xe.at[pl.ds(PAIRS - 16, 16)], halo.at[0], HALO, seqpeer(1))
    push(xe.at[pl.ds(0, 16)], halo.at[1], HALO + 1, seqpeer(7))
    for k, w in enumerate((wq, wk, wv, wo)):
        rows = pl.ds(al(HEAD * k + SHARE * c, 32), SHARE)
        push(w, w4.at[rows], W_SIB + k, sib)

    zero = jnp.zeros((SHARE, CIN), BF)
    left = (cw[0], zero, cw[2], cw[1], cw[4], cw[3])
    right = (cw[1], cw[0], cw[3], cw[2], zero, cw[4])
    for g in range(6):
        wt[SHARE * g : SHARE * g + SHARE, 0:CIN] = left[g]
        wt[SHARE * g : SHARE * g + SHARE, CIN:D] = right[g]

    @pl.loop(0, 2)
    def _(i):
        rows = pl.ds(al(i * 256, 256), 256)
        z[:, rows] = nt(wt[...], xe[rows, :])

    land(halo.at[0], HALO)
    land(halo.at[1], HALO + 1)
    at = lax.broadcasted_iota(jnp.int32, (16, D), 0)
    after = halo[1].astype(F32)
    before = halo[0].astype(F32)
    after = jnp.where((at == 0) & (s < 7), after, 0.0)
    before = jnp.where((at == 15) & (s > 0), before, 0.0)
    xe[PAIRS:WIDE, :] = jnp.zeros((WIDE - PAIRS, D), BF)
    xe[PAIRS : PAIRS + 16, :] = after.astype(BF)
    xe[WIDE - 16 : WIDE, :] = before.astype(BF)
    z[:, PAIRS:WIDE] = nt(wt[...], xe[PAIRS:WIDE, :])

    total = jnp.zeros((SHARE, PAIRS), F32)
    for half in range(2):
        r0, r1, r2 = (SHARE * (2 * d + half) for d in range(3))
        pre = pltpu.roll(z[r0 : r0 + SHARE, :], 1, 1)[:, 0:PAIRS]
        pre = pre + z[r1 : r1 + SHARE, 0:PAIRS]
        pre = pre + pltpu.roll(z[r2 : r2 + SHARE, :], WIDE - 1, 1)[:, 0:PAIRS]
        pre = pre + cbias[...]
        square = pre * pre
        bend = jnp.tanh(ROOT2PI * (pre + 0.044715 * (square * pre)))
        total = total + pre * (0.5 * (1.0 + bend))
        slope[half] = 0.5 * (1.0 + bend) + (0.5 * pre) * (1.0 - bend * bend) * (
            ROOT2PI * (1.0 + (3.0 * 0.044715) * square)
        )
    tok_own[...] = (0.5 * total).astype(BF)
    mine = pl.ds(al(SHARE * m, 32), SHARE)

    def spread(own, full, base):
        for r in range(1, 16):
            cols = pl.ds(al(TOK * ((m + r) % 2), TOK), TOK)
            push(own.at[:, cols], full.at[mine], base + r, mppeer(r))
        full[mine, :] = own[:, pl.ds(al(TOK * c, TOK), TOK)]

    def gathered(full, base):
        for r in range(1, 16):
            rows = pl.ds(al(SHARE * ((m - r + 16) % 16), 32), SHARE)
            land(full.at[rows], base + r)

    spread(tok_own, tok_t, TOK_AG)
    cot_own[...] = jnp.transpose(cot[...].astype(F32)).astype(BF)
    spread(cot_own, cot_t, COT_AG)

    for k, w in enumerate((wq, wk, wv, wo)):
        w4[pl.ds(al(HEAD * k + SHARE * c, 32), SHARE), :] = w[...]
    for k in range(4):
        land(w4.at[pl.ds(al(HEAD * k + SHARE * (1 - c), 32), SHARE)], W_SIB + k)

    gathered(tok_t, TOK_AG)
    wide = tok_t[...].astype(F32)
    inverse = lax.rsqrt(jnp.sum(wide * wide, axis=0, keepdims=True) * (1.0 / D) + EPS)
    norm_t[...] = (wide * inverse).astype(BF)
    qkv = mm(w4[0 : 3 * HEAD, :], norm_t[...]).astype(BF)
    q[0] = qkv[0:HEAD]
    kv[0] = qkv[HEAD : 3 * HEAD]
    push(kv.at[0], kv.at[2], KV_Z, zpart)
    push(kv.at[0], kv.at[1], KV_SIB, sib)
    for r in range(1, 4):
        push(q.at[0], q.at[r], Q_X + r, xpeer(r))

    gathered(cot_t, COT_AG)
    do[0] = mm(w4[3 * HEAD : 4 * HEAD, :], cot_t[...]).astype(BF)
    for r in range(1, 4):
        push(do.at[0], do.at[r], DO_X + r, xpeer(r))

    land(kv.at[2], KV_Z)
    push(kv.at[2], kv.at[3], KV_SIB + 1, sib)
    land(kv.at[1], KV_SIB)
    land(kv.at[3], KV_SIB + 1)
    for i in range(4):
        kn[i] = jnp.transpose(kv[i, 0:HEAD].astype(F32)).astype(BF)
        vn[i] = jnp.transpose(kv[i, HEAD : 2 * HEAD].astype(F32)).astype(BF)
    for r in range(1, 4):
        land(q.at[r], Q_X + r)
        land(do.at[r], DO_X + r)

    @pl.loop(0, 4)
    def _(j):
        top = jnp.full((1, TOK), -jnp.inf, F32)
        for i in range(4):
            scores = mm(kn[i], q[j]) * SCALE
            et[j, TOK * i : TOK * i + TOK, :] = scores
            top = jnp.maximum(top, jnp.max(scores, axis=0, keepdims=True))
        norm = jnp.zeros((1, TOK), F32)
        delta = jnp.zeros((1, TOK), F32)
        out = jnp.zeros((HEAD, TOK), F32)
        for i in range(4):
            rows = slice(TOK * i, TOK * i + TOK)
            e = jnp.exp(et[j, rows, :] - top)
            et[j, rows, :] = e
            norm = norm + jnp.sum(e, axis=0, keepdims=True)
            out = out + mm(kv[i, HEAD : 2 * HEAD, :], e.astype(BF))
            grad = mm(vn[i], do[j])
            dp[j, rows, :] = grad
            delta = delta + jnp.sum(e * grad, axis=0, keepdims=True)
        o_f[j] = out
        st[j, 0:1, :] = top
        st[j, 1:2, :] = norm
        st[j, 2:3, :] = delta
        st[j, 3:8, :] = jnp.zeros((5, TOK), F32)

    for r in range(1, 4):
        push(st, st_in.at[r], ST_X + r, xpeer(r))
    for r in range(1, 4):
        land(st_in.at[r], ST_X + r)

    factors = []
    deltas = []
    for j in range(4):
        every = [st[j]] + [st_in[r, (j - r) % 4] for r in range(1, 4)]
        top = functools.reduce(jnp.maximum, [e[0:1] for e in every])
        norm = sum(e[1:2] * jnp.exp(e[0:1] - top) for e in every)
        log_total = jnp.log(norm) + top
        factors.append(jnp.exp(every[0][0:1] - log_total))
        deltas.append(sum(e[2:3] * jnp.exp(e[0:1] - log_total) for e in every))
        o_f[j] = o_f[j] * factors[j]
    for j in range(4):
        fac[j, 0:1, :] = factors[j]
        fac[j, 1:2, :] = deltas[j]
    for r in range(1, 4):
        o_send[r] = o_f[r].astype(BF)
        push(o_send.at[r], o_in.at[4 - r], O_X + 4 - r, xpeer(4 - r))

    dkv[...] = jnp.zeros_like(dkv)

    @pl.loop(0, 4)
    def _(j):
        factor = fac[j, 0:1, :]
        delta = fac[j, 1:2, :]
        grad_q = jnp.zeros((HEAD, TOK), F32)
        for i in range(4):
            rows = slice(TOK * i, TOK * i + TOK)
            p = et[j, rows, :] * factor
            ds = (p * (dp[j, rows, :] - delta) * SCALE).astype(BF)
            grad_q = grad_q + mm(kv[i, 0:HEAD, :], ds)
            dkv[i, 0:HEAD, :] += nt(q[j], ds)
            dkv[i, HEAD : 2 * HEAD, :] += nt(do[j], p.astype(BF))
        dq_f[j] = grad_q

    dkv_send[0] = dkv[3].astype(BF)
    push(dkv_send.at[0], dkv_in.at[0], DKV_SIB, sib)
    dkv_send[1] = dkv[1].astype(BF)
    push(dkv_send.at[1], dkv_in.at[1], DKV_SIB + 1, sib)
    for r in range(1, 4):
        dq_send[r] = dq_f[r].astype(BF)
        push(dq_send.at[r], dq_in.at[4 - r], DQ_X + 4 - r, xpeer(4 - r))
    land(dkv_in.at[0], DKV_SIB)
    z_send[...] = (dkv[2] + dkv_in[0].astype(F32)).astype(BF)
    push(z_send, z_in, DKV_Z, zpart)

    for r in range(1, 4):
        land(o_in.at[r], O_X + r)
    ot[...] = (o_f[0] + sum(o_in[r].astype(F32) for r in range(1, 4))).astype(BF)

    def scatter(send, into, base):
        for r in range(1, 16):
            rows = pl.ds(al(SHARE * ((m + r) % 16), 32), SHARE)
            push(send.at[rows], into.at[r], base + r, mppeer(r))
        into[0] = send[mine, :]

    def reduced(into, base):
        for r in range(1, 16):
            land(into.at[r], base + r)
        same = sum(into[r].astype(F32) for r in range(0, 16, 2))
        other = sum(into[r].astype(F32) for r in range(1, 16, 2))
        first = jnp.where(c == 0, same, other)
        second = jnp.where(c == 0, other, same)
        return first, second

    @pl.loop(0, 4)
    def _(k):
        cols = pl.ds(al(384 * k, 128), 384)
        a_send[cols, :] = tn(w4[3 * HEAD : 4 * HEAD, cols], ot[...]).astype(BF)

    scatter(a_send, a_in, OUT_RS)

    land(dkv_in.at[1], DKV_SIB + 1)
    for r in range(1, 4):
        land(dq_in.at[r], DQ_X + r)
    grad_q = dq_f[0] + sum(dq_in[r].astype(F32) for r in range(1, 4))
    dqkv[0:HEAD, :] = grad_q.astype(BF)
    land(z_in, DKV_Z)
    dqkv[HEAD : 3 * HEAD, :] = (dkv[0] + dkv_in[1].astype(F32) + z_in[...].astype(F32)).astype(BF)

    @pl.loop(0, 4)
    def _(k):
        cols = pl.ds(al(384 * k, 128), 384)
        ng[cols, :] = tn(w4[0 : 3 * HEAD, cols], dqkv[...])

    wide = tok_t[...].astype(F32)
    inverse = lax.rsqrt(jnp.sum(wide * wide, axis=0, keepdims=True) * (1.0 / D) + EPS)
    unit = wide * inverse
    row_stat = jnp.sum(ng[...] * unit, axis=0, keepdims=True) * (1.0 / D)
    n_send[...] = (inverse * (ng[...] - unit * row_stat)).astype(BF)
    scatter(n_send, n_in, NORM_RS)

    @pl.loop(0, 4)
    def _(k):
        cols = pl.ds(al(384 * k, 128), 384)
        g_part[0 : 3 * HEAD, cols] = nt(dqkv[...], norm_t[cols, :])
        g_part[3 * HEAD : 4 * HEAD, cols] = nt(ot[...], cot_t[cols, :])

    for k in range(4):
        g_send[k] = g_part[pl.ds(al(HEAD * k + SHARE * (1 - c), 32), SHARE), :].astype(BF)
    push(g_send, g_sib, G_SIB, sib)
    land(g_sib, G_SIB)
    for k in range(4):
        own = g_part[pl.ds(al(HEAD * k + SHARE * c, 32), SHARE), :]
        g_acc[k] = (own + g_sib[k].astype(F32)).astype(BF)

    def g_piece(buf, seq):
        return buf.at[:, pl.ds(al(48 * (seq // 4), 16), 48), pl.ds(al(384 * (seq % 4), 128), 384)]

    for r in range(1, 8):
        push(g_piece(g_acc, (s + r) % 8), g_in.at[r], G_RS + r, seqpeer(r))

    tok_wide = tok_own[...].astype(F32)
    first, second = reduced(a_in, OUT_RS)
    out = jnp.concatenate([first, second], axis=1) + tok_wide
    o_layer[...] = jnp.transpose(out).astype(BF)

    first, second = reduced(n_in, NORM_RS)
    tok_grad = cot_own[...].astype(F32) + jnp.concatenate([first, second], axis=1)
    pad = jnp.zeros((SHARE, WIDE - PAIRS), F32)
    for half in range(2):
        pg = jnp.concatenate([0.5 * tok_grad * slope[half], pad], axis=1)
        for d in range(3):
            shift = (WIDE - 1, 0, 1)[d]
            moved = pltpu.roll(pg, shift, 1) if shift else pg
            row = SHARE * (2 * d + half)
            pgs[row : row + SHARE, :] = moved.astype(BF)
    both = pgs[2 * SHARE : 3 * SHARE, 0:PAIRS], pgs[3 * SHARE : 4 * SHARE, 0:PAIRS]
    ones = jnp.ones((16, PAIRS), BF)
    bias = nt(ones, both[0]) + nt(ones, both[1])
    c_send[TAPS * SHARE :, :] = jnp.zeros((32, CIN), BF)
    c_send[TAPS * SHARE : TAPS * SHARE + 16, 0:SHARE] = bias.astype(BF)

    @pl.loop(0, 3)
    def _(k):
        cols = pl.ds(al(256 * k, 256), 256)
        odd_cols = pl.ds(al(CIN + 256 * k, 256), 256)
        me = mm(pgs[...], xe[:, cols])
        mo = mm(pgs[...], xe[:, odd_cols])

        def part(arr, d, half):
            row = SHARE * (2 * (d + 1) + half)
            return arr[row : row + SHARE]

        taps = (
            part(me, -1, 0) + part(mo, -1, 1),
            part(mo, -1, 0) + part(me, 0, 1),
            part(me, 0, 0) + part(mo, 0, 1),
            part(mo, 0, 0) + part(me, 1, 1),
            part(me, 1, 0) + part(mo, 1, 1),
        )
        for t in range(TAPS):
            c_send[SHARE * t : SHARE * t + SHARE, cols] = taps[t].astype(BF)

    def c_piece(buf, seq):
        return buf.at[pl.ds(al(64 * seq, 64), 64)]

    for r in range(1, 8):
        push(c_piece(c_send, (s + r) % 8), c_in.at[r], C_RS + r, seqpeer(r))

    for r in range(1, 8):
        land(g_in.at[r], G_RS + r)
    own_rows = pl.ds(al(48 * zl, 16), 48)
    own_cols = pl.ds(al(384 * x, 128), 384)
    acc = g_acc[:, own_rows, own_cols].astype(F32)
    for r in range(1, 8):
        acc = acc + g_in[r].astype(F32)
    g_red[...] = acc.astype(BF)
    for r in range(1, 8):
        push(g_red, g_piece(g_all, s), G_AG + r, seqpeer(r))
    g_all[:, own_rows, own_cols] = g_red[...]

    for r in range(1, 8):
        land(c_in.at[r], C_RS + r)
    acc = c_send[pl.ds(al(64 * s, 64), 64), :].astype(F32)
    for r in range(1, 8):
        acc = acc + c_in[r].astype(F32)
    c_red[...] = acc.astype(BF)
    for r in range(1, 8):
        push(c_red, c_piece(c_all, s), C_AG + r, seqpeer(r))
    c_all[pl.ds(al(64 * s, 64), 64), :] = c_red[...]

    for r in range(1, 8):
        land(g_piece(g_all, (s - r + 8) % 8), G_AG + r)
    for k, o in enumerate((o_q, o_k, o_v, o_o)):
        o[...] = g_all[k].astype(F32)
    for r in range(1, 8):
        land(c_piece(c_all, (s - r + 8) % 8), C_AG + r)
    for t in range(TAPS):
        o_conv[t] = c_all[SHARE * t : SHARE * t + SHARE, :].astype(F32)
    o_bias[...] = c_all[TAPS * SHARE : TAPS * SHARE + 16, 0:SHARE].astype(F32)[0:1]
    for copy in sent:
        copy.wait_send()


def scratch():
    def v(*shape, dtype=BF):
        return pltpu.VMEM(shape, dtype)

    return [
        v(6, 1024, 128, dtype=F32), v(32, D, dtype=F32), v(WIDE, D), v(2, 16, D), v(576, D), v(768, D),
        v(576, WIDE, dtype=F32), v(2, SHARE, PAIRS, dtype=F32), v(SHARE, PAIRS), v(SHARE, PAIRS),
        v(D, TOK), v(D, TOK), v(D, TOK),
        v(4, HEAD, TOK), v(4, 384, TOK), v(4, TOK, HEAD), v(4, TOK, HEAD), v(4, HEAD, TOK),
        v(4, 1024, TOK, dtype=F32), v(4, 1024, TOK, dtype=F32),
        v(4, 8, TOK, dtype=F32), v(4, 4, 8, TOK, dtype=F32),
        v(4, HEAD, TOK, dtype=F32), v(4, HEAD, TOK), v(4, HEAD, TOK), v(HEAD, TOK),
        v(4, 8, TOK, dtype=F32),
        v(4, HEAD, TOK, dtype=F32), v(4, HEAD, TOK), v(4, HEAD, TOK),
        v(4, 384, TOK, dtype=F32), v(2, 384, TOK), v(2, 384, TOK), v(384, TOK), v(384, TOK),
        v(576, TOK), v(D, TOK, dtype=F32),
        v(D, TOK), v(16, SHARE, TOK), v(D, TOK), v(16, SHARE, TOK),
        v(768, D, dtype=F32), v(4, SHARE, D), v(4, SHARE, D), v(4, SHARE, D),
        v(8, 4, 48, 384), v(4, 48, 384), v(4, SHARE, D),
        v(576, WIDE), v(512, CIN), v(8, 64, CIN), v(64, CIN), v(512, CIN),
        pltpu.SemaphoreType.DMA((SEMS,)), pltpu.SemaphoreType.DMA((SEMS,)),
    ]


def body(features, base_tokens, base_proj, conv_weight, conv_bias, w_query, w_key, w_value, w_out, cotangent):
    vmem = pl.BlockSpec(memory_space=pltpu.VMEM)
    square = jax.ShapeDtypeStruct((SHARE, D), F32)
    outs = pl.pallas_call(
        kernel,
        out_shape=(
            jax.ShapeDtypeStruct((PAIRS, SHARE), BF),
            jax.ShapeDtypeStruct((TAPS, SHARE, CIN), F32),
            jax.ShapeDtypeStruct((1, SHARE), F32),
            square, square, square, square,
        ),
        in_specs=[vmem] * 10,
        out_specs=(vmem,) * 7,
        scratch_shapes=scratch(),
        compiler_params=pltpu.CompilerParams(
            collective_id=0, has_side_effects=True, vmem_limit_bytes=60 * 1024 * 1024
        ),
        cost_estimate=pl.CostEstimate(flops=8_000_000_000, bytes_accessed=8_000_000, transcendentals=1_300_000),
        name="section",
    )(
        features, base_tokens.reshape(PAIRS, 128), base_proj, conv_weight, conv_bias.reshape(SHARE, 1),
        w_query, w_key, w_value, w_out, cotangent,
    )
    layer, conv, bias, gq, gk, gv, go = outs
    return layer, conv, bias.reshape(SHARE), gq, gk, gv, go


def solution(mesh):
    placed = (
        P("seq", None), P("seq"), P(), P(None, "mp", None), P("mp"),
        P("mp", None), P("mp", None), P("mp", None), P("mp", None), P("seq", "mp"),
    )
    return jax.shard_map(
        body,
        mesh=mesh,
        in_specs=placed,
        out_specs=(
            P("seq", "mp"), P(None, "mp", None), P("mp"),
            P("mp", None), P("mp", None), P("mp", None), P("mp", None),
        ),
        check_vma=False,
    )
```

time: 542 us -> 140 us (0.26)
  waiting for transfers between devices: 378 us -> 0 us
  Pallas kernels: 0 us -> 126 us
  matrix products: 56 us -> 0 us
  blocking collectives: 50.1 us -> 0 us
  other arithmetic: 23.1 us -> 0 us
  between operations: 14.2 us -> 0.65 us
  starting transfers between devices: 7.24 us -> 0 us
    all_gather x4 -> x0, waiting for transfers between devices: 157 us -> none  [the longest x1 52.2 us: body(): whole_tok = lax.all_gather(own_tok, 'mp', axis=1, tiled=True)]
    reduce_scatter x4 -> x0, waiting for transfers between devices: 150 us -> none  [the longest x1 56.4 us: body(): lax.psum_scatter(partial_norm.astype(jnp.bfloat16), 'mp', scatter_dimensi...]
    pallas_call x0 -> x1, Pallas kernels: none -> 126 us  [body(): pl.pallas_call(kernel, out_shape=(jax.ShapeDtypeStruct((PAIRS, SHARE), BF...]
    psum x1 -> x0, waiting for transfers between devices: 65.4 us -> none  [body(): lax.psum(conv_grad.astype(jnp.bfloat16), 'seq').astype(jnp.float32)]
    dot_general x29 -> x0, matrix products: 56 us -> none  [the longest x1 6.23 us: one_block(): lax.dot_general(row_grads, value_rows, (((1,), (1,)), ((), ())), preferre...]
    psum x2 -> x0, blocking collectives: 50.1 us -> none  [the longest x1 35.1 us: body(): row_stat = lax.psum(jnp.sum(norm_cols * unit_cols, axis=1), 'mp') / D]
    convert_element_type x9 -> x0, other arithmetic: 13.1 us -> none  [the longest x1 4.46 us: one_block(): (attn_probs * (grad_probs - row_delta) * score_scale).astype(jnp.bfloat16)]
    ppermute x6 -> x0, starting transfers between devices: 6.66 us -> none  [the longest x1 3.94 us: with_halo(): lax.ppermute(tail, axis, [(i, (i + 1) % count) for i in range(ends)])]
  transfers between devices with their start and end apart: 15 -> 0, of which waited for: 12 -> 0; matrix products, arithmetic and copies ran while one was open for 9% -> 0% of each run, Pallas kernels for 0% -> 0%
where the time goes in v1:
time: 140 us; the launch traced here: 138 us
  Pallas kernels  126 us (90%)
  local copies, waits for them, and re-layouts  11.2 us (8%)
    pallas_call x1, Pallas kernels, body(): pl.pallas_call(kernel, out_shape=(jax.ShapeDtypeStruct((PAIRS, SHARE), BF...  126 us
    unnamed x18, local copies, waits for them, and re-layouts  9.79 us

profile of v1, /device:TPU:1, one launch (start us, length us, event | category | flops | bytes accessed | tf_op | source)
XLA Modules:
  0.0 138.2 jit_solution(10861947858586077282)
XLA Ops:
  0.6 1.4 copy.17.cbias
  2.0 1.7 %copy.18.cot = bf16[512,96]{1,0:T(8,128)(2,1)} copy(bf16[512,96]{0,1:T(8,128)(2,1)} %param.19) | data formatting | bytes 196608 | tf_op args[9]
  3.7 126.4 %section.1 = (bf16[512,96]{1,0:T(8,128)(2,1)}, f32[5,96,768]{2,1,0:T(8,128)}, f32[1,96]{1,0:T(1,128)}, f32[96,1536]{1,0:T(8,128)}, f32[96,1536]{1,0:T(8,128)}, /*index=5*/f32[96,1536]{1,0:T(8,128)}, f32[96,1536]{1,0:T(8,128)}) custom-call(bf16[1024,768]{1,0:T(8,128)(2,1)} %feat.1, s32[512,128]{1,0:T(8,128)} %bitcast.4, f32[4,768]{1,0:T(4,128)} %bproj.1, ...), custom_call_target="tpu_custom_call" | custom-call | flops 8000000000 | bytes 8000000 | tf_op jit(solution)/shard_map/section/pallas_call | solution.py:466
  130.0 1.6 %copy.19 = bf16[512,96]{0,1:T(8,128)(2,1)} copy(bf16[512,96]{1,0:T(8,128)(2,1)} %get-tuple-element.21) | data formatting | bytes 196608
  131.7 0.0 copy-start.4
  131.7 0.0 copy-start.3
  131.7 0.0 copy-start.2
  131.7 2.7 %copy.26 = f32[5,96,768]{2,1,0:T(8,128)} copy(f32[5,96,768]{2,1,0:T(8,128)} %get-tuple-element.36) | data formatting | bytes 2949120
  134.4 0.0 copy-done.4
  134.4 0.0 copy-start.1
  134.4 0.5 copy.27
  134.9 0.0 copy-done.3
  134.9 0.8 copy.28
  135.7 0.0 copy-done.2
  135.7 0.0 copy-start
  135.7 0.8 copy.29
  136.5 0.0 copy-done.1
  136.6 0.8 copy.30
  137.4 0.0 copy-done
  137.4 0.8 copy.31
Async XLA Ops:
  131.7 2.7 %copy-start.4 = (f32[1,96]{1,0:T(1,128)S(1)}, f32[1,96]{1,0:T(1,128)}, u32[]{:S(2)}) copy-start(f32[1,96]{1,0:T(1,128)} %get-tuple-element.16) | copy-start | bytes 1156
  131.7 3.2 %copy-start.3 = (f32[96,1536]{1,0:T(8,128)S(1)}, f32[96,1536]{1,0:T(8,128)}, u32[]{:S(2)}) copy-start(f32[96,1536]{1,0:T(8,128)} %get-tuple-element.38) | copy-start | bytes 1769476
  131.7 4.1 %copy-start.2 = (f32[96,1536]{1,0:T(8,128)S(1)}, f32[96,1536]{1,0:T(8,128)}, u32[]{:S(2)}) copy-start(f32[96,1536]{1,0:T(8,128)} %get-tuple-element.39) | copy-start | bytes 1769476
  134.4 2.2 %copy-start.1 = (f32[96,1536]{1,0:T(8,128)S(1)}, f32[96,1536]{1,0:T(8,128)}, u32[]{:S(2)}) copy-start(f32[96,1536]{1,0:T(8,128)} %get-tuple-element.40) | copy-start | bytes 1769476
  135.7 1.6 %copy-start = (f32[96,1536]{1,0:T(8,128)S(1)}, f32[96,1536]{1,0:T(8,128)}, u32[]{:S(2)}) copy-start(f32[96,1536]{1,0:T(8,128)} %get-tuple-element.41) | copy-start | bytes 1769476

commit v2 on v1

--- a/solution.py
+++ b/solution.py
@@ -24,10 +24,10 @@
 ROOT2PI = 0.7978845608028654
 
 TOK_AG, COT_AG, OUT_RS, NORM_RS = 0, 16, 32, 48
-G_RS, G_AG, C_RS, C_AG = 64, 72, 80, 88
+C_RS, C_AG = 80, 88
 W_SIB, HALO, Q_X, DO_X, ST_X, O_X, DQ_X = 96, 100, 104, 108, 112, 116, 120
-KV_Z, KV_SIB, DKV_SIB, DKV_Z, G_SIB = 124, 125, 127, 129, 130
-SEMS = 132
+KV_Z, KV_SIB, DKV_SIB, DKV_Z, G_SIB, G_RS, G_AG = 124, 125, 127, 129, 130, 136, 168
+SEMS = 200
 
 
 def mm(a, b):
@@ -43,13 +43,13 @@
 
 
 def kernel(
-    feat, toks, bproj, cw, cbias, wq, wk, wv, wo, cot,
-    o_layer, o_conv, o_bias, o_q, o_k, o_v, o_o,
-    xf, r3, xe, halo, wt, w4, z, slope, tok_own, cot_own, tok_t, cot_t, norm_t,
+    feat_hbm, toks_hbm, bproj, cw_hbm, cbias, wq, wk, wv, wo, cot_hbm,
+    o_layer, c_all, g_all,
+    feat, toks, cw, xf, r3, xe, halo, wt, w4, z, slope, tok_own, cot_own, tok_t, cot_t, norm_t,
     q, kv, kn, vn, do, et, dp, st, st_in, o_f, o_send, o_in, ot, fac,
     dq_f, dq_send, dq_in, dkv, dkv_send, dkv_in, z_send, z_in, dqkv, ng,
-    n_send, n_in, a_send, a_in, g_part, g_send, g_sib, g_acc, g_in, g_red, g_all,
-    pgs, c_send, c_in, c_red, c_all, ssem, rsem,
+    n_send, n_in, a_send, a_in, g_part, g_send, g_sib, g_acc, g_in, g_red,
+    pgs, c_send, c_in, c_red, ssem, rsem, lsem,
 ):
     s = lax.axis_index("seq")
     m = lax.axis_index("mp")
@@ -91,6 +91,38 @@
         pl.semaphore_signal(barrier, inc=1, device_id=mppeer(r), device_id_type=MESH)
     for r in range(1, 8):
         pl.semaphore_signal(barrier, inc=1, device_id=seqpeer(r), device_id_type=MESH)
+
+    loads = [
+        pltpu.make_async_copy(toks_hbm, toks, lsem.at[0]),
+        pltpu.make_async_copy(feat_hbm, feat, lsem.at[1]),
+        pltpu.make_async_copy(cw_hbm, cw, lsem.at[2]),
+        pltpu.make_async_copy(cot_hbm, cot_own, lsem.at[3]),
+    ]
+    for k, w in enumerate((wq, wk, wv, wo)):
+        rows = pl.ds(al(HEAD * k + SHARE * c, 32), SHARE)
+        loads.append(pltpu.make_async_copy(w, w4.at[rows], lsem.at[4 + k]))
+    for load in loads:
+        load.start()
+    mine = pl.ds(al(SHARE * m, 32), SHARE)
+
+    def spread(own, full, base):
+        for r in range(1, 16):
+            cols = pl.ds(al(TOK * ((m + r) % 2), TOK), TOK)
+            push(own.at[:, cols], full.at[mine], base + r, mppeer(r))
+
+    def keep(own, full):
+        full[mine, :] = own[:, pl.ds(al(TOK * c, TOK), TOK)]
+
+    def gathered(full, base):
+        for r in range(1, 16):
+            rows = pl.ds(al(SHARE * ((m - r + 16) % 16), 32), SHARE)
+            land(full.at[rows], base + r)
+
+    pl.semaphore_wait(barrier, 22)
+    spread(cot_hbm, cot_t, COT_AG)
+    for k, w in enumerate((wo, wq, wk, wv)):
+        rows = pl.ds(al(HEAD * ((k + 3) % 4) + SHARE * c, 32), SHARE)
+        push(w, w4.at[rows], W_SIB + (k + 3) % 4, sib)
 
     bp = bproj[...]
     hi = bp.astype(BF).astype(F32)
@@ -104,27 +136,26 @@
     col = lax.broadcasted_iota(jnp.int32, (128, 32), 1)
     group = jnp.where(lane >= BIN_WIDTH, 4, 0)
     counts = jnp.zeros((PAIRS, 32), F32)
+    loads[0].wait()
     for b in range(4):
         pick = jnp.where((col < 24) & (col % 8 == group + b), 1.0, 0.0).astype(BF)
         match = jnp.where(toks[...] == b, 1.0, 0.0).astype(BF)
         counts = counts + mm(match, pick)
     comp = (counts * (1.0 / BIN_WIDTH)).astype(BF)
+    loads[1].wait()
     for k in range(6):
         xf[k] = feat[:, 128 * k : 128 * k + 128].astype(F32)
-    for k in range(6):
+    for k in range(0, 6, 2):
         for half in range(2):
             lo = CIN * half + 128 * k
-            extra = mm(comp, r3[:, lo : lo + 128].astype(BF))
-            own = xf[k, pl.ds(half, PAIRS, stride=2), :]
-            xe[0:PAIRS, lo : lo + 128] = (own + extra).astype(BF)
-
-    pl.semaphore_wait(barrier, 22)
+            extra = mm(comp, r3[:, lo : lo + 256].astype(BF))
+            for i in range(2):
+                own = xf[k + i, pl.ds(half, PAIRS, stride=2), :]
+                xe[0:PAIRS, lo + 128 * i : lo + 128 * i + 128] = (own + extra[:, 128 * i : 128 * i + 128]).astype(BF)
+
     push(xe.at[pl.ds(PAIRS - 16, 16)], halo.at[0], HALO, seqpeer(1))
     push(xe.at[pl.ds(0, 16)], halo.at[1], HALO + 1, seqpeer(7))
-    for k, w in enumerate((wq, wk, wv, wo)):
-        rows = pl.ds(al(HEAD * k + SHARE * c, 32), SHARE)
-        push(w, w4.at[rows], W_SIB + k, sib)
-
+    loads[2].wait()
     zero = jnp.zeros((SHARE, CIN), BF)
     left = (cw[0], zero, cw[2], cw[1], cw[4], cw[3])
     right = (cw[1], cw[0], cw[3], cw[2], zero, cw[4])
@@ -149,13 +180,14 @@
     xe[WIDE - 16 : WIDE, :] = before.astype(BF)
     z[:, PAIRS:WIDE] = nt(wt[...], xe[PAIRS:WIDE, :])
 
+    offset = jnp.transpose(jnp.broadcast_to(cbias[...], (128, SHARE)))[:, 0:1]
     total = jnp.zeros((SHARE, PAIRS), F32)
     for half in range(2):
         r0, r1, r2 = (SHARE * (2 * d + half) for d in range(3))
         pre = pltpu.roll(z[r0 : r0 + SHARE, :], 1, 1)[:, 0:PAIRS]
         pre = pre + z[r1 : r1 + SHARE, 0:PAIRS]
         pre = pre + pltpu.roll(z[r2 : r2 + SHARE, :], WIDE - 1, 1)[:, 0:PAIRS]
-        pre = pre + cbias[...]
+        pre = pre + offset
         square = pre * pre
         bend = jnp.tanh(ROOT2PI * (pre + 0.044715 * (square * pre)))
         total = total + pre * (0.5 * (1.0 + bend))
@@ -163,28 +195,17 @@
             ROOT2PI * (1.0 + (3.0 * 0.044715) * square)
         )
     tok_own[...] = (0.5 * total).astype(BF)
-    mine = pl.ds(al(SHARE * m, 32), SHARE)
-
-    def spread(own, full, base):
-        for r in range(1, 16):
-            cols = pl.ds(al(TOK * ((m + r) % 2), TOK), TOK)
-            push(own.at[:, cols], full.at[mine], base + r, mppeer(r))
-        full[mine, :] = own[:, pl.ds(al(TOK * c, TOK), TOK)]
-
-    def gathered(full, base):
-        for r in range(1, 16):
-            rows = pl.ds(al(SHARE * ((m - r + 16) % 16), 32), SHARE)
-            land(full.at[rows], base + r)
-
     spread(tok_own, tok_t, TOK_AG)
-    cot_own[...] = jnp.transpose(cot[...].astype(F32)).astype(BF)
-    spread(cot_own, cot_t, COT_AG)
-
-    for k, w in enumerate((wq, wk, wv, wo)):
-        w4[pl.ds(al(HEAD * k + SHARE * c, 32), SHARE), :] = w[...]
+    keep(tok_own, tok_t)
+    for load in loads[3:]:
+        load.wait()
     for k in range(4):
         land(w4.at[pl.ds(al(HEAD * k + SHARE * (1 - c), 32), SHARE)], W_SIB + k)
-
+    keep(cot_own, cot_t)
+    gathered(cot_t, COT_AG)
+    do[0] = mm(w4[3 * HEAD : 4 * HEAD, :], cot_t[...]).astype(BF)
+    for r in range(1, 4):
+        push(do.at[0], do.at[r], DO_X + r, xpeer(r))
     gathered(tok_t, TOK_AG)
     wide = tok_t[...].astype(F32)
     inverse = lax.rsqrt(jnp.sum(wide * wide, axis=0, keepdims=True) * (1.0 / D) + EPS)
@@ -196,11 +217,6 @@
     push(kv.at[0], kv.at[1], KV_SIB, sib)
     for r in range(1, 4):
         push(q.at[0], q.at[r], Q_X + r, xpeer(r))
-
-    gathered(cot_t, COT_AG)
-    do[0] = mm(w4[3 * HEAD : 4 * HEAD, :], cot_t[...]).astype(BF)
-    for r in range(1, 4):
-        push(do.at[0], do.at[r], DO_X + r, xpeer(r))
 
     land(kv.at[2], KV_Z)
     push(kv.at[2], kv.at[3], KV_SIB + 1, sib)
@@ -287,6 +303,21 @@
     z_send[...] = (dkv[2] + dkv_in[0].astype(F32)).astype(BF)
     push(z_send, z_in, DKV_Z, zpart)
 
+    def grad_w(k, grads, inputs):
+        g_part[HEAD * k : HEAD * k + HEAD, :] = nt(grads[...], inputs[...])
+        g_send[k] = g_part[pl.ds(al(HEAD * k + SHARE * (1 - c), 32), SHARE), :].astype(BF)
+        push(g_send.at[k], g_sib.at[k], G_SIB + k, sib)
+
+    def grad_sum(k):
+        land(g_sib.at[k], G_SIB + k)
+        own = g_part[pl.ds(al(HEAD * k + SHARE * c, 32), SHARE), :]
+        g_acc[k] = (own + g_sib[k].astype(F32)).astype(BF)
+        for r in range(1, 8):
+            push(g_piece(g_acc, k, (s + r) % 8), g_in.at[r, k], G_RS + 8 * k + r, seqpeer(r))
+
+    def g_piece(buf, k, seq):
+        return buf.at[k, pl.ds(al(48 * (seq // 4), 16), 48), pl.ds(al(384 * (seq % 4), 128), 384)]
+
     for r in range(1, 4):
         land(o_in.at[r], O_X + r)
     ot[...] = (o_f[0] + sum(o_in[r].astype(F32) for r in range(1, 4))).astype(BF)
@@ -312,6 +343,7 @@
         a_send[cols, :] = tn(w4[3 * HEAD : 4 * HEAD, cols], ot[...]).astype(BF)
 
     scatter(a_send, a_in, OUT_RS)
+    grad_w(3, ot, cot_t)
 
     land(dkv_in.at[1], DKV_SIB + 1)
     for r in range(1, 4):
@@ -333,30 +365,15 @@
     n_send[...] = (inverse * (ng[...] - unit * row_stat)).astype(BF)
     scatter(n_send, n_in, NORM_RS)
 
-    @pl.loop(0, 4)
-    def _(k):
-        cols = pl.ds(al(384 * k, 128), 384)
-        g_part[0 : 3 * HEAD, cols] = nt(dqkv[...], norm_t[cols, :])
-        g_part[3 * HEAD : 4 * HEAD, cols] = nt(ot[...], cot_t[cols, :])
-
-    for k in range(4):
-        g_send[k] = g_part[pl.ds(al(HEAD * k + SHARE * (1 - c), 32), SHARE), :].astype(BF)
-    push(g_send, g_sib, G_SIB, sib)
-    land(g_sib, G_SIB)
-    for k in range(4):
-        own = g_part[pl.ds(al(HEAD * k + SHARE * c, 32), SHARE), :]
-        g_acc[k] = (own + g_sib[k].astype(F32)).astype(BF)
-
-    def g_piece(buf, seq):
-        return buf.at[:, pl.ds(al(48 * (seq // 4), 16), 48), pl.ds(al(384 * (seq % 4), 128), 384)]
-
-    for r in range(1, 8):
-        push(g_piece(g_acc, (s + r) % 8), g_in.at[r], G_RS + r, seqpeer(r))
+    for k in range(3):
+        grad_w(k, dqkv.at[HEAD * k : HEAD * k + HEAD], norm_t)
+    for k in (3, 0, 1, 2):
+        grad_sum(k)
 
     tok_wide = tok_own[...].astype(F32)
     first, second = reduced(a_in, OUT_RS)
     out = jnp.concatenate([first, second], axis=1) + tok_wide
-    o_layer[...] = jnp.transpose(out).astype(BF)
+    o_layer[...] = out.astype(BF)
 
     first, second = reduced(n_in, NORM_RS)
     tok_grad = cot_own[...].astype(F32) + jnp.concatenate([first, second], axis=1)
@@ -401,17 +418,17 @@
     for r in range(1, 8):
         push(c_piece(c_send, (s + r) % 8), c_in.at[r], C_RS + r, seqpeer(r))
 
-    for r in range(1, 8):
-        land(g_in.at[r], G_RS + r)
     own_rows = pl.ds(al(48 * zl, 16), 48)
     own_cols = pl.ds(al(384 * x, 128), 384)
-    acc = g_acc[:, own_rows, own_cols].astype(F32)
-    for r in range(1, 8):
-        acc = acc + g_in[r].astype(F32)
-    g_red[...] = acc.astype(BF)
-    for r in range(1, 8):
-        push(g_red, g_piece(g_all, s), G_AG + r, seqpeer(r))
-    g_all[:, own_rows, own_cols] = g_red[...]
+    for k in (3, 0, 1, 2):
+        acc = g_acc[k, own_rows, own_cols].astype(F32)
+        for r in range(1, 8):
+            land(g_in.at[r, k], G_RS + 8 * k + r)
+            acc = acc + g_in[r, k].astype(F32)
+        g_red[k] = acc.astype(BF)
+        for r in range(1, 8):
+            push(g_red.at[k], g_piece(g_all, k, s), G_AG + 8 * k + r, seqpeer(r))
+        g_all[k, own_rows, own_cols] = g_red[k]
 
     for r in range(1, 8):
         land(c_in.at[r], C_RS + r)
@@ -424,14 +441,10 @@
     c_all[pl.ds(al(64 * s, 64), 64), :] = c_red[...]
 
     for r in range(1, 8):
-        land(g_piece(g_all, (s - r + 8) % 8), G_AG + r)
-    for k, o in enumerate((o_q, o_k, o_v, o_o)):
-        o[...] = g_all[k].astype(F32)
+        for k in range(4):
+            land(g_piece(g_all, k, (s - r + 8) % 8), G_AG + 8 * k + r)
     for r in range(1, 8):
         land(c_piece(c_all, (s - r + 8) % 8), C_AG + r)
-    for t in range(TAPS):
-        o_conv[t] = c_all[SHARE * t : SHARE * t + SHARE, :].astype(F32)
-    o_bias[...] = c_all[TAPS * SHARE : TAPS * SHARE + 16, 0:SHARE].astype(F32)[0:1]
     for copy in sent:
         copy.wait_send()
 
@@ -441,6 +454,7 @@
         return pltpu.VMEM(shape, dtype)
 
     return [
+        v(1024, CIN), v(PAIRS, 128, dtype=jnp.int32), v(TAPS, SHARE, CIN),
         v(6, 1024, 128, dtype=F32), v(32, D, dtype=F32), v(WIDE, D), v(2, 16, D), v(576, D), v(768, D),
         v(576, WIDE, dtype=F32), v(2, SHARE, PAIRS, dtype=F32), v(SHARE, PAIRS), v(SHARE, PAIRS),
         v(D, TOK), v(D, TOK), v(D, TOK),
@@ -454,25 +468,30 @@
         v(576, TOK), v(D, TOK, dtype=F32),
         v(D, TOK), v(16, SHARE, TOK), v(D, TOK), v(16, SHARE, TOK),
         v(768, D, dtype=F32), v(4, SHARE, D), v(4, SHARE, D), v(4, SHARE, D),
-        v(8, 4, 48, 384), v(4, 48, 384), v(4, SHARE, D),
-        v(576, WIDE), v(512, CIN), v(8, 64, CIN), v(64, CIN), v(512, CIN),
-        pltpu.SemaphoreType.DMA((SEMS,)), pltpu.SemaphoreType.DMA((SEMS,)),
+        v(8, 4, 48, 384), v(4, 48, 384),
+        v(576, WIDE), v(512, CIN), v(8, 64, CIN), v(64, CIN),
+        pltpu.SemaphoreType.DMA((SEMS,)), pltpu.SemaphoreType.DMA((SEMS,)), pltpu.SemaphoreType.DMA((8,)),
     ]
+
+
+def widen(layer, conv, grads, o_layer, o_conv, o_bias, o_q, o_k, o_v, o_o):
+    for t in range(TAPS):
+        o_conv[t] = conv[SHARE * t : SHARE * t + SHARE, :].astype(F32)
+    o_bias[...] = conv[TAPS * SHARE : TAPS * SHARE + 16, 0:SHARE].astype(F32)[0:1]
+    for k, o in enumerate((o_q, o_k, o_v, o_o)):
+        o[...] = grads[k].astype(F32)
+    o_layer[...] = layer[...]
 
 
 def body(features, base_tokens, base_proj, conv_weight, conv_bias, w_query, w_key, w_value, w_out, cotangent):
     vmem = pl.BlockSpec(memory_space=pltpu.VMEM)
-    square = jax.ShapeDtypeStruct((SHARE, D), F32)
-    outs = pl.pallas_call(
+    hbm = pl.BlockSpec(memory_space=pl.ANY)
+    layer = jax.ShapeDtypeStruct((SHARE, PAIRS), BF)
+    narrow = pl.pallas_call(
         kernel,
-        out_shape=(
-            jax.ShapeDtypeStruct((PAIRS, SHARE), BF),
-            jax.ShapeDtypeStruct((TAPS, SHARE, CIN), F32),
-            jax.ShapeDtypeStruct((1, SHARE), F32),
-            square, square, square, square,
-        ),
-        in_specs=[vmem] * 10,
-        out_specs=(vmem,) * 7,
+        out_shape=(layer, jax.ShapeDtypeStruct((512, CIN), BF), jax.ShapeDtypeStruct((4, SHARE, D), BF)),
+        in_specs=[hbm, hbm, vmem, hbm, vmem, hbm, hbm, hbm, hbm, hbm],
+        out_specs=(vmem,) * 3,
         scratch_shapes=scratch(),
         compiler_params=pltpu.CompilerParams(
             collective_id=0, has_side_effects=True, vmem_limit_bytes=60 * 1024 * 1024
@@ -480,11 +499,22 @@
         cost_estimate=pl.CostEstimate(flops=8_000_000_000, bytes_accessed=8_000_000, transcendentals=1_300_000),
         name="section",
     )(
-        features, base_tokens.reshape(PAIRS, 128), base_proj, conv_weight, conv_bias.reshape(SHARE, 1),
-        w_query, w_key, w_value, w_out, cotangent,
+        features, base_tokens.reshape(PAIRS, 128), base_proj, conv_weight, conv_bias.reshape(1, SHARE),
+        w_query, w_key, w_value, w_out, cotangent.T,
     )
-    layer, conv, bias, gq, gk, gv, go = outs
-    return layer, conv, bias.reshape(SHARE), gq, gk, gv, go
+    square = jax.ShapeDtypeStruct((SHARE, D), F32)
+    layer, conv, bias, gq, gk, gv, go = pl.pallas_call(
+        widen,
+        out_shape=(
+            layer, jax.ShapeDtypeStruct((TAPS, SHARE, CIN), F32), jax.ShapeDtypeStruct((1, SHARE), F32),
+            square, square, square, square,
+        ),
+        in_specs=[vmem] * 3,
+        out_specs=(vmem,) * 7,
+        compiler_params=pltpu.CompilerParams(vmem_limit_bytes=32 * 1024 * 1024),
+        name="widen",
+    )(*narrow)
+    return layer.T, conv, bias.reshape(SHARE), gq, gk, gv, go
 
 
 def solution(mesh):

time: 140 us -> 135 us (0.964)
  local copies, waits for them, and re-layouts: 11.2 us -> 3.29 us
  Pallas kernels: 126 us -> 129 us
    unnamed x18 -> x6, local copies, waits for them, and re-layouts: 9.79 us -> 3.29 us
    pallas_call x1 -> x2, Pallas kernels: 126 us -> 129 us  [the longest x1 127 us: body(): pl.pallas_call(kernel, out_shape=(layer, jax.ShapeDtypeStruct((512, CIN),...]
where the time goes in v2:
time: 135 us; the launch traced here: 133 us
  Pallas kernels  129 us (96%)
  local copies, waits for them, and re-layouts  3.29 us (2%)
    pallas_call x1, Pallas kernels, body(): pl.pallas_call(kernel, out_shape=(layer, jax.ShapeDtypeStruct((512, CIN),...  127 us
    unnamed x6, local copies, waits for them, and re-layouts  3.29 us

profile of v2, /device:TPU:1, one launch (start us, length us, event | category | flops | bytes accessed | tf_op | source)
XLA Modules:
  0.0 132.8 jit_solution(10792267023949192750)
XLA Ops:
  0.6 126.8 %section.1 = (bf16[96,512]{1,0:T(8,128)(2,1)}, bf16[512,768]{1,0:T(8,128)(2,1)}, bf16[4,96,1536]{2,1,0:T(8,128)(2,1)}) custom-call(bf16[1024,768]{1,0:T(8,128)(2,1)} %feat_hbm.1, s32[512,128]{1,0:T(8,128)} %bitcast.5, f32[4,768]{1,0:T(4,128)} %bproj.1, bf16[5,96,768]{2,1,0:T(8,128)(2,1)} %cw_hbm.1, f32[1,96]{1,0:T(1,128)} %bitcast.8, bf16[96,1536]{1,0:T(8,128)(2,1)} %wq.1, ...), custom_call_target="tpu_custom_call" | custom-call | flops 8000000000 | bytes 8000000 | tf_op jit(solution)/shard_map/section/pallas_call | solution.py:490
  127.4 0.0 copy-start
  127.4 1.3 copy-done
  128.7 0.0 copy-start.1
  128.7 1.1 copy-done.1
  129.8 0.0 copy-start.2
  129.8 0.9 copy-done.2
  130.7 2.1 %widen.1 = (bf16[96,512]{1,0:T(8,128)(2,1)}, f32[5,96,768]{2,1,0:T(8,128)}, f32[1,96]{1,0:T(1,128)}, f32[96,1536]{1,0:T(8,128)}, f32[96,1536]{1,0:T(8,128)}, /*index=5*/f32[96,1536]{1,0:T(8,128)}, f32[96,1536]{1,0:T(8,128)}) custom-call(bf16[96,512]{1,0:T(8,128)(2,1)S(1)} %copy-done.2, bf16[512,768]{1,0:T(8,128)(2,1)S(1)} %copy-done.1, ...), custom_call_target="tpu_custom_call" | custom-call | tf_op jit(solution)/shard_map/widen/pallas_call | solution.py:506
Async XLA Ops:
  127.4 1.3 copy-start
  128.7 1.1 copy-start.1
  129.8 0.9 copy-start.2

commit v3 on v2

--- a/solution.py
+++ b/solution.py
@@ -23,11 +23,14 @@
 SCALE = HEAD ** (-0.5)
 ROOT2PI = 0.7978845608028654
 
-TOK_AG, COT_AG, OUT_RS, NORM_RS = 0, 16, 32, 48
-C_RS, C_AG = 80, 88
-W_SIB, HALO, Q_X, DO_X, ST_X, O_X, DQ_X = 96, 100, 104, 108, 112, 116, 120
-KV_Z, KV_SIB, DKV_SIB, DKV_Z, G_SIB, G_RS, G_AG = 124, 125, 127, 129, 130, 136, 168
-SEMS = 200
+(
+    COT_AG, TOK_AG, W_SIB, HALO, Q_X, DO_X, ST_X, O_X, DQ_X, KV_Z, KV_SIB, KV_FWD, DKV_FAR, DKV_SIB, DKV_Z,
+    OUT_Y, OUT_Z, OUT_SIB, NORM_RS,
+) = range(19)
+G_SIB = 19
+G_STEP = G_SIB + 4
+C_STEP = G_STEP + 16
+SEMS = C_STEP + 8
 
 
 def mm(a, b):
@@ -45,11 +48,12 @@
 def kernel(
     feat_hbm, toks_hbm, bproj, cw_hbm, cbias, wq, wk, wv, wo, cot_hbm,
     o_layer, c_all, g_all,
-    feat, toks, cw, xf, r3, xe, halo, wt, w4, z, slope, tok_own, cot_own, tok_t, cot_t, norm_t,
+    feat, toks, cw, w_t, wo_t, xf, r3, xe, halo, wt, w4, z, slope, tok_own, cot_own, tok_t, cot_t, norm_t,
     q, kv, kn, vn, do, et, dp, st, st_in, o_f, o_send, o_in, ot, fac,
     dq_f, dq_send, dq_in, dkv, dkv_send, dkv_in, z_send, z_in, dqkv, ng,
-    n_send, n_in, a_send, a_in, g_part, g_send, g_sib, g_acc, g_in, g_red,
-    pgs, c_send, c_in, c_red, ssem, rsem, lsem,
+    n_send, n_in, a_send, ay_in, az_send, az_in, az_own, as_send, as_in,
+    g_part, g_send, g_sib, g_acc, gx_in, gz_send, gz_in, gbz_in, gb_held, gx_b, g_red,
+    pgs, c_send, cx_in, cz_send, cz_in, cbz_in, cb_held, cx_b, c_red, ssem, rsem, lsem,
 ):
     s = lax.axis_index("seq")
     m = lax.axis_index("mp")
@@ -58,7 +62,7 @@
     c = m % 2
     sib = (s, m + 1 - 2 * c)
     zpart = ((1 - zl) * 4 + x, m)
-    sent = []
+    sent = {}
 
     def xpeer(r):
         return (zl * 4 + (x + r) % 4, m)
@@ -70,18 +74,18 @@
         return (s, (m + r) % 16)
 
     def push(src, dst, sem, dev):
-        copy = pltpu.make_async_remote_copy(
+        pltpu.make_async_remote_copy(
             src_ref=src, dst_ref=dst, send_sem=ssem.at[sem], recv_sem=rsem.at[sem],
             device_id=dev, device_id_type=MESH,
+        ).start()
+
+    def land(whole, sem):
+        copy = pltpu.make_async_remote_copy(
+            src_ref=whole, dst_ref=whole, send_sem=ssem.at[sem], recv_sem=rsem.at[sem],
+            device_id=sib, device_id_type=MESH,
         )
-        copy.start()
-        sent.append(copy)
-
-    def land(dst, sem):
-        pltpu.make_async_remote_copy(
-            src_ref=dst, dst_ref=dst, send_sem=ssem.at[sem], recv_sem=rsem.at[sem],
-            device_id=sib, device_id_type=MESH,
-        ).wait_recv()
+        copy.wait_recv()
+        sent[sem] = copy
 
     def al(v, n):
         return pl.multiple_of(v, n)
@@ -108,21 +112,19 @@
     def spread(own, full, base):
         for r in range(1, 16):
             cols = pl.ds(al(TOK * ((m + r) % 2), TOK), TOK)
-            push(own.at[:, cols], full.at[mine], base + r, mppeer(r))
+            push(own.at[:, cols], full.at[mine], base, mppeer(r))
 
     def keep(own, full):
         full[mine, :] = own[:, pl.ds(al(TOK * c, TOK), TOK)]
 
     def gathered(full, base):
-        for r in range(1, 16):
-            rows = pl.ds(al(SHARE * ((m - r + 16) % 16), 32), SHARE)
-            land(full.at[rows], base + r)
+        land(full.at[0 : 15 * SHARE], base)
 
     pl.semaphore_wait(barrier, 22)
     spread(cot_hbm, cot_t, COT_AG)
     for k, w in enumerate((wo, wq, wk, wv)):
         rows = pl.ds(al(HEAD * ((k + 3) % 4) + SHARE * c, 32), SHARE)
-        push(w, w4.at[rows], W_SIB + (k + 3) % 4, sib)
+        push(w, w4.at[rows], W_SIB, sib)
 
     bp = bproj[...]
     hi = bp.astype(BF).astype(F32)
@@ -154,7 +156,7 @@
                 xe[0:PAIRS, lo + 128 * i : lo + 128 * i + 128] = (own + extra[:, 128 * i : 128 * i + 128]).astype(BF)
 
     push(xe.at[pl.ds(PAIRS - 16, 16)], halo.at[0], HALO, seqpeer(1))
-    push(xe.at[pl.ds(0, 16)], halo.at[1], HALO + 1, seqpeer(7))
+    push(xe.at[pl.ds(0, 16)], halo.at[1], HALO, seqpeer(7))
     loads[2].wait()
     zero = jnp.zeros((SHARE, CIN), BF)
     left = (cw[0], zero, cw[2], cw[1], cw[4], cw[3])
@@ -168,8 +170,7 @@
         rows = pl.ds(al(i * 256, 256), 256)
         z[:, rows] = nt(wt[...], xe[rows, :])
 
-    land(halo.at[0], HALO)
-    land(halo.at[1], HALO + 1)
+    land(halo, HALO)
     at = lax.broadcasted_iota(jnp.int32, (16, D), 0)
     after = halo[1].astype(F32)
     before = halo[0].astype(F32)
@@ -199,13 +200,19 @@
     keep(tok_own, tok_t)
     for load in loads[3:]:
         load.wait()
-    for k in range(4):
-        land(w4.at[pl.ds(al(HEAD * k + SHARE * (1 - c), 32), SHARE)], W_SIB + k)
+    land(w4.at[0 : 4 * SHARE], W_SIB)
     keep(cot_own, cot_t)
     gathered(cot_t, COT_AG)
     do[0] = mm(w4[3 * HEAD : 4 * HEAD, :], cot_t[...]).astype(BF)
     for r in range(1, 4):
-        push(do.at[0], do.at[r], DO_X + r, xpeer(r))
+        push(do.at[0], do.at[r], DO_X, xpeer(r))
+
+    @pl.loop(0, 4)
+    def _(k):
+        cols = pl.ds(al(384 * k, 128), 384)
+        w_t[cols, :] = jnp.transpose(w4[0 : 3 * HEAD, cols].astype(F32)).astype(BF)
+        wo_t[cols, :] = jnp.transpose(w4[3 * HEAD : 4 * HEAD, cols].astype(F32)).astype(BF)
+
     gathered(tok_t, TOK_AG)
     wide = tok_t[...].astype(F32)
     inverse = lax.rsqrt(jnp.sum(wide * wide, axis=0, keepdims=True) * (1.0 / D) + EPS)
@@ -216,19 +223,23 @@
     push(kv.at[0], kv.at[2], KV_Z, zpart)
     push(kv.at[0], kv.at[1], KV_SIB, sib)
     for r in range(1, 4):
-        push(q.at[0], q.at[r], Q_X + r, xpeer(r))
+        push(q.at[0], q.at[r], Q_X, xpeer(r))
 
     land(kv.at[2], KV_Z)
-    push(kv.at[2], kv.at[3], KV_SIB + 1, sib)
-    land(kv.at[1], KV_SIB)
-    land(kv.at[3], KV_SIB + 1)
-    for i in range(4):
+    push(kv.at[2], kv.at[3], KV_FWD, sib)
+
+    def turn(i):
         kn[i] = jnp.transpose(kv[i, 0:HEAD].astype(F32)).astype(BF)
         vn[i] = jnp.transpose(kv[i, HEAD : 2 * HEAD].astype(F32)).astype(BF)
-    for r in range(1, 4):
-        land(q.at[r], Q_X + r)
-        land(do.at[r], DO_X + r)
-
+
+    turn(0)
+    land(kv.at[1], KV_SIB)
+    turn(1)
+    turn(2)
+    land(q.at[1:4], Q_X)
+    land(do.at[1:4], DO_X)
+    land(kv.at[3], KV_FWD)
+    turn(3)
     @pl.loop(0, 4)
     def _(j):
         top = jnp.full((1, TOK), -jnp.inf, F32)
@@ -253,55 +264,54 @@
         st[j, 1:2, :] = norm
         st[j, 2:3, :] = delta
         st[j, 3:8, :] = jnp.zeros((5, TOK), F32)
-
-    for r in range(1, 4):
-        push(st, st_in.at[r], ST_X + r, xpeer(r))
-    for r in range(1, 4):
-        land(st_in.at[r], ST_X + r)
+        for r in range(1, 4):
+            push(st.at[j], st_in.at[r, (j + r) % 4], ST_X, xpeer(r))
+
+    land(st_in.at[1:4], ST_X)
 
     factors = []
     deltas = []
     for j in range(4):
-        every = [st[j]] + [st_in[r, (j - r) % 4] for r in range(1, 4)]
+        every = [st[j]] + [st_in[r, j] for r in range(1, 4)]
         top = functools.reduce(jnp.maximum, [e[0:1] for e in every])
         norm = sum(e[1:2] * jnp.exp(e[0:1] - top) for e in every)
         log_total = jnp.log(norm) + top
         factors.append(jnp.exp(every[0][0:1] - log_total))
         deltas.append(sum(e[2:3] * jnp.exp(e[0:1] - log_total) for e in every))
-        o_f[j] = o_f[j] * factors[j]
     for j in range(4):
         fac[j, 0:1, :] = factors[j]
         fac[j, 1:2, :] = deltas[j]
     for r in range(1, 4):
-        o_send[r] = o_f[r].astype(BF)
-        push(o_send.at[r], o_in.at[4 - r], O_X + 4 - r, xpeer(4 - r))
-
-    dkv[...] = jnp.zeros_like(dkv)
-
-    @pl.loop(0, 4)
-    def _(j):
-        factor = fac[j, 0:1, :]
-        delta = fac[j, 1:2, :]
-        grad_q = jnp.zeros((HEAD, TOK), F32)
-        for i in range(4):
-            rows = slice(TOK * i, TOK * i + TOK)
-            p = et[j, rows, :] * factor
-            ds = (p * (dp[j, rows, :] - delta) * SCALE).astype(BF)
-            grad_q = grad_q + mm(kv[i, 0:HEAD, :], ds)
+        o_send[r] = (o_f[r] * factors[r]).astype(BF)
+        push(o_send.at[r], o_in.at[4 - r], O_X, xpeer(4 - r))
+
+    def backward(i):
+        rows = slice(TOK * i, TOK * i + TOK)
+        dkv[i] = jnp.zeros((2 * HEAD, TOK), F32)
+
+        @pl.loop(0, 4)
+        def _(j):
+            p = et[j, rows, :] * fac[j, 0:1, :]
+            ds = (p * (dp[j, rows, :] - fac[j, 1:2, :]) * SCALE).astype(BF)
+            part = mm(kv[i, 0:HEAD, :], ds)
+            dq_f[j] = part if i == 3 else dq_f[j] + part
             dkv[i, 0:HEAD, :] += nt(q[j], ds)
             dkv[i, HEAD : 2 * HEAD, :] += nt(do[j], p.astype(BF))
-        dq_f[j] = grad_q
-
+
+    backward(3)
     dkv_send[0] = dkv[3].astype(BF)
-    push(dkv_send.at[0], dkv_in.at[0], DKV_SIB, sib)
+    push(dkv_send.at[0], dkv_in.at[0], DKV_FAR, sib)
+    backward(2)
+    land(dkv_in.at[0], DKV_FAR)
+    z_send[...] = (dkv[2] + dkv_in[0].astype(F32)).astype(BF)
+    push(z_send, z_in, DKV_Z, zpart)
+    backward(1)
     dkv_send[1] = dkv[1].astype(BF)
-    push(dkv_send.at[1], dkv_in.at[1], DKV_SIB + 1, sib)
+    push(dkv_send.at[1], dkv_in.at[1], DKV_SIB, sib)
+    backward(0)
     for r in range(1, 4):
         dq_send[r] = dq_f[r].astype(BF)
-        push(dq_send.at[r], dq_in.at[4 - r], DQ_X + 4 - r, xpeer(4 - r))
-    land(dkv_in.at[0], DKV_SIB)
-    z_send[...] = (dkv[2] + dkv_in[0].astype(F32)).astype(BF)
-    push(z_send, z_in, DKV_Z, zpart)
+        push(dq_send.at[r], dq_in.at[4 - r], DQ_X, xpeer(4 - r))
 
     def grad_w(k, grads, inputs):
         g_part[HEAD * k : HEAD * k + HEAD, :] = nt(grads[...], inputs[...])
@@ -312,51 +322,125 @@
         land(g_sib.at[k], G_SIB + k)
         own = g_part[pl.ds(al(HEAD * k + SHARE * c, 32), SHARE), :]
         g_acc[k] = (own + g_sib[k].astype(F32)).astype(BF)
-        for r in range(1, 8):
-            push(g_piece(g_acc, k, (s + r) % 8), g_in.at[r, k], G_RS + 8 * k + r, seqpeer(r))
-
-    def g_piece(buf, k, seq):
-        return buf.at[k, pl.ds(al(48 * (seq // 4), 16), 48), pl.ds(al(384 * (seq % 4), 128), 384)]
-
-    for r in range(1, 4):
-        land(o_in.at[r], O_X + r)
-    ot[...] = (o_f[0] + sum(o_in[r].astype(F32) for r in range(1, 4))).astype(BF)
+
+    def g_col(k):
+        return lambda buf, at: buf.at[k, :, pl.ds(al(384 * at, 128), 384)]
+
+    def g_row(k):
+        return lambda buf, at: buf.at[k, pl.ds(al(48 * at, 16), 48), :]
+
+    def g_piece(k):
+        return lambda buf, z, at: buf.at[k, pl.ds(al(48 * z, 16), 48), pl.ds(al(384 * at, 128), 384)]
+
+    def c_col(buf, at):
+        return buf.at[:, pl.ds(al(64 * at, 64), 64), 0:384]
+
+    def c_row(buf, at):
+        return buf.at[at, :, 384:CIN]
+
+    def c_piece(lanes):
+        return lambda buf, z, at: buf.at[z, pl.ds(al(64 * at, 64), 64), lanes]
+
+    def a_first(src, col, into, sem):
+        for r in range(1, 4):
+            push(col(src, (x + r) % 4), into.at[r], sem, xpeer(r))
+
+    def a_second(src, piece, into, part, send, into_z, sem):
+        land(into.at[1:4], sem)
+
+        def total(z):
+            own = piece(src, z, x)[...].astype(F32)
+            return own + sum(part(into, r, z)[...].astype(F32) for r in range(1, 4))
+
+        send[...] = total(1 - zl).astype(BF)
+        push(send, into_z, sem + 1, zpart)
+        return total(zl)
+
+    def a_third(held, piece, full, red, into_z, sem):
+        land(into_z, sem + 1)
+        red[...] = (held + into_z[...].astype(F32)).astype(BF)
+        push(red, piece(full, zl, x), sem + 2, zpart)
+        piece(full, zl, x)[...] = red[...]
+
+    def a_fourth(col, full, red, sem):
+        land(red, sem + 2)
+        for r in range(1, 4):
+            push(col(full, x), col(full, x), sem + 3, xpeer(r))
+
+    def b_first(src, row, into_z, sem):
+        push(row(src, 1 - zl), into_z, sem, zpart)
+
+    def b_second(src, row, part, held, into_z, into, sem):
+        land(into_z, sem)
+        held[...] = (row(src, zl)[...].astype(F32) + into_z[...].astype(F32)).astype(BF)
+        for r in range(1, 4):
+            push(part(held, (x + r) % 4), into.at[r], sem + 1, xpeer(r))
+
+    def b_third(part, piece, full, held, into, red, sem):
+        land(into.at[1:4], sem + 1)
+        red[...] = (part(held, x)[...].astype(F32) + sum(into[r].astype(F32) for r in range(1, 4))).astype(BF)
+        for r in range(1, 4):
+            push(red, piece(full, zl, x), sem + 2, xpeer(r))
+        piece(full, zl, x)[...] = red[...]
+
+    def b_fourth(row, full, into, sem):
+        land(into.at[1:4], sem + 2)
+        push(row(full, zl), row(full, zl), sem + 3, zpart)
+
+    def ga_part(buf, r, z):
+        return buf.at[r, pl.ds(al(48 * z, 16), 48), :]
+
+    def ca_part(buf, r, z):
+        return buf.at[r, z]
+
+    def gb_part(buf, at):
+        return buf.at[:, pl.ds(al(384 * at, 128), 384)]
+
+    def cb_part(buf, at):
+        return buf.at[pl.ds(al(64 * at, 64), 64)]
 
     def scatter(send, into, base):
         for r in range(1, 16):
             rows = pl.ds(al(SHARE * ((m + r) % 16), 32), SHARE)
-            push(send.at[rows], into.at[r], base + r, mppeer(r))
+            push(send.at[rows], into.at[r], base, mppeer(r))
         into[0] = send[mine, :]
 
     def reduced(into, base):
-        for r in range(1, 16):
-            land(into.at[r], base + r)
+        land(into.at[1:16], base)
         same = sum(into[r].astype(F32) for r in range(0, 16, 2))
         other = sum(into[r].astype(F32) for r in range(1, 16, 2))
         first = jnp.where(c == 0, same, other)
         second = jnp.where(c == 0, other, same)
         return first, second
 
+    land(o_in.at[1:4], O_X)
+    ot[...] = (o_f[0] * factors[0] + sum(o_in[r].astype(F32) for r in range(1, 4))).astype(BF)
+    grad_w(3, ot, cot_t)
+
     @pl.loop(0, 4)
     def _(k):
         cols = pl.ds(al(384 * k, 128), 384)
-        a_send[cols, :] = tn(w4[3 * HEAD : 4 * HEAD, cols], ot[...]).astype(BF)
-
-    scatter(a_send, a_in, OUT_RS)
-    grad_w(3, ot, cot_t)
-
-    land(dkv_in.at[1], DKV_SIB + 1)
+        a_send[k // 2, pl.ds(al(384 * (k % 2), 128), 384), :] = mm(wo_t[cols, :], ot[...]).astype(BF)
+
+    y = (m // 2) % 4
+    zh = m // 8
     for r in range(1, 4):
-        land(dq_in.at[r], DQ_X + r)
+        rows = pl.ds(al(HEAD * ((y + r) % 4), 64), HEAD)
+        push(a_send.at[:, rows], ay_in.at[r], OUT_Y, (s, zh * 8 + ((y + r) % 4) * 2 + c))
+    grad_sum(3)
+    a_first(g_acc, g_col(3), gx_in.at[3], G_STEP + 12)
+
+    land(dkv_in.at[1], DKV_SIB)
+    land(z_in, DKV_Z)
+    dqkv[HEAD : 3 * HEAD, :] = (dkv[0] + dkv_in[1].astype(F32) + z_in[...].astype(F32)).astype(BF)
+    land(dq_in.at[1:4], DQ_X)
     grad_q = dq_f[0] + sum(dq_in[r].astype(F32) for r in range(1, 4))
     dqkv[0:HEAD, :] = grad_q.astype(BF)
-    land(z_in, DKV_Z)
-    dqkv[HEAD : 3 * HEAD, :] = (dkv[0] + dkv_in[1].astype(F32) + z_in[...].astype(F32)).astype(BF)
 
     @pl.loop(0, 4)
     def _(k):
         cols = pl.ds(al(384 * k, 128), 384)
-        ng[cols, :] = tn(w4[0 : 3 * HEAD, cols], dqkv[...])
+        ng[cols, :] = mm(w_t[cols, :], dqkv[...])
 
     wide = tok_t[...].astype(F32)
     inverse = lax.rsqrt(jnp.sum(wide * wide, axis=0, keepdims=True) * (1.0 / D) + EPS)
@@ -367,14 +451,23 @@
 
     for k in range(3):
         grad_w(k, dqkv.at[HEAD * k : HEAD * k + HEAD], norm_t)
-    for k in (3, 0, 1, 2):
+    for k in range(3):
         grad_sum(k)
-
-    tok_wide = tok_own[...].astype(F32)
-    first, second = reduced(a_in, OUT_RS)
-    out = jnp.concatenate([first, second], axis=1) + tok_wide
-    o_layer[...] = out.astype(BF)
-
+        if k == 1:
+            b_first(g_acc, g_row(1), gbz_in, G_STEP + 4)
+        else:
+            a_first(g_acc, g_col(k), gx_in.at[k], G_STEP + 4 * k)
+    held = {}
+    held[3] = a_second(g_acc, g_piece(3), gx_in.at[3], ga_part, gz_send.at[3], gz_in.at[3], G_STEP + 12)
+    land(ay_in.at[1:4], OUT_Y)
+    rows = pl.ds(al(HEAD * y, 64), HEAD)
+
+    def over_y(z):
+        return a_send[z, rows, :].astype(F32) + sum(ay_in[r, z].astype(F32) for r in range(1, 4))
+
+    az_send[...] = over_y(1 - zh).astype(BF)
+    push(az_send, az_in, OUT_Z, (s, (m + 8) % 16))
+    az_own[...] = over_y(zh)
     first, second = reduced(n_in, NORM_RS)
     tok_grad = cot_own[...].astype(F32) + jnp.concatenate([first, second], axis=1)
     pad = jnp.zeros((SHARE, WIDE - PAIRS), F32)
@@ -388,8 +481,8 @@
     both = pgs[2 * SHARE : 3 * SHARE, 0:PAIRS], pgs[3 * SHARE : 4 * SHARE, 0:PAIRS]
     ones = jnp.ones((16, PAIRS), BF)
     bias = nt(ones, both[0]) + nt(ones, both[1])
-    c_send[TAPS * SHARE :, :] = jnp.zeros((32, CIN), BF)
-    c_send[TAPS * SHARE : TAPS * SHARE + 16, 0:SHARE] = bias.astype(BF)
+    c_send[1, 224:256, :] = jnp.zeros((32, CIN), BF)
+    c_send[1, 224:240, 0:SHARE] = bias.astype(BF)
 
     @pl.loop(0, 3)
     def _(k):
@@ -410,42 +503,53 @@
             part(me, 1, 0) + part(mo, 1, 1),
         )
         for t in range(TAPS):
-            c_send[SHARE * t : SHARE * t + SHARE, cols] = taps[t].astype(BF)
-
-    def c_piece(buf, seq):
-        return buf.at[pl.ds(al(64 * seq, 64), 64)]
-
-    for r in range(1, 8):
-        push(c_piece(c_send, (s + r) % 8), c_in.at[r], C_RS + r, seqpeer(r))
-
-    own_rows = pl.ds(al(48 * zl, 16), 48)
-    own_cols = pl.ds(al(384 * x, 128), 384)
-    for k in (3, 0, 1, 2):
-        acc = g_acc[k, own_rows, own_cols].astype(F32)
-        for r in range(1, 8):
-            land(g_in.at[r, k], G_RS + 8 * k + r)
-            acc = acc + g_in[r, k].astype(F32)
-        g_red[k] = acc.astype(BF)
-        for r in range(1, 8):
-            push(g_red.at[k], g_piece(g_all, k, s), G_AG + 8 * k + r, seqpeer(r))
-        g_all[k, own_rows, own_cols] = g_red[k]
-
-    for r in range(1, 8):
-        land(c_in.at[r], C_RS + r)
-    acc = c_send[pl.ds(al(64 * s, 64), 64), :].astype(F32)
-    for r in range(1, 8):
-        acc = acc + c_in[r].astype(F32)
-    c_red[...] = acc.astype(BF)
-    for r in range(1, 8):
-        push(c_red, c_piece(c_all, s), C_AG + r, seqpeer(r))
-    c_all[pl.ds(al(64 * s, 64), 64), :] = c_red[...]
-
-    for r in range(1, 8):
-        for k in range(4):
-            land(g_piece(g_all, k, (s - r + 8) % 8), G_AG + 8 * k + r)
-    for r in range(1, 8):
-        land(c_piece(c_all, (s - r + 8) % 8), C_AG + r)
-    for copy in sent:
+            tap = taps[t].astype(BF)
+            if t < 2:
+                c_send[0, SHARE * t : SHARE * t + SHARE, cols] = tap
+            elif t == 2:
+                c_send[0, 192:256, cols] = tap[0:64]
+                c_send[1, 0:32, cols] = tap[64:96]
+            else:
+                c_send[1, SHARE * t - 256 : SHARE * t - 160, cols] = tap
+
+    low, high = slice(0, 384), slice(384, CIN)
+    a_first(c_send, c_col, cx_in, C_STEP)
+    b_first(c_send, c_row, cbz_in, C_STEP + 4)
+
+    a_third(held[3], g_piece(3), g_all, g_red.at[3], gz_in.at[3], G_STEP + 12)
+    for k in (0, 2):
+        held[k] = a_second(g_acc, g_piece(k), gx_in.at[k], ga_part, gz_send.at[k], gz_in.at[k], G_STEP + 4 * k)
+    b_second(g_acc, g_row(1), gb_part, gb_held, gbz_in, gx_b, G_STEP + 4)
+    a_fourth(g_col(3), g_all, g_red.at[3], G_STEP + 12)
+    held_c = a_second(c_send, c_piece(low), cx_in, ca_part, cz_send, cz_in, C_STEP)
+    b_second(c_send, c_row, cb_part, cb_held, cbz_in, cx_b, C_STEP + 4)
+    for k in (0, 2):
+        a_third(held[k], g_piece(k), g_all, g_red.at[k], gz_in.at[k], G_STEP + 4 * k)
+    b_third(gb_part, g_piece(1), g_all, gb_held, gx_b, g_red.at[1], G_STEP + 4)
+    a_third(held_c, c_piece(low), c_all, c_red.at[0], cz_in, C_STEP)
+    b_third(cb_part, c_piece(high), c_all, cb_held, cx_b, c_red.at[1], C_STEP + 4)
+    for k in (0, 2):
+        a_fourth(g_col(k), g_all, g_red.at[k], G_STEP + 4 * k)
+    a_fourth(c_col, c_all, c_red.at[0], C_STEP)
+    b_fourth(g_row(1), g_all, gx_b, G_STEP + 4)
+    b_fourth(c_row, c_all, cx_b, C_STEP + 4)
+
+    land(az_in, OUT_Z)
+    az_own[...] = az_own[...] + az_in[...].astype(F32)
+    as_send[...] = az_own[pl.ds(al(SHARE * (1 - c), 32), SHARE), :].astype(BF)
+    push(as_send, as_in, OUT_SIB, sib)
+    own = az_own[pl.ds(al(SHARE * c, 32), SHARE), :]
+    land(as_in, OUT_SIB)
+    other = as_in[...].astype(F32)
+    out = jnp.concatenate([jnp.where(c == 0, own, other), jnp.where(c == 0, other, own)], axis=1)
+    o_layer[...] = (out + tok_own[...].astype(F32)).astype(BF)
+
+    for k in (3, 0, 2):
+        land(gx_in.at[k, 1:4], G_STEP + 4 * k + 3)
+    land(gbz_in, G_STEP + 7)
+    land(cx_in.at[1:4], C_STEP + 3)
+    land(cbz_in, C_STEP + 7)
+    for copy in sent.values():
         copy.wait_send()
 
 
@@ -454,7 +558,7 @@
         return pltpu.VMEM(shape, dtype)
 
     return [
-        v(1024, CIN), v(PAIRS, 128, dtype=jnp.int32), v(TAPS, SHARE, CIN),
+        v(1024, CIN), v(PAIRS, 128, dtype=jnp.int32), v(TAPS, SHARE, CIN), v(D, 3 * HEAD), v(D, HEAD),
         v(6, 1024, 128, dtype=F32), v(32, D, dtype=F32), v(WIDE, D), v(2, 16, D), v(576, D), v(768, D),
         v(576, WIDE, dtype=F32), v(2, SHARE, PAIRS, dtype=F32), v(SHARE, PAIRS), v(SHARE, PAIRS),
         v(D, TOK), v(D, TOK), v(D, TOK),
@@ -466,21 +570,37 @@
         v(4, HEAD, TOK, dtype=F32), v(4, HEAD, TOK), v(4, HEAD, TOK),
         v(4, 384, TOK, dtype=F32), v(2, 384, TOK), v(2, 384, TOK), v(384, TOK), v(384, TOK),
         v(576, TOK), v(D, TOK, dtype=F32),
-        v(D, TOK), v(16, SHARE, TOK), v(D, TOK), v(16, SHARE, TOK),
+        v(D, TOK), v(16, SHARE, TOK),
+        v(2, 768, TOK), v(4, 2, HEAD, TOK), v(HEAD, TOK), v(HEAD, TOK), v(HEAD, TOK, dtype=F32), v(SHARE, TOK), v(SHARE, TOK),
         v(768, D, dtype=F32), v(4, SHARE, D), v(4, SHARE, D), v(4, SHARE, D),
-        v(8, 4, 48, 384), v(4, 48, 384),
-        v(576, WIDE), v(512, CIN), v(8, 64, CIN), v(64, CIN),
+        v(4, 4, SHARE, 384), v(4, 48, 384), v(4, 48, 384), v(48, D), v(48, D), v(4, 48, 384), v(4, 48, 384),
+        v(576, WIDE), v(2, 256, CIN),
+        v(4, 2, 64, 384), v(64, 384), v(64, 384), v(256, 384), v(256, 384), v(4, 64, 384), v(2, 64, 384),
         pltpu.SemaphoreType.DMA((SEMS,)), pltpu.SemaphoreType.DMA((SEMS,)), pltpu.SemaphoreType.DMA((8,)),
     ]
 
 
-def widen(layer, conv, grads, o_layer, o_conv, o_bias, o_q, o_k, o_v, o_o):
+def widen(layer, conv, grads, o_layer, o_conv, o_bias, o_q, o_k, o_v, o_o, cin, gin, cout, gout, lsem, osem):
+    loads = [pltpu.make_async_copy(grads.at[k], gin.at[k], lsem.at[k]) for k in range(4)]
+    loads.append(pltpu.make_async_copy(conv, cin, lsem.at[4]))
+    for load in loads:
+        load.start()
+    through = pltpu.make_async_copy(layer, o_layer, lsem.at[5])
+    through.start()
+    stores = [through]
+    for k, o in enumerate((o_q, o_k, o_v, o_o)):
+        loads[k].wait()
+        gout[k] = gin[k].astype(F32)
+        stores.append(pltpu.make_async_copy(gout.at[k], o, osem.at[k]))
+        stores[-1].start()
+    loads[4].wait()
     for t in range(TAPS):
-        o_conv[t] = conv[SHARE * t : SHARE * t + SHARE, :].astype(F32)
-    o_bias[...] = conv[TAPS * SHARE : TAPS * SHARE + 16, 0:SHARE].astype(F32)[0:1]
-    for k, o in enumerate((o_q, o_k, o_v, o_o)):
-        o[...] = grads[k].astype(F32)
-    o_layer[...] = layer[...]
+        cout[t] = cin[SHARE * t : SHARE * t + SHARE, :].astype(F32)
+        stores.append(pltpu.make_async_copy(cout.at[t], o_conv.at[t], osem.at[4 + t]))
+        stores[-1].start()
+    o_bias[...] = cin[TAPS * SHARE : TAPS * SHARE + 16, 0:SHARE].astype(F32)[0:1]
+    for store in stores:
+        store.wait()
 
 
 def body(features, base_tokens, base_proj, conv_weight, conv_bias, w_query, w_key, w_value, w_out, cotangent):
@@ -489,7 +609,7 @@
     layer = jax.ShapeDtypeStruct((SHARE, PAIRS), BF)
     narrow = pl.pallas_call(
         kernel,
-        out_shape=(layer, jax.ShapeDtypeStruct((512, CIN), BF), jax.ShapeDtypeStruct((4, SHARE, D), BF)),
+        out_shape=(layer, jax.ShapeDtypeStruct((2, 256, CIN), BF), jax.ShapeDtypeStruct((4, SHARE, D), BF)),
         in_specs=[hbm, hbm, vmem, hbm, vmem, hbm, hbm, hbm, hbm, hbm],
         out_specs=(vmem,) * 3,
         scratch_shapes=scratch(),
@@ -509,11 +629,16 @@
             layer, jax.ShapeDtypeStruct((TAPS, SHARE, CIN), F32), jax.ShapeDtypeStruct((1, SHARE), F32),
             square, square, square, square,
         ),
-        in_specs=[vmem] * 3,
-        out_specs=(vmem,) * 7,
+        in_specs=[hbm] * 3,
+        out_specs=(hbm, hbm, vmem, hbm, hbm, hbm, hbm),
+        scratch_shapes=[
+            pltpu.VMEM((512, CIN), BF), pltpu.VMEM((4, SHARE, D), BF),
+            pltpu.VMEM((TAPS, SHARE, CIN), F32), pltpu.VMEM((4, SHARE, D), F32),
+            pltpu.SemaphoreType.DMA((6,)), pltpu.SemaphoreType.DMA((9,)),
+        ],
         compiler_params=pltpu.CompilerParams(vmem_limit_bytes=32 * 1024 * 1024),
         name="widen",
-    )(*narrow)
+    )(narrow[0], narrow[1].reshape(512, CIN), narrow[2])
     return layer.T, conv, bias.reshape(SHARE), gq, gk, gv, go
 
 

time: 135 us -> 114 us (0.84); the launches traced: 133 us -> 113 us
  Pallas kernels: 129 us -> 109 us
    pallas_call x1, Pallas kernels: 127 us -> 107 us  [body(): pl.pallas_call(kernel, out_shape=(layer, jax.ShapeDtypeStruct((2, 256, CI...]
where the time goes in v3:
time: 114 us; the launch traced here: 113 us
  Pallas kernels  109 us (96%)
  local copies, waits for them, and re-layouts  3.29 us (3%)
    pallas_call x1, Pallas kernels, body(): pl.pallas_call(kernel, out_shape=(layer, jax.ShapeDtypeStruct((2, 256, CI...  107 us
    unnamed x6, local copies, waits for them, and re-layouts  3.29 us
    pallas_call x1, Pallas kernels, body(): pl.pallas_call(widen, out_shape=(layer, jax.ShapeDtypeStruct((TAPS, SHARE...  2.85 us

profile of v3, /device:TPU:1, one launch (start us, length us, event | category | flops | bytes accessed | tf_op | source)
XLA Modules:
  0.0 113.4 jit_solution(2559851201473840390)
XLA Ops:
  0.6 106.6 %section.1 = (bf16[96,512]{1,0:T(8,128)(2,1)}, bf16[2,256,768]{2,1,0:T(8,128)(2,1)}, bf16[4,96,1536]{2,1,0:T(8,128)(2,1)}) custom-call(bf16[1024,768]{1,0:T(8,128)(2,1)} %feat_hbm.1, s32[512,128]{1,0:T(8,128)} %bitcast.7, f32[4,768]{1,0:T(4,128)} %bproj.1, bf16[5,96,768]{2,1,0:T(8,128)(2,1)} %cw_hbm.1, f32[1,96]{1,0:T(1,128)} %bitcast.10, ...), custom_call_target="tpu_custom_call" | custom-call | flops 8000000000 | bytes 8000000 | tf_op jit(solution)/shard_map/section/pallas_call | solution.py:610
  107.3 0.0 copy-start
  107.3 1.3 %copy-done = bf16[4,96,1536]{2,1,0:T(8,128)(2,1)S(1)} copy-done((bf16[4,96,1536]{2,1,0:T(8,128)(2,1)S(1)}, bf16[4,96,1536]{2,1,0:T(8,128)(2,1)}, u32[]{:S(2)}) %copy-start) | copy-done | bytes 1179672
  108.5 0.0 copy-start.1
  108.5 1.1 copy-done.1
  109.7 0.0 copy-start.2
  109.7 0.9 copy-done.2
  110.6 2.8 %widen.1 = (bf16[96,512]{1,0:T(8,128)(2,1)}, f32[5,96,768]{2,1,0:T(8,128)}, f32[1,96]{1,0:T(1,128)}, f32[96,1536]{1,0:T(8,128)}, f32[96,1536]{1,0:T(8,128)}, /*index=5*/f32[96,1536]{1,0:T(8,128)}, f32[96,1536]{1,0:T(8,128)}) custom-call(bf16[96,512]{1,0:T(8,128)(2,1)S(1)} %copy-done.2, bf16[512,768]{1,0:T(8,128)(2,1)S(1)} %bitcast.6, ...), custom_call_target="tpu_custom_call" | custom-call | tf_op jit(solution)/shard_map/widen/pallas_call | solution.py:626
Async XLA Ops:
  107.3 1.3 %copy-start = (bf16[4,96,1536]{2,1,0:T(8,128)(2,1)S(1)}, bf16[4,96,1536]{2,1,0:T(8,128)(2,1)}, u32[]{:S(2)}) copy-start(bf16[4,96,1536]{2,1,0:T(8,128)(2,1)} %get-tuple-element.19.grads) | copy-start | bytes 3538948
  108.5 1.1 copy-start.1
  109.7 0.9 copy-start.2

commit v4 on v3

--- a/solution.py
+++ b/solution.py
@@ -50,7 +50,7 @@
     o_layer, c_all, g_all,
     feat, toks, cw, w_t, wo_t, xf, r3, xe, halo, wt, w4, z, slope, tok_own, cot_own, tok_t, cot_t, norm_t,
     q, kv, kn, vn, do, et, dp, st, st_in, o_f, o_send, o_in, ot, fac,
-    dq_f, dq_send, dq_in, dkv, dkv_send, dkv_in, z_send, z_in, dqkv, ng,
+    dq_f, dq_send, dq_in, dk, dv, qn, don, norm_n, cot_n, dkv_send, dkv_in, z_send, z_in, dqkv, ng,
     n_send, n_in, a_send, ay_in, az_send, az_in, az_own, as_send, as_in,
     g_part, g_send, g_sib, g_acc, gx_in, gz_send, gz_in, gbz_in, gb_held, gx_b, g_red,
     pgs, c_send, cx_in, cz_send, cz_in, cbz_in, cb_held, cx_b, c_red, ssem, rsem, lsem,
@@ -145,14 +145,14 @@
         counts = counts + mm(match, pick)
     comp = (counts * (1.0 / BIN_WIDTH)).astype(BF)
     loads[1].wait()
-    for k in range(6):
-        xf[k] = feat[:, 128 * k : 128 * k + 128].astype(F32)
     for k in range(0, 6, 2):
+        for i in range(2):
+            xf[i] = feat[:, 128 * (k + i) : 128 * (k + i) + 128].astype(F32)
         for half in range(2):
             lo = CIN * half + 128 * k
             extra = mm(comp, r3[:, lo : lo + 256].astype(BF))
             for i in range(2):
-                own = xf[k + i, pl.ds(half, PAIRS, stride=2), :]
+                own = xf[i, pl.ds(half, PAIRS, stride=2), :]
                 xe[0:PAIRS, lo + 128 * i : lo + 128 * i + 128] = (own + extra[:, 128 * i : 128 * i + 128]).astype(BF)
 
     push(xe.at[pl.ds(PAIRS - 16, 16)], halo.at[0], HALO, seqpeer(1))
@@ -212,6 +212,7 @@
         cols = pl.ds(al(384 * k, 128), 384)
         w_t[cols, :] = jnp.transpose(w4[0 : 3 * HEAD, cols].astype(F32)).astype(BF)
         wo_t[cols, :] = jnp.transpose(w4[3 * HEAD : 4 * HEAD, cols].astype(F32)).astype(BF)
+        cot_n[:, cols] = jnp.transpose(cot_t[cols, :].astype(F32)).astype(BF)
 
     gathered(tok_t, TOK_AG)
     wide = tok_t[...].astype(F32)
@@ -225,12 +226,20 @@
     for r in range(1, 4):
         push(q.at[0], q.at[r], Q_X, xpeer(r))
 
+    don[0] = jnp.transpose(do[0].astype(F32)).astype(BF)
+    qn[0] = jnp.transpose(q[0].astype(F32)).astype(BF)
+
+    @pl.loop(0, 4)
+    def _(k):
+        cols = pl.ds(al(384 * k, 128), 384)
+        norm_n[:, cols] = jnp.transpose(norm_t[cols, :].astype(F32)).astype(BF)
+
     land(kv.at[2], KV_Z)
     push(kv.at[2], kv.at[3], KV_FWD, sib)
 
     def turn(i):
-        kn[i] = jnp.transpose(kv[i, 0:HEAD].astype(F32)).astype(BF)
-        vn[i] = jnp.transpose(kv[i, HEAD : 2 * HEAD].astype(F32)).astype(BF)
+        kn[TOK * i : TOK * i + TOK, :] = jnp.transpose(kv[i, 0:HEAD].astype(F32)).astype(BF)
+        vn[TOK * i : TOK * i + TOK, :] = jnp.transpose(kv[i, HEAD : 2 * HEAD].astype(F32)).astype(BF)
 
     turn(0)
     land(kv.at[1], KV_SIB)
@@ -238,27 +247,25 @@
     turn(2)
     land(q.at[1:4], Q_X)
     land(do.at[1:4], DO_X)
+    for j in range(1, 4):
+        qn[j] = jnp.transpose(q[j].astype(F32)).astype(BF)
+        don[j] = jnp.transpose(do[j].astype(F32)).astype(BF)
     land(kv.at[3], KV_FWD)
     turn(3)
     @pl.loop(0, 4)
     def _(j):
-        top = jnp.full((1, TOK), -jnp.inf, F32)
-        for i in range(4):
-            scores = mm(kn[i], q[j]) * SCALE
-            et[j, TOK * i : TOK * i + TOK, :] = scores
-            top = jnp.maximum(top, jnp.max(scores, axis=0, keepdims=True))
-        norm = jnp.zeros((1, TOK), F32)
-        delta = jnp.zeros((1, TOK), F32)
-        out = jnp.zeros((HEAD, TOK), F32)
-        for i in range(4):
-            rows = slice(TOK * i, TOK * i + TOK)
-            e = jnp.exp(et[j, rows, :] - top)
-            et[j, rows, :] = e
-            norm = norm + jnp.sum(e, axis=0, keepdims=True)
-            out = out + mm(kv[i, HEAD : 2 * HEAD, :], e.astype(BF))
-            grad = mm(vn[i], do[j])
-            dp[j, rows, :] = grad
-            delta = delta + jnp.sum(e * grad, axis=0, keepdims=True)
+        scores = mm(kn[...], q[j]) * SCALE
+        top = jnp.max(scores, axis=0, keepdims=True)
+        e = jnp.exp(scores - top)
+        et[j] = e
+        norm = jnp.sum(e, axis=0, keepdims=True)
+        grad = mm(vn[...], do[j])
+        dp[j] = grad
+        delta = jnp.sum(e * grad, axis=0, keepdims=True)
+        short = e.astype(BF)
+        out = mm(kv[0, HEAD : 2 * HEAD, :], short[0:TOK])
+        for i in range(1, 4):
+            out = out + mm(kv[i, HEAD : 2 * HEAD, :], short[TOK * i : TOK * i + TOK])
         o_f[j] = out
         st[j, 0:1, :] = top
         st[j, 1:2, :] = norm
@@ -285,43 +292,54 @@
         o_send[r] = (o_f[r] * factors[r]).astype(BF)
         push(o_send.at[r], o_in.at[4 - r], O_X, xpeer(4 - r))
 
-    def backward(i):
-        rows = slice(TOK * i, TOK * i + TOK)
-        dkv[i] = jnp.zeros((2 * HEAD, TOK), F32)
-
-        @pl.loop(0, 4)
-        def _(j):
-            p = et[j, rows, :] * fac[j, 0:1, :]
-            ds = (p * (dp[j, rows, :] - fac[j, 1:2, :]) * SCALE).astype(BF)
-            part = mm(kv[i, 0:HEAD, :], ds)
-            dq_f[j] = part if i == 3 else dq_f[j] + part
-            dkv[i, 0:HEAD, :] += nt(q[j], ds)
-            dkv[i, HEAD : 2 * HEAD, :] += nt(do[j], p.astype(BF))
-
-    backward(3)
-    dkv_send[0] = dkv[3].astype(BF)
+    def backward(first, j):
+        rows = slice(TOK * first, TOK * first + 2 * TOK)
+        p = et[j, rows, :] * fac[j, 0:1, :]
+        ds = (p * (dp[j, rows, :] - fac[j, 1:2, :]) * SCALE).astype(BF)
+        part = mm(kv[first, 0:HEAD, :], ds[0:TOK]) + mm(kv[first + 1, 0:HEAD, :], ds[TOK : 2 * TOK])
+        dk[rows, :] += mm(ds, qn[j])
+        dv[rows, :] += mm(p.astype(BF), don[j])
+        return part
+
+    dk[...] = jnp.zeros_like(dk)
+    dv[...] = jnp.zeros_like(dv)
+
+    @pl.loop(0, 4)
+    def _(j):
+        dq_f[j] = backward(2, j)
+
+    def key_rows(i):
+        return slice(TOK * i, TOK * i + TOK)
+
+    def pack(buf, i):
+        buf[:, 0:HEAD] = dk[key_rows(i), :].astype(BF)
+        buf[:, HEAD : 2 * HEAD] = dv[key_rows(i), :].astype(BF)
+
+    pack(dkv_send.at[0], 3)
     push(dkv_send.at[0], dkv_in.at[0], DKV_FAR, sib)
-    backward(2)
+
+    @pl.loop(1, 4)
+    def _(j):
+        dq_send[j] = (dq_f[j] + backward(0, j)).astype(BF)
+        push(dq_send.at[j], dq_in.at[4 - j], DQ_X, xpeer(4 - j))
+
     land(dkv_in.at[0], DKV_FAR)
-    z_send[...] = (dkv[2] + dkv_in[0].astype(F32)).astype(BF)
+    z_send[:, 0:HEAD] = (dk[key_rows(2), :] + dkv_in[0, :, 0:HEAD].astype(F32)).astype(BF)
+    z_send[:, HEAD : 2 * HEAD] = (dv[key_rows(2), :] + dkv_in[0, :, HEAD : 2 * HEAD].astype(F32)).astype(BF)
     push(z_send, z_in, DKV_Z, zpart)
-    backward(1)
-    dkv_send[1] = dkv[1].astype(BF)
+    dq_f[0] = dq_f[0] + backward(0, 0)
+    pack(dkv_send.at[1], 1)
     push(dkv_send.at[1], dkv_in.at[1], DKV_SIB, sib)
-    backward(0)
-    for r in range(1, 4):
-        dq_send[r] = dq_f[r].astype(BF)
-        push(dq_send.at[r], dq_in.at[4 - r], DQ_X, xpeer(4 - r))
 
     def grad_w(k, grads, inputs):
-        g_part[HEAD * k : HEAD * k + HEAD, :] = nt(grads[...], inputs[...])
-        g_send[k] = g_part[pl.ds(al(HEAD * k + SHARE * (1 - c), 32), SHARE), :].astype(BF)
+        g_part[...] = mm(grads[...], inputs[...])
+        g_send[k] = g_part[pl.ds(al(SHARE * (1 - c), 32), SHARE), :].astype(BF)
+        g_acc[k] = g_part[pl.ds(al(SHARE * c, 32), SHARE), :].astype(BF)
         push(g_send.at[k], g_sib.at[k], G_SIB + k, sib)
 
     def grad_sum(k):
         land(g_sib.at[k], G_SIB + k)
-        own = g_part[pl.ds(al(HEAD * k + SHARE * c, 32), SHARE), :]
-        g_acc[k] = (own + g_sib[k].astype(F32)).astype(BF)
+        g_acc[k] = (g_acc[k].astype(F32) + g_sib[k].astype(F32)).astype(BF)
 
     def g_col(k):
         return lambda buf, at: buf.at[k, :, pl.ds(al(384 * at, 128), 384)]
@@ -415,7 +433,7 @@
 
     land(o_in.at[1:4], O_X)
     ot[...] = (o_f[0] * factors[0] + sum(o_in[r].astype(F32) for r in range(1, 4))).astype(BF)
-    grad_w(3, ot, cot_t)
+    grad_w(3, ot, cot_n)
 
     @pl.loop(0, 4)
     def _(k):
@@ -432,7 +450,10 @@
 
     land(dkv_in.at[1], DKV_SIB)
     land(z_in, DKV_Z)
-    dqkv[HEAD : 3 * HEAD, :] = (dkv[0] + dkv_in[1].astype(F32) + z_in[...].astype(F32)).astype(BF)
+    grad_k = dk[key_rows(0), :] + (dkv_in[1, :, 0:HEAD].astype(F32) + z_in[:, 0:HEAD].astype(F32))
+    grad_v = dv[key_rows(0), :] + (dkv_in[1, :, HEAD : 2 * HEAD].astype(F32) + z_in[:, HEAD : 2 * HEAD].astype(F32))
+    dqkv[HEAD : 2 * HEAD, :] = jnp.transpose(grad_k).astype(BF)
+    dqkv[2 * HEAD : 3 * HEAD, :] = jnp.transpose(grad_v).astype(BF)
     land(dq_in.at[1:4], DQ_X)
     grad_q = dq_f[0] + sum(dq_in[r].astype(F32) for r in range(1, 4))
     dqkv[0:HEAD, :] = grad_q.astype(BF)
@@ -450,7 +471,7 @@
     scatter(n_send, n_in, NORM_RS)
 
     for k in range(3):
-        grad_w(k, dqkv.at[HEAD * k : HEAD * k + HEAD], norm_t)
+        grad_w(k, dqkv.at[HEAD * k : HEAD * k + HEAD], norm_n)
     for k in range(3):
         grad_sum(k)
         if k == 1:
@@ -459,15 +480,6 @@
             a_first(g_acc, g_col(k), gx_in.at[k], G_STEP + 4 * k)
     held = {}
     held[3] = a_second(g_acc, g_piece(3), gx_in.at[3], ga_part, gz_send.at[3], gz_in.at[3], G_STEP + 12)
-    land(ay_in.at[1:4], OUT_Y)
-    rows = pl.ds(al(HEAD * y, 64), HEAD)
-
-    def over_y(z):
-        return a_send[z, rows, :].astype(F32) + sum(ay_in[r, z].astype(F32) for r in range(1, 4))
-
-    az_send[...] = over_y(1 - zh).astype(BF)
-    push(az_send, az_in, OUT_Z, (s, (m + 8) % 16))
-    az_own[...] = over_y(zh)
     first, second = reduced(n_in, NORM_RS)
     tok_grad = cot_own[...].astype(F32) + jnp.concatenate([first, second], axis=1)
     pad = jnp.zeros((SHARE, WIDE - PAIRS), F32)
@@ -516,6 +528,15 @@
     a_first(c_send, c_col, cx_in, C_STEP)
     b_first(c_send, c_row, cbz_in, C_STEP + 4)
 
+    land(ay_in.at[1:4], OUT_Y)
+    rows = pl.ds(al(HEAD * y, 64), HEAD)
+
+    def over_y(z):
+        return a_send[z, rows, :].astype(F32) + sum(ay_in[r, z].astype(F32) for r in range(1, 4))
+
+    az_send[...] = over_y(1 - zh).astype(BF)
+    push(az_send, az_in, OUT_Z, (s, (m + 8) % 16))
+    az_own[...] = over_y(zh)
     a_third(held[3], g_piece(3), g_all, g_red.at[3], gz_in.at[3], G_STEP + 12)
     for k in (0, 2):
         held[k] = a_second(g_acc, g_piece(k), gx_in.at[k], ga_part, gz_send.at[k], gz_in.at[k], G_STEP + 4 * k)
@@ -559,20 +580,21 @@
 
     return [
         v(1024, CIN), v(PAIRS, 128, dtype=jnp.int32), v(TAPS, SHARE, CIN), v(D, 3 * HEAD), v(D, HEAD),
-        v(6, 1024, 128, dtype=F32), v(32, D, dtype=F32), v(WIDE, D), v(2, 16, D), v(576, D), v(768, D),
+        v(2, 1024, 128, dtype=F32), v(32, D, dtype=F32), v(WIDE, D), v(2, 16, D), v(576, D), v(768, D),
         v(576, WIDE, dtype=F32), v(2, SHARE, PAIRS, dtype=F32), v(SHARE, PAIRS), v(SHARE, PAIRS),
         v(D, TOK), v(D, TOK), v(D, TOK),
-        v(4, HEAD, TOK), v(4, 384, TOK), v(4, TOK, HEAD), v(4, TOK, HEAD), v(4, HEAD, TOK),
+        v(4, HEAD, TOK), v(4, 384, TOK), v(1024, HEAD), v(1024, HEAD), v(4, HEAD, TOK),
         v(4, 1024, TOK, dtype=F32), v(4, 1024, TOK, dtype=F32),
         v(4, 8, TOK, dtype=F32), v(4, 4, 8, TOK, dtype=F32),
         v(4, HEAD, TOK, dtype=F32), v(4, HEAD, TOK), v(4, HEAD, TOK), v(HEAD, TOK),
         v(4, 8, TOK, dtype=F32),
         v(4, HEAD, TOK, dtype=F32), v(4, HEAD, TOK), v(4, HEAD, TOK),
-        v(4, 384, TOK, dtype=F32), v(2, 384, TOK), v(2, 384, TOK), v(384, TOK), v(384, TOK),
+        v(1024, HEAD, dtype=F32), v(1024, HEAD, dtype=F32), v(4, TOK, HEAD), v(4, TOK, HEAD), v(TOK, D), v(TOK, D),
+        v(2, TOK, 384), v(2, TOK, 384), v(TOK, 384), v(TOK, 384),
         v(576, TOK), v(D, TOK, dtype=F32),
         v(D, TOK), v(16, SHARE, TOK),
         v(2, 768, TOK), v(4, 2, HEAD, TOK), v(HEAD, TOK), v(HEAD, TOK), v(HEAD, TOK, dtype=F32), v(SHARE, TOK), v(SHARE, TOK),
-        v(768, D, dtype=F32), v(4, SHARE, D), v(4, SHARE, D), v(4, SHARE, D),
+        v(HEAD, D, dtype=F32), v(4, SHARE, D), v(4, SHARE, D), v(4, SHARE, D),
         v(4, 4, SHARE, 384), v(4, 48, 384), v(4, 48, 384), v(48, D), v(48, D), v(4, 48, 384), v(4, 48, 384),
         v(576, WIDE), v(2, 256, CIN),
         v(4, 2, 64, 384), v(64, 384), v(64, 384), v(256, 384), v(256, 384), v(4, 64, 384), v(2, 64, 384),
@@ -636,7 +658,7 @@
             pltpu.VMEM((TAPS, SHARE, CIN), F32), pltpu.VMEM((4, SHARE, D), F32),
             pltpu.SemaphoreType.DMA((6,)), pltpu.SemaphoreType.DMA((9,)),
         ],
-        compiler_params=pltpu.CompilerParams(vmem_limit_bytes=32 * 1024 * 1024),
+        compiler_params=pltpu.CompilerParams(vmem_limit_bytes=60 * 1024 * 1024),
         name="widen",
     )(narrow[0], narrow[1].reshape(512, CIN), narrow[2])
     return layer.T, conv, bias.reshape(SHARE), gq, gk, gv, go

time: 114 us -> 114 us (level)
  local copies, waits for them, and re-layouts: 3.29 us -> 0 us
  Pallas kernels: 109 us -> 112 us
    unnamed x6 -> x0, local copies, waits for them, and re-layouts: 3.29 us -> none
    pallas_call x1, Pallas kernels: 2.85 us -> 4.74 us  [body(): pl.pallas_call(widen, out_shape=(layer, jax.ShapeDtypeStruct((TAPS, SHARE...]
where the time goes in v4:
time: 114 us; the launch traced here: 112 us
  Pallas kernels  112 us (98%)
    pallas_call x1, Pallas kernels, body(): pl.pallas_call(kernel, out_shape=(layer, jax.ShapeDtypeStruct((2, 256, CI...  107 us
    pallas_call x1, Pallas kernels, body(): pl.pallas_call(widen, out_shape=(layer, jax.ShapeDtypeStruct((TAPS, SHARE...  4.74 us

profile of v4, /device:TPU:1, one launch (start us, length us, event | category | flops | bytes accessed | tf_op | source)
XLA Modules:
  0.0 112.3 jit_solution(15122569937972799038)
XLA Ops:
  0.6 106.9 %section.1 = (bf16[96,512]{1,0:T(8,128)(2,1)}, bf16[2,256,768]{2,1,0:T(8,128)(2,1)}, bf16[4,96,1536]{2,1,0:T(8,128)(2,1)}) custom-call(bf16[1024,768]{1,0:T(8,128)(2,1)} %feat_hbm.1, s32[512,128]{1,0:T(8,128)} %bitcast.7, f32[4,768]{1,0:T(4,128)} %bproj.1, bf16[5,96,768]{2,1,0:T(8,128)(2,1)} %cw_hbm.1, f32[1,96]{1,0:T(1,128)} %bitcast.10, ...), custom_call_target="tpu_custom_call" | custom-call | flops 8000000000 | bytes 8000000 | tf_op jit(solution)/shard_map/section/pallas_call | solution.py:632
  107.6 4.7 %widen.1 = (bf16[96,512]{1,0:T(8,128)(2,1)}, f32[5,96,768]{2,1,0:T(8,128)}, f32[1,96]{1,0:T(1,128)}, f32[96,1536]{1,0:T(8,128)}, f32[96,1536]{1,0:T(8,128)}, /*index=5*/f32[96,1536]{1,0:T(8,128)}, f32[96,1536]{1,0:T(8,128)}) custom-call(bf16[96,512]{1,0:T(8,128)(2,1)} %get-tuple-element.17.layer, bf16[512,768]{1,0:T(8,128)(2,1)} %bitcast.6, ...), custom_call_target="tpu_custom_call" | custom-call | tf_op jit(solution)/shard_map/widen/pallas_call | solution.py:648

commit v5 on v4

--- a/solution.py
+++ b/solution.py
@@ -29,7 +29,7 @@
 ) = range(19)
 G_SIB = 19
 G_STEP = G_SIB + 4
-C_STEP = G_STEP + 16
+C_STEP = G_STEP + 24
 SEMS = C_STEP + 8
 
 
@@ -52,7 +52,7 @@
     q, kv, kn, vn, do, et, dp, st, st_in, o_f, o_send, o_in, ot, fac,
     dq_f, dq_send, dq_in, dk, dv, qn, don, norm_n, cot_n, dkv_send, dkv_in, z_send, z_in, dqkv, ng,
     n_send, n_in, a_send, ay_in, az_send, az_in, az_own, as_send, as_in,
-    g_part, g_send, g_sib, g_acc, gx_in, gz_send, gz_in, gbz_in, gb_held, gx_b, g_red,
+    g_part, g_send, g_sib, g_acc, gr_in, gr_send, gz_send, gz_in, g_red,
     pgs, c_send, cx_in, cz_send, cz_in, cbz_in, cb_held, cx_b, c_red, ssem, rsem, lsem,
 ):
     s = lax.axis_index("seq")
@@ -318,15 +318,20 @@
     pack(dkv_send.at[0], 3)
     push(dkv_send.at[0], dkv_in.at[0], DKV_FAR, sib)
 
-    @pl.loop(1, 4)
-    def _(j):
+    def query_block(j):
         dq_send[j] = (dq_f[j] + backward(0, j)).astype(BF)
         push(dq_send.at[j], dq_in.at[4 - j], DQ_X, xpeer(4 - j))
 
+    query_block(2)
     land(dkv_in.at[0], DKV_FAR)
     z_send[:, 0:HEAD] = (dk[key_rows(2), :] + dkv_in[0, :, 0:HEAD].astype(F32)).astype(BF)
     z_send[:, HEAD : 2 * HEAD] = (dv[key_rows(2), :] + dkv_in[0, :, HEAD : 2 * HEAD].astype(F32)).astype(BF)
     push(z_send, z_in, DKV_Z, zpart)
+
+    @pl.loop(0, 2)
+    def _(i):
+        query_block(1 + 2 * i)
+
     dq_f[0] = dq_f[0] + backward(0, 0)
     pack(dkv_send.at[1], 1)
     push(dkv_send.at[1], dkv_in.at[1], DKV_SIB, sib)
@@ -341,12 +346,6 @@
         land(g_sib.at[k], G_SIB + k)
         g_acc[k] = (g_acc[k].astype(F32) + g_sib[k].astype(F32)).astype(BF)
 
-    def g_col(k):
-        return lambda buf, at: buf.at[k, :, pl.ds(al(384 * at, 128), 384)]
-
-    def g_row(k):
-        return lambda buf, at: buf.at[k, pl.ds(al(48 * at, 16), 48), :]
-
     def g_piece(k):
         return lambda buf, z, at: buf.at[k, pl.ds(al(48 * z, 16), 48), pl.ds(al(384 * at, 128), 384)]
 
@@ -379,6 +378,50 @@
         red[...] = (held + into_z[...].astype(F32)).astype(BF)
         push(red, piece(full, zl, x), sem + 2, zpart)
         piece(full, zl, x)[...] = red[...]
+
+    right, left = xpeer(1), xpeer(3)
+
+    def r_first(src, piece, into, sem):
+        push(piece(src, 0, (x + 2) % 4), into.at[0], sem, right)
+        push(piece(src, 1, (x + 2) % 4), into.at[1], sem, left)
+        push(piece(src, 1, (x + 1) % 4), into.at[3], sem + 1, right)
+        push(piece(src, 0, (x + 3) % 4), into.at[4], sem + 1, left)
+
+    def r_second(src, piece, into, send, sem):
+        land(into.at[0:2], sem)
+        send[0] = (piece(src, 0, (x + 1) % 4)[...].astype(F32) + into[0].astype(F32)).astype(BF)
+        send[1] = (piece(src, 1, (x + 3) % 4)[...].astype(F32) + into[1].astype(F32)).astype(BF)
+        push(send.at[0], into.at[2], sem + 1, right)
+        push(send.at[1], into.at[5], sem + 1, left)
+
+    def r_third(src, piece, into, send, into_z, sem):
+        land(into.at[2:6], sem + 1)
+
+        def total(z):
+            own = piece(src, z, x)[...].astype(F32)
+            return own + into[2 + z].astype(F32) + into[4 + z].astype(F32)
+
+        send[...] = total(1 - zl).astype(BF)
+        push(send, into_z, sem + 2, zpart)
+        return total(zl)
+
+    def r_fourth(held, piece, full, red, into_z, sem):
+        land(into_z, sem + 2)
+        red[...] = (held + into_z[...].astype(F32)).astype(BF)
+        push(red, piece(full, zl, x), sem + 3, zpart)
+        for dev in (right, left):
+            push(red, piece(full, zl, x), sem + 4, dev)
+        piece(full, zl, x)[...] = red[...]
+
+    def r_fifth(piece, full, red, sem):
+        land(red, sem + 3)
+        for dev in (right, left):
+            push(piece(full, 1 - zl, x), piece(full, 1 - zl, x), sem + 4, dev)
+
+    def r_sixth(piece, full, into, sem):
+        land(into.at[0:4], sem + 4)
+        push(piece(full, 0, (x + 3) % 4), piece(full, 0, (x + 3) % 4), sem + 5, right)
+        push(piece(full, 1, (x + 1) % 4), piece(full, 1, (x + 1) % 4), sem + 5, left)
 
     def a_fourth(col, full, red, sem):
         land(red, sem + 2)
@@ -405,14 +448,8 @@
         land(into.at[1:4], sem + 2)
         push(row(full, zl), row(full, zl), sem + 3, zpart)
 
-    def ga_part(buf, r, z):
-        return buf.at[r, pl.ds(al(48 * z, 16), 48), :]
-
     def ca_part(buf, r, z):
         return buf.at[r, z]
-
-    def gb_part(buf, at):
-        return buf.at[:, pl.ds(al(384 * at, 128), 384)]
 
     def cb_part(buf, at):
         return buf.at[pl.ds(al(64 * at, 64), 64)]
@@ -442,11 +479,8 @@
 
     y = (m // 2) % 4
     zh = m // 8
-    for r in range(1, 4):
-        rows = pl.ds(al(HEAD * ((y + r) % 4), 64), HEAD)
-        push(a_send.at[:, rows], ay_in.at[r], OUT_Y, (s, zh * 8 + ((y + r) % 4) * 2 + c))
     grad_sum(3)
-    a_first(g_acc, g_col(3), gx_in.at[3], G_STEP + 12)
+    r_first(g_acc, g_piece(3), gr_in.at[3], G_STEP + 18)
 
     land(dkv_in.at[1], DKV_SIB)
     land(z_in, DKV_Z)
@@ -469,18 +503,19 @@
     row_stat = jnp.sum(ng[...] * unit, axis=0, keepdims=True) * (1.0 / D)
     n_send[...] = (inverse * (ng[...] - unit * row_stat)).astype(BF)
     scatter(n_send, n_in, NORM_RS)
+    for r in range(1, 4):
+        rows = pl.ds(al(HEAD * ((y + r) % 4), 64), HEAD)
+        push(a_send.at[:, rows], ay_in.at[r], OUT_Y, (s, zh * 8 + ((y + r) % 4) * 2 + c))
 
     for k in range(3):
         grad_w(k, dqkv.at[HEAD * k : HEAD * k + HEAD], norm_n)
     for k in range(3):
         grad_sum(k)
-        if k == 1:
-            b_first(g_acc, g_row(1), gbz_in, G_STEP + 4)
-        else:
-            a_first(g_acc, g_col(k), gx_in.at[k], G_STEP + 4 * k)
-    held = {}
-    held[3] = a_second(g_acc, g_piece(3), gx_in.at[3], ga_part, gz_send.at[3], gz_in.at[3], G_STEP + 12)
+        r_first(g_acc, g_piece(k), gr_in.at[k], G_STEP + 6 * k)
+    r_second(g_acc, g_piece(3), gr_in.at[3], gr_send.at[3], G_STEP + 18)
     first, second = reduced(n_in, NORM_RS)
+    for k in range(3):
+        r_second(g_acc, g_piece(k), gr_in.at[k], gr_send.at[k], G_STEP + 6 * k)
     tok_grad = cot_own[...].astype(F32) + jnp.concatenate([first, second], axis=1)
     pad = jnp.zeros((SHARE, WIDE - PAIRS), F32)
     for half in range(2):
@@ -537,23 +572,22 @@
     az_send[...] = over_y(1 - zh).astype(BF)
     push(az_send, az_in, OUT_Z, (s, (m + 8) % 16))
     az_own[...] = over_y(zh)
-    a_third(held[3], g_piece(3), g_all, g_red.at[3], gz_in.at[3], G_STEP + 12)
-    for k in (0, 2):
-        held[k] = a_second(g_acc, g_piece(k), gx_in.at[k], ga_part, gz_send.at[k], gz_in.at[k], G_STEP + 4 * k)
-    b_second(g_acc, g_row(1), gb_part, gb_held, gbz_in, gx_b, G_STEP + 4)
-    a_fourth(g_col(3), g_all, g_red.at[3], G_STEP + 12)
+    held = {}
+    order = (3, 0, 1, 2)
+    for k in order:
+        held[k] = r_third(g_acc, g_piece(k), gr_in.at[k], gz_send.at[k], gz_in.at[k], G_STEP + 6 * k)
     held_c = a_second(c_send, c_piece(low), cx_in, ca_part, cz_send, cz_in, C_STEP)
     b_second(c_send, c_row, cb_part, cb_held, cbz_in, cx_b, C_STEP + 4)
-    for k in (0, 2):
-        a_third(held[k], g_piece(k), g_all, g_red.at[k], gz_in.at[k], G_STEP + 4 * k)
-    b_third(gb_part, g_piece(1), g_all, gb_held, gx_b, g_red.at[1], G_STEP + 4)
+    for k in order:
+        r_fourth(held[k], g_piece(k), g_all, g_red.at[k], gz_in.at[k], G_STEP + 6 * k)
     a_third(held_c, c_piece(low), c_all, c_red.at[0], cz_in, C_STEP)
     b_third(cb_part, c_piece(high), c_all, cb_held, cx_b, c_red.at[1], C_STEP + 4)
-    for k in (0, 2):
-        a_fourth(g_col(k), g_all, g_red.at[k], G_STEP + 4 * k)
+    for k in order:
+        r_fifth(g_piece(k), g_all, g_red.at[k], G_STEP + 6 * k)
     a_fourth(c_col, c_all, c_red.at[0], C_STEP)
-    b_fourth(g_row(1), g_all, gx_b, G_STEP + 4)
     b_fourth(c_row, c_all, cx_b, C_STEP + 4)
+    for k in order:
+        r_sixth(g_piece(k), g_all, gr_in.at[k], G_STEP + 6 * k)
 
     land(az_in, OUT_Z)
     az_own[...] = az_own[...] + az_in[...].astype(F32)
@@ -565,9 +599,8 @@
     out = jnp.concatenate([jnp.where(c == 0, own, other), jnp.where(c == 0, other, own)], axis=1)
     o_layer[...] = (out + tok_own[...].astype(F32)).astype(BF)
 
-    for k in (3, 0, 2):
-        land(gx_in.at[k, 1:4], G_STEP + 4 * k + 3)
-    land(gbz_in, G_STEP + 7)
+    for k in order:
+        land(gr_in.at[k, 0:2], G_STEP + 6 * k + 5)
     land(cx_in.at[1:4], C_STEP + 3)
     land(cbz_in, C_STEP + 7)
     for copy in sent.values():
@@ -595,7 +628,7 @@
         v(D, TOK), v(16, SHARE, TOK),
         v(2, 768, TOK), v(4, 2, HEAD, TOK), v(HEAD, TOK), v(HEAD, TOK), v(HEAD, TOK, dtype=F32), v(SHARE, TOK), v(SHARE, TOK),
         v(HEAD, D, dtype=F32), v(4, SHARE, D), v(4, SHARE, D), v(4, SHARE, D),
-        v(4, 4, SHARE, 384), v(4, 48, 384), v(4, 48, 384), v(48, D), v(48, D), v(4, 48, 384), v(4, 48, 384),
+        v(4, 6, 48, 384), v(4, 2, 48, 384), v(4, 48, 384), v(4, 48, 384), v(4, 48, 384),
         v(576, WIDE), v(2, 256, CIN),
         v(4, 2, 64, 384), v(64, 384), v(64, 384), v(256, 384), v(256, 384), v(4, 64, 384), v(2, 64, 384),
         pltpu.SemaphoreType.DMA((SEMS,)), pltpu.SemaphoreType.DMA((SEMS,)), pltpu.SemaphoreType.DMA((8,)),

time: 114 us -> 110 us (0.965)
  Pallas kernels: 112 us -> 109 us
    pallas_call x1, Pallas kernels: 107 us -> 104 us  [body(): pl.pallas_call(kernel, out_shape=(layer, jax.ShapeDtypeStruct((2, 256, CI...]
where the time goes in v5:
time: 110 us; the launch traced here: 109 us
  Pallas kernels  109 us (99%)
    pallas_call x1, Pallas kernels, body(): pl.pallas_call(kernel, out_shape=(layer, jax.ShapeDtypeStruct((2, 256, CI...  104 us
    pallas_call x1, Pallas kernels, body(): pl.pallas_call(widen, out_shape=(layer, jax.ShapeDtypeStruct((TAPS, SHARE...  4.74 us

profile of v5, /device:TPU:1, one launch (start us, length us, event | category | flops | bytes accessed | tf_op | source)
XLA Modules:
  0.0 109.2 jit_solution(11413146434387129166)
XLA Ops:
  0.6 103.8 %section.1 = (bf16[96,512]{1,0:T(8,128)(2,1)}, bf16[2,256,768]{2,1,0:T(8,128)(2,1)}, bf16[4,96,1536]{2,1,0:T(8,128)(2,1)}) custom-call(bf16[1024,768]{1,0:T(8,128)(2,1)} %feat_hbm.1, s32[512,128]{1,0:T(8,128)} %bitcast.7, f32[4,768]{1,0:T(4,128)} %bproj.1, bf16[5,96,768]{2,1,0:T(8,128)(2,1)} %cw_hbm.1, f32[1,96]{1,0:T(1,128)} %bitcast.10, ...), custom_call_target="tpu_custom_call" | custom-call | flops 8000000000 | bytes 8000000 | tf_op jit(solution)/shard_map/section/pallas_call | solution.py:665
  104.4 4.7 %widen.1 = (bf16[96,512]{1,0:T(8,128)(2,1)}, f32[5,96,768]{2,1,0:T(8,128)}, f32[1,96]{1,0:T(1,128)}, f32[96,1536]{1,0:T(8,128)}, f32[96,1536]{1,0:T(8,128)}, /*index=5*/f32[96,1536]{1,0:T(8,128)}, f32[96,1536]{1,0:T(8,128)}) custom-call(bf16[96,512]{1,0:T(8,128)(2,1)} %get-tuple-element.17.layer, bf16[512,768]{1,0:T(8,128)(2,1)} %bitcast.6, ...), custom_call_target="tpu_custom_call" | custom-call | tf_op jit(solution)/shard_map/widen/pallas_call | solution.py:681

commit v6 on v5

--- a/solution.py
+++ b/solution.py
@@ -24,10 +24,10 @@
 ROOT2PI = 0.7978845608028654
 
 (
-    COT_AG, TOK_AG, W_SIB, HALO, Q_X, DO_X, ST_X, O_X, DQ_X, KV_Z, KV_SIB, KV_FWD, DKV_FAR, DKV_SIB, DKV_Z,
+    COT_AG, TOK_AG, W_SIB, HALO, Q_X, DO_X, ST_X, O_X, DQ_X, K_Z, V_Z, KV_SIB, K_FWD, V_FWD, DKV_FAR, DKV_SIB, DKV_Z,
     OUT_Y, OUT_Z, OUT_SIB, NORM_RS,
-) = range(19)
-G_SIB = 19
+) = range(21)
+G_SIB = 21
 G_STEP = G_SIB + 4
 C_STEP = G_STEP + 24
 SEMS = C_STEP + 8
@@ -50,7 +50,7 @@
     o_layer, c_all, g_all,
     feat, toks, cw, w_t, wo_t, xf, r3, xe, halo, wt, w4, z, slope, tok_own, cot_own, tok_t, cot_t, norm_t,
     q, kv, kn, vn, do, et, dp, st, st_in, o_f, o_send, o_in, ot, fac,
-    dq_f, dq_send, dq_in, dk, dv, qn, don, norm_n, cot_n, dkv_send, dkv_in, z_send, z_in, dqkv, ng,
+    dq_f, dq_send, dq_in, dk, dv, qn, don, norm_n, cot_n, wide_stat, dkv_send, dkv_in, z_send, z_in, dqkv,
     n_send, n_in, a_send, ay_in, az_send, az_in, az_own, as_send, as_in,
     g_part, g_send, g_sib, g_acc, gr_in, gr_send, gz_send, gz_in, g_red,
     pgs, c_send, cx_in, cz_send, cz_in, cbz_in, cb_held, cx_b, c_red, ssem, rsem, lsem,
@@ -109,8 +109,8 @@
         load.start()
     mine = pl.ds(al(SHARE * m, 32), SHARE)
 
-    def spread(own, full, base):
-        for r in range(1, 16):
+    def spread(own, full, base, steps=range(1, 16)):
+        for r in steps:
             cols = pl.ds(al(TOK * ((m + r) % 2), TOK), TOK)
             push(own.at[:, cols], full.at[mine], base, mppeer(r))
 
@@ -121,7 +121,7 @@
         land(full.at[0 : 15 * SHARE], base)
 
     pl.semaphore_wait(barrier, 22)
-    spread(cot_hbm, cot_t, COT_AG)
+    spread(cot_hbm, cot_t, COT_AG, range(1, 10))
     for k, w in enumerate((wo, wq, wk, wv)):
         rows = pl.ds(al(HEAD * ((k + 3) % 4) + SHARE * c, 32), SHARE)
         push(w, w4.at[rows], W_SIB, sib)
@@ -197,82 +197,96 @@
         )
     tok_own[...] = (0.5 * total).astype(BF)
     spread(tok_own, tok_t, TOK_AG)
+    spread(cot_hbm, cot_t, COT_AG, range(10, 16))
     keep(tok_own, tok_t)
     for load in loads[3:]:
         load.wait()
     land(w4.at[0 : 4 * SHARE], W_SIB)
+
+    @pl.loop(0, 4)
+    def _(k):
+        cols = pl.ds(al(384 * k, 128), 384)
+        w_t[cols, :] = jnp.transpose(w4[0 : 3 * HEAD, cols].astype(F32)).astype(BF)
+        wo_t[cols, :] = jnp.transpose(w4[3 * HEAD : 4 * HEAD, cols].astype(F32)).astype(BF)
+
+    gathered(tok_t, TOK_AG)
+    wide = tok_t[...].astype(F32)
+    inverse = lax.rsqrt(jnp.sum(wide * wide, axis=0, keepdims=True) * (1.0 / D) + EPS)
+    wide_stat[1:2, :] = inverse
+    norm_t[...] = (wide * inverse).astype(BF)
+    kv[0, 0:HEAD] = mm(w4[HEAD : 2 * HEAD, :], norm_t[...]).astype(BF)
+    keys, values = slice(0, HEAD), slice(HEAD, 2 * HEAD)
+    push(kv.at[0, keys], kv.at[2, keys], K_Z, zpart)
+    push(kv.at[0, keys], kv.at[1, keys], KV_SIB, sib)
+    q[0] = mm(w4[0:HEAD, :], norm_t[...]).astype(BF)
+    for r in range(1, 4):
+        push(q.at[0], q.at[r], Q_X, xpeer(r))
+    kv[0, HEAD : 2 * HEAD] = mm(w4[2 * HEAD : 3 * HEAD, :], norm_t[...]).astype(BF)
+    push(kv.at[0, values], kv.at[2, values], V_Z, zpart)
+    push(kv.at[0, values], kv.at[1, values], KV_SIB, sib)
     keep(cot_own, cot_t)
     gathered(cot_t, COT_AG)
     do[0] = mm(w4[3 * HEAD : 4 * HEAD, :], cot_t[...]).astype(BF)
     for r in range(1, 4):
         push(do.at[0], do.at[r], DO_X, xpeer(r))
 
-    @pl.loop(0, 4)
-    def _(k):
-        cols = pl.ds(al(384 * k, 128), 384)
-        w_t[cols, :] = jnp.transpose(w4[0 : 3 * HEAD, cols].astype(F32)).astype(BF)
-        wo_t[cols, :] = jnp.transpose(w4[3 * HEAD : 4 * HEAD, cols].astype(F32)).astype(BF)
-        cot_n[:, cols] = jnp.transpose(cot_t[cols, :].astype(F32)).astype(BF)
-
-    gathered(tok_t, TOK_AG)
-    wide = tok_t[...].astype(F32)
-    inverse = lax.rsqrt(jnp.sum(wide * wide, axis=0, keepdims=True) * (1.0 / D) + EPS)
-    norm_t[...] = (wide * inverse).astype(BF)
-    qkv = mm(w4[0 : 3 * HEAD, :], norm_t[...]).astype(BF)
-    q[0] = qkv[0:HEAD]
-    kv[0] = qkv[HEAD : 3 * HEAD]
-    push(kv.at[0], kv.at[2], KV_Z, zpart)
-    push(kv.at[0], kv.at[1], KV_SIB, sib)
-    for r in range(1, 4):
-        push(q.at[0], q.at[r], Q_X, xpeer(r))
-
+    def turn_k(i):
+        kn[TOK * i : TOK * i + TOK, :] = jnp.transpose(kv[i, 0:HEAD].astype(F32)).astype(BF)
+
+    def turn_v(i):
+        vn[TOK * i : TOK * i + TOK, :] = jnp.transpose(kv[i, HEAD : 2 * HEAD].astype(F32)).astype(BF)
+
+    land(kv.at[2, keys], K_Z)
+    push(kv.at[2, keys], kv.at[3, keys], K_FWD, sib)
+    turn_k(0)
+    turn_v(0)
     don[0] = jnp.transpose(do[0].astype(F32)).astype(BF)
     qn[0] = jnp.transpose(q[0].astype(F32)).astype(BF)
-
-    @pl.loop(0, 4)
-    def _(k):
-        cols = pl.ds(al(384 * k, 128), 384)
-        norm_n[:, cols] = jnp.transpose(norm_t[cols, :].astype(F32)).astype(BF)
-
-    land(kv.at[2], KV_Z)
-    push(kv.at[2], kv.at[3], KV_FWD, sib)
-
-    def turn(i):
-        kn[TOK * i : TOK * i + TOK, :] = jnp.transpose(kv[i, 0:HEAD].astype(F32)).astype(BF)
-        vn[TOK * i : TOK * i + TOK, :] = jnp.transpose(kv[i, HEAD : 2 * HEAD].astype(F32)).astype(BF)
-
-    turn(0)
     land(kv.at[1], KV_SIB)
-    turn(1)
-    turn(2)
+    turn_k(1)
+    turn_v(1)
+    turn_k(2)
+    land(kv.at[2, values], V_Z)
+    push(kv.at[2, values], kv.at[3, values], V_FWD, sib)
+    turn_v(2)
+    land(kv.at[3, keys], K_FWD)
+    turn_k(3)
     land(q.at[1:4], Q_X)
-    land(do.at[1:4], DO_X)
-    for j in range(1, 4):
-        qn[j] = jnp.transpose(q[j].astype(F32)).astype(BF)
-        don[j] = jnp.transpose(do[j].astype(F32)).astype(BF)
-    land(kv.at[3], KV_FWD)
-    turn(3)
+    land(kv.at[3, values], V_FWD)
+    turn_v(3)
     @pl.loop(0, 4)
     def _(j):
         scores = mm(kn[...], q[j]) * SCALE
         top = jnp.max(scores, axis=0, keepdims=True)
         e = jnp.exp(scores - top)
         et[j] = e
-        norm = jnp.sum(e, axis=0, keepdims=True)
-        grad = mm(vn[...], do[j])
-        dp[j] = grad
-        delta = jnp.sum(e * grad, axis=0, keepdims=True)
+        st[j, 0:1, :] = top
+        st[j, 1:2, :] = jnp.sum(e, axis=0, keepdims=True)
         short = e.astype(BF)
         out = mm(kv[0, HEAD : 2 * HEAD, :], short[0:TOK])
         for i in range(1, 4):
             out = out + mm(kv[i, HEAD : 2 * HEAD, :], short[TOK * i : TOK * i + TOK])
         o_f[j] = out
-        st[j, 0:1, :] = top
-        st[j, 1:2, :] = norm
-        st[j, 2:3, :] = delta
+
+    land(do.at[1:4], DO_X)
+
+    @pl.loop(0, 4)
+    def _(j):
+        grad = mm(vn[...], do[j])
+        dp[j] = grad
+        st[j, 2:3, :] = jnp.sum(et[j] * grad, axis=0, keepdims=True)
         st[j, 3:8, :] = jnp.zeros((5, TOK), F32)
         for r in range(1, 4):
             push(st.at[j], st_in.at[r, (j + r) % 4], ST_X, xpeer(r))
+
+    for j in range(1, 4):
+        qn[j] = jnp.transpose(q[j].astype(F32)).astype(BF)
+        don[j] = jnp.transpose(do[j].astype(F32)).astype(BF)
+
+    @pl.loop(0, 4)
+    def _(k):
+        cols = pl.ds(al(384 * k, 128), 384)
+        norm_n[:, cols] = jnp.transpose(norm_t[cols, :].astype(F32)).astype(BF)
 
     land(st_in.at[1:4], ST_X)
 
@@ -454,12 +468,6 @@
     def cb_part(buf, at):
         return buf.at[pl.ds(al(64 * at, 64), 64)]
 
-    def scatter(send, into, base):
-        for r in range(1, 16):
-            rows = pl.ds(al(SHARE * ((m + r) % 16), 32), SHARE)
-            push(send.at[rows], into.at[r], base, mppeer(r))
-        into[0] = send[mine, :]
-
     def reduced(into, base):
         land(into.at[1:16], base)
         same = sum(into[r].astype(F32) for r in range(0, 16, 2))
@@ -470,6 +478,12 @@
 
     land(o_in.at[1:4], O_X)
     ot[...] = (o_f[0] * factors[0] + sum(o_in[r].astype(F32) for r in range(1, 4))).astype(BF)
+
+    @pl.loop(0, 4)
+    def _(k):
+        cols = pl.ds(al(384 * k, 128), 384)
+        cot_n[:, cols] = jnp.transpose(cot_t[cols, :].astype(F32)).astype(BF)
+
     grad_w(3, ot, cot_n)
 
     @pl.loop(0, 4)
@@ -492,17 +506,29 @@
     grad_q = dq_f[0] + sum(dq_in[r].astype(F32) for r in range(1, 4))
     dqkv[0:HEAD, :] = grad_q.astype(BF)
 
+    row_stat = jnp.sum(dqkv[0:HEAD, :].astype(F32) * q[0].astype(F32), axis=0, keepdims=True)
+    row_stat = row_stat + jnp.sum(dqkv[HEAD:, :].astype(F32) * kv[0].astype(F32), axis=0, keepdims=True)
+    wide_stat[0:1, :] = row_stat * (1.0 / D)
+
+    def scatter_rows(k):
+        cols = pl.ds(al(384 * k, 128), 384)
+        inverse = wide_stat[1:2, :]
+        unit = tok_t[cols, :].astype(F32) * inverse
+        n_send[cols, :] = (inverse * (mm(w_t[cols, :], dqkv[...]) - unit * wide_stat[0:1, :])).astype(BF)
+        for i in range(4):
+            peer = 4 * k + i
+            slot = (peer + 16 - m) % 16
+            rows = pl.ds(al(SHARE * peer, 32), SHARE)
+
+            @pl.when(slot > 0)
+            def _():
+                push(n_send.at[rows], n_in.at[slot], NORM_RS, (s, peer))
+
     @pl.loop(0, 4)
     def _(k):
-        cols = pl.ds(al(384 * k, 128), 384)
-        ng[cols, :] = mm(w_t[cols, :], dqkv[...])
-
-    wide = tok_t[...].astype(F32)
-    inverse = lax.rsqrt(jnp.sum(wide * wide, axis=0, keepdims=True) * (1.0 / D) + EPS)
-    unit = wide * inverse
-    row_stat = jnp.sum(ng[...] * unit, axis=0, keepdims=True) * (1.0 / D)
-    n_send[...] = (inverse * (ng[...] - unit * row_stat)).astype(BF)
-    scatter(n_send, n_in, NORM_RS)
+        scatter_rows((k + m // 4) % 4)
+
+    n_in[0] = n_send[mine, :]
     for r in range(1, 4):
         rows = pl.ds(al(HEAD * ((y + r) % 4), 64), HEAD)
         push(a_send.at[:, rows], ay_in.at[r], OUT_Y, (s, zh * 8 + ((y + r) % 4) * 2 + c))
@@ -512,10 +538,13 @@
     for k in range(3):
         grad_sum(k)
         r_first(g_acc, g_piece(k), gr_in.at[k], G_STEP + 6 * k)
-    r_second(g_acc, g_piece(3), gr_in.at[3], gr_send.at[3], G_STEP + 18)
+    held = {}
+    order = (3, 0, 1, 2)
+    for k in order:
+        r_second(g_acc, g_piece(k), gr_in.at[k], gr_send.at[k], G_STEP + 6 * k)
+    for k in order:
+        held[k] = r_third(g_acc, g_piece(k), gr_in.at[k], gz_send.at[k], gz_in.at[k], G_STEP + 6 * k)
     first, second = reduced(n_in, NORM_RS)
-    for k in range(3):
-        r_second(g_acc, g_piece(k), gr_in.at[k], gr_send.at[k], G_STEP + 6 * k)
     tok_grad = cot_own[...].astype(F32) + jnp.concatenate([first, second], axis=1)
     pad = jnp.zeros((SHARE, WIDE - PAIRS), F32)
     for half in range(2):
@@ -572,10 +601,6 @@
     az_send[...] = over_y(1 - zh).astype(BF)
     push(az_send, az_in, OUT_Z, (s, (m + 8) % 16))
     az_own[...] = over_y(zh)
-    held = {}
-    order = (3, 0, 1, 2)
-    for k in order:
-        held[k] = r_third(g_acc, g_piece(k), gr_in.at[k], gz_send.at[k], gz_in.at[k], G_STEP + 6 * k)
     held_c = a_second(c_send, c_piece(low), cx_in, ca_part, cz_send, cz_in, C_STEP)
     b_second(c_send, c_row, cb_part, cb_held, cbz_in, cx_b, C_STEP + 4)
     for k in order:
@@ -622,9 +647,9 @@
         v(4, HEAD, TOK, dtype=F32), v(4, HEAD, TOK), v(4, HEAD, TOK), v(HEAD, TOK),
         v(4, 8, TOK, dtype=F32),
         v(4, HEAD, TOK, dtype=F32), v(4, HEAD, TOK), v(4, HEAD, TOK),
-        v(1024, HEAD, dtype=F32), v(1024, HEAD, dtype=F32), v(4, TOK, HEAD), v(4, TOK, HEAD), v(TOK, D), v(TOK, D),
+        v(1024, HEAD, dtype=F32), v(1024, HEAD, dtype=F32), v(4, TOK, HEAD), v(4, TOK, HEAD), v(TOK, D), v(TOK, D), v(8, TOK, dtype=F32),
         v(2, TOK, 384), v(2, TOK, 384), v(TOK, 384), v(TOK, 384),
-        v(576, TOK), v(D, TOK, dtype=F32),
+        v(576, TOK),
         v(D, TOK), v(16, SHARE, TOK),
         v(2, 768, TOK), v(4, 2, HEAD, TOK), v(HEAD, TOK), v(HEAD, TOK), v(HEAD, TOK, dtype=F32), v(SHARE, TOK), v(SHARE, TOK),
         v(HEAD, D, dtype=F32), v(4, SHARE, D), v(4, SHARE, D), v(4, SHARE, D),

time: 110 us -> 109 us (level); the launches traced: 109 us -> 107 us
  Pallas kernels: 109 us -> 106 us
    pallas_call x1, Pallas kernels: 104 us -> 101 us  [body(): pl.pallas_call(kernel, out_shape=(layer, jax.ShapeDtypeStruct((2, 256, CI...]
where the time goes in v6:
time: 109 us; the launch traced here: 107 us
  Pallas kernels  106 us (97%)
    pallas_call x1, Pallas kernels, body(): pl.pallas_call(kernel, out_shape=(layer, jax.ShapeDtypeStruct((2, 256, CI...  101 us
    pallas_call x1, Pallas kernels, body(): pl.pallas_call(widen, out_shape=(layer, jax.ShapeDtypeStruct((TAPS, SHARE...  4.74 us

profile of v6, /device:TPU:1, one launch (start us, length us, event | category | flops | bytes accessed | tf_op | source)
XLA Modules:
  0.0 106.7 jit_solution(9752933506481180341)
XLA Ops:
  0.6 101.4 %section.1 = (bf16[96,512]{1,0:T(8,128)(2,1)}, bf16[2,256,768]{2,1,0:T(8,128)(2,1)}, bf16[4,96,1536]{2,1,0:T(8,128)(2,1)}) custom-call(bf16[1024,768]{1,0:T(8,128)(2,1)} %feat_hbm.1, s32[512,128]{1,0:T(8,128)} %bitcast.7, f32[4,768]{1,0:T(4,128)} %bproj.1, bf16[5,96,768]{2,1,0:T(8,128)(2,1)} %cw_hbm.1, f32[1,96]{1,0:T(1,128)} %bitcast.10, ...), custom_call_target="tpu_custom_call" | custom-call | flops 8000000000 | bytes 8000000 | tf_op jit(solution)/shard_map/section/pallas_call | solution.py:690
  102.0 4.7 %widen.1 = (bf16[96,512]{1,0:T(8,128)(2,1)}, f32[5,96,768]{2,1,0:T(8,128)}, f32[1,96]{1,0:T(1,128)}, f32[96,1536]{1,0:T(8,128)}, f32[96,1536]{1,0:T(8,128)}, /*index=5*/f32[96,1536]{1,0:T(8,128)}, f32[96,1536]{1,0:T(8,128)}) custom-call(bf16[96,512]{1,0:T(8,128)(2,1)} %get-tuple-element.17.layer, bf16[512,768]{1,0:T(8,128)(2,1)} %bitcast.6, ...), custom_call_target="tpu_custom_call" | custom-call | tf_op jit(solution)/shard_map/widen/pallas_call | solution.py:706

commit v7 on v6

--- a/solution.py
+++ b/solution.py
@@ -486,15 +486,8 @@
 
     grad_w(3, ot, cot_n)
 
-    @pl.loop(0, 4)
-    def _(k):
-        cols = pl.ds(al(384 * k, 128), 384)
-        a_send[k // 2, pl.ds(al(384 * (k % 2), 128), 384), :] = mm(wo_t[cols, :], ot[...]).astype(BF)
-
     y = (m // 2) % 4
     zh = m // 8
-    grad_sum(3)
-    r_first(g_acc, g_piece(3), gr_in.at[3], G_STEP + 18)
 
     land(dkv_in.at[1], DKV_SIB)
     land(z_in, DKV_Z)
@@ -529,22 +522,28 @@
         scatter_rows((k + m // 4) % 4)
 
     n_in[0] = n_send[mine, :]
-    for r in range(1, 4):
-        rows = pl.ds(al(HEAD * ((y + r) % 4), 64), HEAD)
-        push(a_send.at[:, rows], ay_in.at[r], OUT_Y, (s, zh * 8 + ((y + r) % 4) * 2 + c))
+
+    grad_sum(3)
+    r_first(g_acc, g_piece(3), gr_in.at[3], G_STEP + 18)
 
     for k in range(3):
         grad_w(k, dqkv.at[HEAD * k : HEAD * k + HEAD], norm_n)
     for k in range(3):
         grad_sum(k)
         r_first(g_acc, g_piece(k), gr_in.at[k], G_STEP + 6 * k)
+    @pl.loop(0, 4)
+    def _(k):
+        cols = pl.ds(al(384 * k, 128), 384)
+        a_send[k // 2, pl.ds(al(384 * (k % 2), 128), 384), :] = mm(wo_t[cols, :], ot[...]).astype(BF)
+
     held = {}
     order = (3, 0, 1, 2)
     for k in order:
         r_second(g_acc, g_piece(k), gr_in.at[k], gr_send.at[k], G_STEP + 6 * k)
-    for k in order:
-        held[k] = r_third(g_acc, g_piece(k), gr_in.at[k], gz_send.at[k], gz_in.at[k], G_STEP + 6 * k)
     first, second = reduced(n_in, NORM_RS)
+    for r in range(1, 4):
+        rows = pl.ds(al(HEAD * ((y + r) % 4), 64), HEAD)
+        push(a_send.at[:, rows], ay_in.at[r], OUT_Y, (s, zh * 8 + ((y + r) % 4) * 2 + c))
     tok_grad = cot_own[...].astype(F32) + jnp.concatenate([first, second], axis=1)
     pad = jnp.zeros((SHARE, WIDE - PAIRS), F32)
     for half in range(2):
@@ -592,21 +591,23 @@
     a_first(c_send, c_col, cx_in, C_STEP)
     b_first(c_send, c_row, cbz_in, C_STEP + 4)
 
-    land(ay_in.at[1:4], OUT_Y)
-    rows = pl.ds(al(HEAD * y, 64), HEAD)
-
-    def over_y(z):
-        return a_send[z, rows, :].astype(F32) + sum(ay_in[r, z].astype(F32) for r in range(1, 4))
-
-    az_send[...] = over_y(1 - zh).astype(BF)
-    push(az_send, az_in, OUT_Z, (s, (m + 8) % 16))
-    az_own[...] = over_y(zh)
+    for k in order:
+        held[k] = r_third(g_acc, g_piece(k), gr_in.at[k], gz_send.at[k], gz_in.at[k], G_STEP + 6 * k)
     held_c = a_second(c_send, c_piece(low), cx_in, ca_part, cz_send, cz_in, C_STEP)
     b_second(c_send, c_row, cb_part, cb_held, cbz_in, cx_b, C_STEP + 4)
     for k in order:
         r_fourth(held[k], g_piece(k), g_all, g_red.at[k], gz_in.at[k], G_STEP + 6 * k)
     a_third(held_c, c_piece(low), c_all, c_red.at[0], cz_in, C_STEP)
     b_third(cb_part, c_piece(high), c_all, cb_held, cx_b, c_red.at[1], C_STEP + 4)
+    land(ay_in.at[1:4], OUT_Y)
+    rows = pl.ds(al(HEAD * y, 64), HEAD)
+
+    def over_y(z):
+        return a_send[z, rows, :].astype(F32) + sum(ay_in[r, z].astype(F32) for r in range(1, 4))
+
+    az_send[...] = over_y(1 - zh).astype(BF)
+    push(az_send, az_in, OUT_Z, (s, (m + 8) % 16))
+    az_own[...] = over_y(zh)
     for k in order:
         r_fifth(g_piece(k), g_all, g_red.at[k], G_STEP + 6 * k)
     a_fourth(c_col, c_all, c_red.at[0], C_STEP)

time: 109 us -> 107 us (0.982); the launches traced: 107 us -> 107 us
  no operation moved by 1% of the time
where the time goes in v7:
time: 107 us
  Pallas kernels  106 us (99%)
    pallas_call x1, Pallas kernels, body(): pl.pallas_call(kernel, out_shape=(layer, jax.ShapeDtypeStruct((2, 256, CI...  102 us
    pallas_call x1, Pallas kernels, body(): pl.pallas_call(widen, out_shape=(layer, jax.ShapeDtypeStruct((TAPS, SHARE...  4.74 us

profile of v7, /device:TPU:1, one launch (start us, length us, event | category | flops | bytes accessed | tf_op | source)
XLA Modules:
  0.0 107.1 jit_solution(14034454428573622526)
XLA Ops:
  0.6 101.7 %section.1 = (bf16[96,512]{1,0:T(8,128)(2,1)}, bf16[2,256,768]{2,1,0:T(8,128)(2,1)}, bf16[4,96,1536]{2,1,0:T(8,128)(2,1)}) custom-call(bf16[1024,768]{1,0:T(8,128)(2,1)} %feat_hbm.1, s32[512,128]{1,0:T(8,128)} %bitcast.7, f32[4,768]{1,0:T(4,128)} %bproj.1, bf16[5,96,768]{2,1,0:T(8,128)(2,1)} %cw_hbm.1, f32[1,96]{1,0:T(1,128)} %bitcast.10, ...), custom_call_target="tpu_custom_call" | custom-call | flops 8000000000 | bytes 8000000 | tf_op jit(solution)/shard_map/section/pallas_call | solution.py:691
  102.3 4.7 %widen.1 = (bf16[96,512]{1,0:T(8,128)(2,1)}, f32[5,96,768]{2,1,0:T(8,128)}, f32[1,96]{1,0:T(1,128)}, f32[96,1536]{1,0:T(8,128)}, f32[96,1536]{1,0:T(8,128)}, /*index=5*/f32[96,1536]{1,0:T(8,128)}, f32[96,1536]{1,0:T(8,128)}) custom-call(bf16[96,512]{1,0:T(8,128)(2,1)} %get-tuple-element.17.layer, bf16[512,768]{1,0:T(8,128)(2,1)} %bitcast.6, ...), custom_call_target="tpu_custom_call" | custom-call | tf_op jit(solution)/shard_map/widen/pallas_call | solution.py:707

commit v8 on v7

--- a/solution.py
+++ b/solution.py
@@ -109,10 +109,21 @@
         load.start()
     mine = pl.ds(al(SHARE * m, 32), SHARE)
 
-    def spread(own, full, base, steps=range(1, 16)):
-        for r in steps:
-            cols = pl.ds(al(TOK * ((m + r) % 2), TOK), TOK)
-            push(own.at[:, cols], full.at[mine], base, mppeer(r))
+    y = (m // 2) % 4
+    zh = m // 8
+    around = (
+        (1, 0, 0), (0, 1, 0), (0, 3, 0), (1, 2, 0), (0, 2, 1), (1, 1, 1), (1, 3, 1), (1, 0, 1),
+        (0, 1, 1), (0, 3, 1), (1, 2, 1), (0, 2, 0), (1, 1, 0), (1, 3, 0), (0, 0, 1),
+    )
+
+    def around_mp(step):
+        dz, dy, dc = step
+        return ((zh + dz) % 2) * 8 + ((y + dy) % 4) * 2 + (c + dc) % 2
+
+    def spread(own, full, base, steps=around):
+        for step in steps:
+            cols = pl.ds(al(TOK * ((c + step[2]) % 2), TOK), TOK)
+            push(own.at[:, cols], full.at[mine], base, (s, around_mp(step)))
 
     def keep(own, full):
         full[mine, :] = own[:, pl.ds(al(TOK * c, TOK), TOK)]
@@ -121,7 +132,7 @@
         land(full.at[0 : 15 * SHARE], base)
 
     pl.semaphore_wait(barrier, 22)
-    spread(cot_hbm, cot_t, COT_AG, range(1, 10))
+    spread(cot_hbm, cot_t, COT_AG, around[:9])
     for k, w in enumerate((wo, wq, wk, wv)):
         rows = pl.ds(al(HEAD * ((k + 3) % 4) + SHARE * c, 32), SHARE)
         push(w, w4.at[rows], W_SIB, sib)
@@ -197,7 +208,7 @@
         )
     tok_own[...] = (0.5 * total).astype(BF)
     spread(tok_own, tok_t, TOK_AG)
-    spread(cot_hbm, cot_t, COT_AG, range(10, 16))
+    spread(cot_hbm, cot_t, COT_AG, around[9:])
     keep(tok_own, tok_t)
     for load in loads[3:]:
         load.wait()
@@ -427,6 +438,20 @@
             push(red, piece(full, zl, x), sem + 4, dev)
         piece(full, zl, x)[...] = red[...]
 
+    def s_fourth(held, piece, full, red, into_z, sem):
+        land(into_z, sem + 2)
+        red[...] = (held + into_z[...].astype(F32)).astype(BF)
+        for r in range(1, 4):
+            push(red, piece(full, zl, x), sem + 3, xpeer(r))
+        piece(full, zl, x)[...] = red[...]
+
+    def s_fifth(row, full, into, sem):
+        land(into.at[0:3], sem + 3)
+        push(row(full, zl), row(full, zl), sem + 4, zpart)
+
+    def g_row(k):
+        return lambda buf, at: buf.at[k, pl.ds(al(48 * at, 16), 48), :]
+
     def r_fifth(piece, full, red, sem):
         land(red, sem + 3)
         for dev in (right, left):
@@ -486,8 +511,6 @@
 
     grad_w(3, ot, cot_n)
 
-    y = (m // 2) % 4
-    zh = m // 8
 
     land(dkv_in.at[1], DKV_SIB)
     land(z_in, DKV_Z)
@@ -508,19 +531,15 @@
         inverse = wide_stat[1:2, :]
         unit = tok_t[cols, :].astype(F32) * inverse
         n_send[cols, :] = (inverse * (mm(w_t[cols, :], dqkv[...]) - unit * wide_stat[0:1, :])).astype(BF)
-        for i in range(4):
-            peer = 4 * k + i
-            slot = (peer + 16 - m) % 16
-            rows = pl.ds(al(SHARE * peer, 32), SHARE)
-
-            @pl.when(slot > 0)
-            def _():
-                push(n_send.at[rows], n_in.at[slot], NORM_RS, (s, peer))
 
     @pl.loop(0, 4)
     def _(k):
-        scatter_rows((k + m // 4) % 4)
-
+        scatter_rows(k)
+
+    for step in around:
+        peer = around_mp(step)
+        slot = step[0] * 8 + step[1] * 2 + step[2]
+        push(n_send.at[pl.ds(al(SHARE * peer, 32), SHARE)], n_in.at[slot], NORM_RS, (s, peer))
     n_in[0] = n_send[mine, :]
 
     grad_sum(3)
@@ -596,7 +615,8 @@
     held_c = a_second(c_send, c_piece(low), cx_in, ca_part, cz_send, cz_in, C_STEP)
     b_second(c_send, c_row, cb_part, cb_held, cbz_in, cx_b, C_STEP + 4)
     for k in order:
-        r_fourth(held[k], g_piece(k), g_all, g_red.at[k], gz_in.at[k], G_STEP + 6 * k)
+        fourth = r_fourth if k in (0, 3) else s_fourth
+        fourth(held[k], g_piece(k), g_all, g_red.at[k], gz_in.at[k], G_STEP + 6 * k)
     a_third(held_c, c_piece(low), c_all, c_red.at[0], cz_in, C_STEP)
     b_third(cb_part, c_piece(high), c_all, cb_held, cx_b, c_red.at[1], C_STEP + 4)
     land(ay_in.at[1:4], OUT_Y)
@@ -608,11 +628,13 @@
     az_send[...] = over_y(1 - zh).astype(BF)
     push(az_send, az_in, OUT_Z, (s, (m + 8) % 16))
     az_own[...] = over_y(zh)
-    for k in order:
+    for k in (3, 0):
         r_fifth(g_piece(k), g_all, g_red.at[k], G_STEP + 6 * k)
     a_fourth(c_col, c_all, c_red.at[0], C_STEP)
     b_fourth(c_row, c_all, cx_b, C_STEP + 4)
-    for k in order:
+    for k in (1, 2):
+        s_fifth(g_row(k), g_all, gr_in.at[k], G_STEP + 6 * k)
+    for k in (3, 0):
         r_sixth(g_piece(k), g_all, gr_in.at[k], G_STEP + 6 * k)
 
     land(az_in, OUT_Z)
@@ -625,8 +647,10 @@
     out = jnp.concatenate([jnp.where(c == 0, own, other), jnp.where(c == 0, other, own)], axis=1)
     o_layer[...] = (out + tok_own[...].astype(F32)).astype(BF)
 
-    for k in order:
+    for k in (3, 0):
         land(gr_in.at[k, 0:2], G_STEP + 6 * k + 5)
+    for k in (1, 2):
+        land(gr_in.at[k, 0:4], G_STEP + 6 * k + 4)
     land(cx_in.at[1:4], C_STEP + 3)
     land(cbz_in, C_STEP + 7)
     for copy in sent.values():

time: 107 us -> 108 us (level); the launches traced: 107 us -> 106 us
  no operation moved by 1% of the time
where the time goes in v8:
time: 108 us; the launch traced here: 106 us
  Pallas kernels  106 us (98%)
    pallas_call x1, Pallas kernels, body(): pl.pallas_call(kernel, out_shape=(layer, jax.ShapeDtypeStruct((2, 256, CI...  101 us
    pallas_call x1, Pallas kernels, body(): pl.pallas_call(widen, out_shape=(layer, jax.ShapeDtypeStruct((TAPS, SHARE...  4.74 us

profile of v8, /device:TPU:1, one launch (start us, length us, event | category | flops | bytes accessed | tf_op | source)
XLA Modules:
  0.0 106.3 jit_solution(17836092526313664436)
XLA Ops:
  0.6 100.9 %section.1 = (bf16[96,512]{1,0:T(8,128)(2,1)}, bf16[2,256,768]{2,1,0:T(8,128)(2,1)}, bf16[4,96,1536]{2,1,0:T(8,128)(2,1)}) custom-call(bf16[1024,768]{1,0:T(8,128)(2,1)} %feat_hbm.1, s32[512,128]{1,0:T(8,128)} %bitcast.7, f32[4,768]{1,0:T(4,128)} %bproj.1, bf16[5,96,768]{2,1,0:T(8,128)(2,1)} %cw_hbm.1, f32[1,96]{1,0:T(1,128)} %bitcast.10, ...), custom_call_target="tpu_custom_call" | custom-call | flops 8000000000 | bytes 8000000 | tf_op jit(solution)/shard_map/section/pallas_call | solution.py:715
  101.5 4.7 %widen.1 = (bf16[96,512]{1,0:T(8,128)(2,1)}, f32[5,96,768]{2,1,0:T(8,128)}, f32[1,96]{1,0:T(1,128)}, f32[96,1536]{1,0:T(8,128)}, f32[96,1536]{1,0:T(8,128)}, /*index=5*/f32[96,1536]{1,0:T(8,128)}, f32[96,1536]{1,0:T(8,128)}) custom-call(bf16[96,512]{1,0:T(8,128)(2,1)} %get-tuple-element.17.layer, bf16[512,768]{1,0:T(8,128)(2,1)} %bitcast.6, ...), custom_call_target="tpu_custom_call" | custom-call | tf_op jit(solution)/shard_map/widen/pallas_call | solution.py:731

commit v9 on v8

--- a/solution.py
+++ b/solution.py
@@ -25,9 +25,9 @@
 
 (
     COT_AG, TOK_AG, W_SIB, HALO, Q_X, DO_X, ST_X, O_X, DQ_X, K_Z, V_Z, KV_SIB, K_FWD, V_FWD, DKV_FAR, DKV_SIB, DKV_Z,
-    OUT_Y, OUT_Z, OUT_SIB, NORM_RS,
-) = range(21)
-G_SIB = 21
+    OUT_Y, OUT_Z, OUT_SIB, NORM_RS, VIA_C, VIA_T, VIA_N,
+) = range(24)
+G_SIB = 24
 G_STEP = G_SIB + 4
 C_STEP = G_STEP + 24
 SEMS = C_STEP + 8
@@ -53,14 +53,26 @@
     dq_f, dq_send, dq_in, dk, dv, qn, don, norm_n, cot_n, wide_stat, dkv_send, dkv_in, z_send, z_in, dqkv,
     n_send, n_in, a_send, ay_in, az_send, az_in, az_own, as_send, as_in,
     g_part, g_send, g_sib, g_acc, gr_in, gr_send, gz_send, gz_in, g_red,
-    pgs, c_send, cx_in, cz_send, cz_in, cbz_in, cb_held, cx_b, c_red, ssem, rsem, lsem,
+    pgs, c_send, cx_in, cz_send, cz_in, cbz_in, cb_held, cx_b, c_red, via_c, via_t, via_n, ssem, rsem, lsem,
 ):
     s = lax.axis_index("seq")
     m = lax.axis_index("mp")
     zl = s // 4
     x = s % 4
     c = m % 2
+    y = (m // 2) % 4
+    zh = m // 8
     sib = (s, m + 1 - 2 * c)
+    z_down, z_up = (zh * 2 + zl + 3) % 4, (zh * 2 + zl + 1) % 4
+
+    def at_z(z4, row, core):
+        return ((z4 % 2) * 4 + x, (z4 // 2) * 8 + row * 2 + core)
+
+    relayed = ((1, 0, 0), (1, 0, 1), (1, 1, 0), (1, 3, 1))
+
+    def far_end(step):
+        return at_z(z_down, (y + step[1]) % 4, (c + step[2]) % 2)
+
     zpart = ((1 - zl) * 4 + x, m)
     sent = {}
 
@@ -95,6 +107,9 @@
         pl.semaphore_signal(barrier, inc=1, device_id=mppeer(r), device_id_type=MESH)
     for r in range(1, 8):
         pl.semaphore_signal(barrier, inc=1, device_id=seqpeer(r), device_id_type=MESH)
+    for step in relayed:
+        source = at_z(z_up, (y + 4 - step[1]) % 4, (c + step[2]) % 2)
+        pl.semaphore_signal(barrier, inc=1, device_id=source, device_id_type=MESH)
 
     loads = [
         pltpu.make_async_copy(toks_hbm, toks, lsem.at[0]),
@@ -109,21 +124,28 @@
         load.start()
     mine = pl.ds(al(SHARE * m, 32), SHARE)
 
-    y = (m // 2) % 4
-    zh = m // 8
     around = (
-        (1, 0, 0), (0, 1, 0), (0, 3, 0), (1, 2, 0), (0, 2, 1), (1, 1, 1), (1, 3, 1), (1, 0, 1),
-        (0, 1, 1), (0, 3, 1), (1, 2, 1), (0, 2, 0), (1, 1, 0), (1, 3, 0), (0, 0, 1),
+        (1, 1, 0), (1, 2, 0), (0, 1, 0), (0, 3, 0), (1, 3, 1), (1, 1, 1), (1, 0, 1), (0, 2, 1), (1, 0, 0),
+        (1, 2, 1), (0, 1, 1), (0, 3, 1), (1, 3, 0), (0, 2, 0), (0, 0, 1),
     )
 
     def around_mp(step):
         dz, dy, dc = step
         return ((zh + dz) % 2) * 8 + ((y + dy) % 4) * 2 + (c + dc) % 2
 
-    def spread(own, full, base, steps=around):
+    def spread(own, full, base, via, via_sem, steps=around):
         for step in steps:
             cols = pl.ds(al(TOK * ((c + step[2]) % 2), TOK), TOK)
-            push(own.at[:, cols], full.at[mine], base, (s, around_mp(step)))
+            if step in relayed:
+                push(own.at[:, cols], via.at[relayed.index(step)], via_sem, at_z(z_down, y, c))
+            else:
+                push(own.at[:, cols], full.at[mine], base, (s, around_mp(step)))
+
+    def pass_on(full, base, via, via_sem):
+        land(via, via_sem)
+        rows = pl.ds(al(SHARE * ((z_up // 2) * 8 + y * 2 + c), 32), SHARE)
+        for i, step in enumerate(relayed):
+            push(via.at[i], full.at[rows], base, far_end(step))
 
     def keep(own, full):
         full[mine, :] = own[:, pl.ds(al(TOK * c, TOK), TOK)]
@@ -131,8 +153,8 @@
     def gathered(full, base):
         land(full.at[0 : 15 * SHARE], base)
 
-    pl.semaphore_wait(barrier, 22)
-    spread(cot_hbm, cot_t, COT_AG, around[:9])
+    pl.semaphore_wait(barrier, 26)
+    spread(cot_hbm, cot_t, COT_AG, via_c, VIA_C, around[:9])
     for k, w in enumerate((wo, wq, wk, wv)):
         rows = pl.ds(al(HEAD * ((k + 3) % 4) + SHARE * c, 32), SHARE)
         push(w, w4.at[rows], W_SIB, sib)
@@ -181,6 +203,7 @@
         rows = pl.ds(al(i * 256, 256), 256)
         z[:, rows] = nt(wt[...], xe[rows, :])
 
+    pass_on(cot_t, COT_AG, via_c, VIA_C)
     land(halo, HALO)
     at = lax.broadcasted_iota(jnp.int32, (16, D), 0)
     after = halo[1].astype(F32)
@@ -207,9 +230,10 @@
             ROOT2PI * (1.0 + (3.0 * 0.044715) * square)
         )
     tok_own[...] = (0.5 * total).astype(BF)
-    spread(tok_own, tok_t, TOK_AG)
-    spread(cot_hbm, cot_t, COT_AG, around[9:])
+    spread(tok_own, tok_t, TOK_AG, via_t, VIA_T)
+    spread(cot_hbm, cot_t, COT_AG, via_c, VIA_C, around[9:])
     keep(tok_own, tok_t)
+    pass_on(tok_t, TOK_AG, via_t, VIA_T)
     for load in loads[3:]:
         load.wait()
     land(w4.at[0 : 4 * SHARE], W_SIB)
@@ -539,7 +563,11 @@
     for step in around:
         peer = around_mp(step)
         slot = step[0] * 8 + step[1] * 2 + step[2]
-        push(n_send.at[pl.ds(al(SHARE * peer, 32), SHARE)], n_in.at[slot], NORM_RS, (s, peer))
+        piece = n_send.at[pl.ds(al(SHARE * peer, 32), SHARE)]
+        if step in relayed:
+            push(piece, via_n.at[relayed.index(step)], VIA_N, at_z(z_down, y, c))
+        else:
+            push(piece, n_in.at[slot], NORM_RS, (s, peer))
     n_in[0] = n_send[mine, :]
 
     grad_sum(3)
@@ -547,6 +575,9 @@
 
     for k in range(3):
         grad_w(k, dqkv.at[HEAD * k : HEAD * k + HEAD], norm_n)
+    land(via_n, VIA_N)
+    for i, step in enumerate(relayed):
+        push(via_n.at[i], n_in.at[step[0] * 8 + step[1] * 2 + step[2]], NORM_RS, far_end(step))
     for k in range(3):
         grad_sum(k)
         r_first(g_acc, g_piece(k), gr_in.at[k], G_STEP + 6 * k)
@@ -681,6 +712,7 @@
         v(4, 6, 48, 384), v(4, 2, 48, 384), v(4, 48, 384), v(4, 48, 384), v(4, 48, 384),
         v(576, WIDE), v(2, 256, CIN),
         v(4, 2, 64, 384), v(64, 384), v(64, 384), v(256, 384), v(256, 384), v(4, 64, 384), v(2, 64, 384),
+        v(4, SHARE, TOK), v(4, SHARE, TOK), v(4, SHARE, TOK),
         pltpu.SemaphoreType.DMA((SEMS,)), pltpu.SemaphoreType.DMA((SEMS,)), pltpu.SemaphoreType.DMA((8,)),
     ]
 

time: 108 us -> 128 us (1.19)
  Pallas kernels: 106 us -> 126 us
    pallas_call x1, Pallas kernels: 101 us -> 121 us  [body(): pl.pallas_call(kernel, out_shape=(layer, jax.ShapeDtypeStruct((2, 256, CI...]
where the time goes in v9:
time: 128 us; the launch traced here: 127 us
  Pallas kernels  126 us (98%)
    pallas_call x1, Pallas kernels, body(): pl.pallas_call(kernel, out_shape=(layer, jax.ShapeDtypeStruct((2, 256, CI...  121 us
    pallas_call x1, Pallas kernels, body(): pl.pallas_call(widen, out_shape=(layer, jax.ShapeDtypeStruct((TAPS, SHARE...  4.74 us

profile of v9, /device:TPU:1, one launch (start us, length us, event | category | flops | bytes accessed | tf_op | source)
XLA Modules:
  0.0 126.9 jit_solution(4664218865580422290)
XLA Ops:
  0.6 121.5 %section.1 = (bf16[96,512]{1,0:T(8,128)(2,1)}, bf16[2,256,768]{2,1,0:T(8,128)(2,1)}, bf16[4,96,1536]{2,1,0:T(8,128)(2,1)}) custom-call(bf16[1024,768]{1,0:T(8,128)(2,1)} %feat_hbm.1, s32[512,128]{1,0:T(8,128)} %bitcast.7, f32[4,768]{1,0:T(4,128)} %bproj.1, bf16[5,96,768]{2,1,0:T(8,128)(2,1)} %cw_hbm.1, f32[1,96]{1,0:T(1,128)} %bitcast.10, ...), custom_call_target="tpu_custom_call" | custom-call | flops 8000000000 | bytes 8000000 | tf_op jit(solution)/shard_map/section/pallas_call | solution.py:747
  122.1 4.7 %widen.1 = (bf16[96,512]{1,0:T(8,128)(2,1)}, f32[5,96,768]{2,1,0:T(8,128)}, f32[1,96]{1,0:T(1,128)}, f32[96,1536]{1,0:T(8,128)}, f32[96,1536]{1,0:T(8,128)}, /*index=5*/f32[96,1536]{1,0:T(8,128)}, f32[96,1536]{1,0:T(8,128)}) custom-call(bf16[96,512]{1,0:T(8,128)(2,1)} %get-tuple-element.17.layer, bf16[512,768]{1,0:T(8,128)(2,1)} %bitcast.6, ...), custom_call_target="tpu_custom_call" | custom-call | tf_op jit(solution)/shard_map/widen/pallas_call | solution.py:763

commit v10 on v8

--- a/solution.py
+++ b/solution.py
@@ -438,20 +438,6 @@
             push(red, piece(full, zl, x), sem + 4, dev)
         piece(full, zl, x)[...] = red[...]
 
-    def s_fourth(held, piece, full, red, into_z, sem):
-        land(into_z, sem + 2)
-        red[...] = (held + into_z[...].astype(F32)).astype(BF)
-        for r in range(1, 4):
-            push(red, piece(full, zl, x), sem + 3, xpeer(r))
-        piece(full, zl, x)[...] = red[...]
-
-    def s_fifth(row, full, into, sem):
-        land(into.at[0:3], sem + 3)
-        push(row(full, zl), row(full, zl), sem + 4, zpart)
-
-    def g_row(k):
-        return lambda buf, at: buf.at[k, pl.ds(al(48 * at, 16), 48), :]
-
     def r_fifth(piece, full, red, sem):
         land(red, sem + 3)
         for dev in (right, left):
@@ -615,8 +601,7 @@
     held_c = a_second(c_send, c_piece(low), cx_in, ca_part, cz_send, cz_in, C_STEP)
     b_second(c_send, c_row, cb_part, cb_held, cbz_in, cx_b, C_STEP + 4)
     for k in order:
-        fourth = r_fourth if k in (0, 3) else s_fourth
-        fourth(held[k], g_piece(k), g_all, g_red.at[k], gz_in.at[k], G_STEP + 6 * k)
+        r_fourth(held[k], g_piece(k), g_all, g_red.at[k], gz_in.at[k], G_STEP + 6 * k)
     a_third(held_c, c_piece(low), c_all, c_red.at[0], cz_in, C_STEP)
     b_third(cb_part, c_piece(high), c_all, cb_held, cx_b, c_red.at[1], C_STEP + 4)
     land(ay_in.at[1:4], OUT_Y)
@@ -628,13 +613,11 @@
     az_send[...] = over_y(1 - zh).astype(BF)
     push(az_send, az_in, OUT_Z, (s, (m + 8) % 16))
     az_own[...] = over_y(zh)
-    for k in (3, 0):
+    for k in order:
         r_fifth(g_piece(k), g_all, g_red.at[k], G_STEP + 6 * k)
     a_fourth(c_col, c_all, c_red.at[0], C_STEP)
     b_fourth(c_row, c_all, cx_b, C_STEP + 4)
-    for k in (1, 2):
-        s_fifth(g_row(k), g_all, gr_in.at[k], G_STEP + 6 * k)
-    for k in (3, 0):
+    for k in order:
         r_sixth(g_piece(k), g_all, gr_in.at[k], G_STEP + 6 * k)
 
     land(az_in, OUT_Z)
@@ -647,10 +630,8 @@
     out = jnp.concatenate([jnp.where(c == 0, own, other), jnp.where(c == 0, other, own)], axis=1)
     o_layer[...] = (out + tok_own[...].astype(F32)).astype(BF)
 
-    for k in (3, 0):
+    for k in order:
         land(gr_in.at[k, 0:2], G_STEP + 6 * k + 5)
-    for k in (1, 2):
-        land(gr_in.at[k, 0:4], G_STEP + 6 * k + 4)
     land(cx_in.at[1:4], C_STEP + 3)
     land(cbz_in, C_STEP + 7)
     for copy in sent.values():

time: 108 us -> 107 us (level); the launches traced: 106 us -> 107 us
  no operation moved by 1% of the time
where the time goes in v10:
time: 107 us
  Pallas kernels  106 us (99%)
    pallas_call x1, Pallas kernels, body(): pl.pallas_call(kernel, out_shape=(layer, jax.ShapeDtypeStruct((2, 256, CI...  101 us
    pallas_call x1, Pallas kernels, body(): pl.pallas_call(widen, out_shape=(layer, jax.ShapeDtypeStruct((TAPS, SHARE...  4.74 us

profile of v10, /device:TPU:1, one launch (start us, length us, event | category | flops | bytes accessed | tf_op | source)
XLA Modules:
  0.0 106.7 jit_solution(2934498637379813987)
XLA Ops:
  0.6 101.4 %section.1 = (bf16[96,512]{1,0:T(8,128)(2,1)}, bf16[2,256,768]{2,1,0:T(8,128)(2,1)}, bf16[4,96,1536]{2,1,0:T(8,128)(2,1)}) custom-call(bf16[1024,768]{1,0:T(8,128)(2,1)} %feat_hbm.1, s32[512,128]{1,0:T(8,128)} %bitcast.7, f32[4,768]{1,0:T(4,128)} %bproj.1, bf16[5,96,768]{2,1,0:T(8,128)(2,1)} %cw_hbm.1, f32[1,96]{1,0:T(1,128)} %bitcast.10, ...), custom_call_target="tpu_custom_call" | custom-call | flops 8000000000 | bytes 8000000 | tf_op jit(solution)/shard_map/section/pallas_call | solution.py:696
  102.0 4.7 %widen.1 = (bf16[96,512]{1,0:T(8,128)(2,1)}, f32[5,96,768]{2,1,0:T(8,128)}, f32[1,96]{1,0:T(1,128)}, f32[96,1536]{1,0:T(8,128)}, f32[96,1536]{1,0:T(8,128)}, /*index=5*/f32[96,1536]{1,0:T(8,128)}, f32[96,1536]{1,0:T(8,128)}) custom-call(bf16[96,512]{1,0:T(8,128)(2,1)} %get-tuple-element.17.layer, bf16[512,768]{1,0:T(8,128)(2,1)} %bitcast.6, ...), custom_call_target="tpu_custom_call" | custom-call | tf_op jit(solution)/shard_map/widen/pallas_call | solution.py:712
